TPU v7x, 32 devices: a whole 2x2x4 slice. The times are simulated.
32 devices in a mesh: fast: 16 (over z, y, core), slow: 2 (over x).
Axes of the slice: x: 2, y: 2, z: 4, core: 2. Of those that a mesh axis runs over, the one named last changes fastest.
Arguments:
- object_field: float32 [2, 4096, 512], P(None, 'fast', 'slow'), may hold values from -5 to 5
- probe_modes: float32 [2, 2, 128, 128], replicated, may hold values from -3 to 3
- descan: float32 [2, 3], replicated, may hold values from -0.5 to 0.5
- scan_positions: int32 [2, 32, 2], P(None, 'fast', 'slow'), may hold values from 0 to 3968, as said below
- amplitudes: float32 [32, 256, 128], P('fast', 'slow'), may hold values from 0.2 to 4
Outputs:
- object_out: float32 [2, 4096, 512], P(None, 'fast', 'slow')
- probe_out: float32 [2, 2, 128, 128], replicated
- descan_out: float32 [2, 3], replicated
Inputs may be any that keep to these rules, and one draw needn't show every extreme that they name: `scan_positions`: window starts of tile (i, j) lie from i * 256 - 64 to i * 256 + 192 along the fast-scan direction and from j * 256 - 64 to j * 256 + 192 along the slow one, and every window lies inside the object.
All inputs are finite; a program needn't handle non-finite values.
Results may differ from a plain program's by a relative error of at most 0.0003.
Values sent between devices are 32-bit elements; how exact they have to be, the bound alone decides.
No kernel may reach another device: no remote copies, remote signals or barrier semaphores. Data moves between devices by JAX's collectives and lax.ppermute only.
A program may use at most 64 MiB of HBM per device.

v0:
```python
import functools
import math

import jax
import jax.numpy as jnp
import numpy as np
from jax import lax
from jax.experimental import pallas as pl
from jax.experimental.pallas import tpu as pltpu
from jax.sharding import PartitionSpec as P

OBJECT_STEP = 0.1
PROBE_STEP = 8.0
DESCAN_STEP = 0.02
FLOOR_LEVEL = 0.25
PROBE_POWER = 0.5
LANES = 128
EXTRA = 8
AXES = ("fast", "slow")
F32 = jnp.float32
BF16 = jnp.bfloat16
VMEM = pl.BlockSpec(memory_space=pltpu.VMEM)
SMEM = pl.BlockSpec(memory_space=pltpu.SMEM)
LIMIT = 40 * 1024 * 1024


def transform_tables(width):
    counter = np.arange(width)
    angles = 2.0 * np.pi / width * (counter[:, None] * counter[None, :] % width)
    real = np.cos(angles) / math.sqrt(width)
    imag = -np.sin(angles) / math.sqrt(width)
    forward = np.block([[real, imag], [-imag, real]]).astype(np.float32)
    backward = np.block([[real, -imag], [imag, real]]).astype(np.float32)
    parts = []
    for table in (forward, backward):
        high = table.astype(BF16)
        parts += [high, (table - high.astype(np.float32)).astype(BF16)]
    return jnp.asarray(np.stack(parts))


def split(value):
    high = value.astype(BF16)
    return high, (value - high.astype(F32)).astype(BF16)


def dot(a, b):
    return jnp.dot(a, b, preferred_element_type=F32)


def product(left, right):
    (left_high, left_low), (right_high, right_low) = left, right
    return dot(left_high, right_high) + dot(left_high, right_low) + dot(left_low, right_high)


def lane_of(shape):
    return lax.broadcasted_iota(jnp.int32, shape, len(shape) - 1)


def window_place(starts, j, tile_rows, tile_cols, width, fast, slow):
    rim = width // 2
    row = starts[0, j, 0] - fast * tile_rows + rim
    col = starts[1, j, 0] - slow * tile_cols
    lane = jnp.where(col < 0, col + tile_cols + width, col)
    block = jnp.minimum(row // 8, (tile_rows + width - width - 8) // 8)
    return block * 8, row - block * 8, lane


def gradients(
    object_ref, probe, descan_rows, starts, measured_ref, tables_ref, gradient_ref, wave_ref, far_ref, sizes
):
    tile_rows, tile_cols, width, modes, count, n_fast, n_slow, fast, slow = sizes
    ext_cols = tile_cols + width
    high = width + 8
    probe_real, probe_imag = probe
    lane_row = lane_of((1, width)).astype(F32)
    centred = (lane_row - width // 2) / width
    tables = [tables_ref[k] for k in range(4)]
    forward, backward = (tables[0], tables[1]), (tables[2], tables[3])

    fractions = []
    phases = []
    for j in range(count):
        frac_row = jnp.full((1, width), starts[0, j, 0], jnp.int32).astype(F32) / (tile_rows * n_fast)
        frac_col = jnp.full((1, width), starts[1, j, 0], jnp.int32).astype(F32) / (tile_cols * n_slow)
        fractions.append((frac_row, frac_col))
        for k in range(2):
            d = descan_rows[3 * k : 3 * k + 3]
            phases.append((2 * math.pi) * ((d[0] + d[1] * frac_row + d[2] * frac_col) * centred))
    while len(phases) % 8:
        phases.append(jnp.zeros((1, width), F32))
    phases = jnp.concatenate(phases, axis=0)
    cosines, sines = jnp.cos(phases), jnp.sin(phases)

    def along_rows(row):
        return jnp.transpose(jnp.broadcast_to(row, (width, width)))

    lits = []
    ramps = []
    for j in range(count):
        row_start, row_shift, lane = window_place(starts, j, tile_rows, tile_cols, width, fast, slow)
        row_start = pl.multiple_of(row_start, 8)
        row_cos, row_sin = along_rows(cosines[2 * j : 2 * j + 1]), along_rows(sines[2 * j : 2 * j + 1])
        col_cos, col_sin = cosines[2 * j + 1 : 2 * j + 2], sines[2 * j + 1 : 2 * j + 2]
        ramp_real = row_cos * col_cos - row_sin * col_sin
        ramp_imag = row_cos * col_sin + row_sin * col_cos
        patch = []
        for part in range(2):
            rows = object_ref[part, pl.ds(row_start, high), :]
            rows = pltpu.roll(rows, lax.rem(ext_cols - lane, ext_cols), 1)[:, :width]
            patch.append(pltpu.roll(rows, lax.rem(high - row_shift, high), 0)[:width])
        lit_real = patch[0] * ramp_real - patch[1] * ramp_imag
        lit_imag = patch[0] * ramp_imag + patch[1] * ramp_real
        lits.append((lit_real, lit_imag))
        ramps.append((ramp_real, ramp_imag))
        for m in range(modes):
            p_real = probe_real[m * width : (m + 1) * width]
            p_imag = probe_imag[m * width : (m + 1) * width]
            at = (j * modes + m) * width
            wave_ref[at : at + width, :width] = p_real * lit_real - p_imag * lit_imag
            wave_ref[at : at + width, width:] = p_real * lit_imag + p_imag * lit_real

    half = product(split(wave_ref[...]), forward)
    for w in range(count * modes):
        at = w * width
        far_ref[:width, at : at + width] = half[at : at + width, :width]
        far_ref[width:, at : at + width] = half[at : at + width, width:]
    far = product(backward, split(far_ref[...]))
    far_ref[...] = far
    for j in range(count):
        intensity = None
        for m in range(modes):
            at = (j * modes + m) * width
            real, imag = far_ref[:width, at : at + width], far_ref[width:, at : at + width]
            power = real * real + imag * imag
            intensity = power if intensity is None else intensity + power
        factor = 1.0 - measured_ref[j] / jnp.sqrt(jnp.maximum(intensity, FLOOR_LEVEL))
        for m in range(modes):
            at = (j * modes + m) * width
            far_ref[:width, at : at + width] *= factor
            far_ref[width:, at : at + width] *= factor
    half = product(forward, split(far_ref[...]))
    for w in range(count * modes):
        at = w * width
        wave_ref[at : at + width, :width] = half[:width, at : at + width]
        wave_ref[at : at + width, width:] = half[width:, at : at + width]
    wave_ref[...] = product(split(wave_ref[...]), backward)

    gradient_ref[...] = jnp.zeros(gradient_ref.shape, F32)
    probe_grad = [[None] * modes, [None] * modes]
    descan_grad = [None] * 6
    centred_rows = along_rows(centred)
    for j in range(count):
        lit_real, lit_imag = lits[j]
        ramp_real, ramp_imag = ramps[j]
        sum_real = sum_imag = None
        for m in range(modes):
            p_real = probe_real[m * width : (m + 1) * width]
            p_imag = probe_imag[m * width : (m + 1) * width]
            at = (j * modes + m) * width
            real, imag = wave_ref[at : at + width, :width], wave_ref[at : at + width, width:]
            q_real = lit_real * real + lit_imag * imag
            q_imag = lit_real * imag - lit_imag * real
            probe_grad[0][m] = q_real if j == 0 else probe_grad[0][m] + q_real
            probe_grad[1][m] = q_imag if j == 0 else probe_grad[1][m] + q_imag
            h_real = p_real * real + p_imag * imag
            h_imag = p_real * imag - p_imag * real
            sum_real = h_real if m == 0 else sum_real + h_real
            sum_imag = h_imag if m == 0 else sum_imag + h_imag
        twist = lit_imag * sum_real - lit_real * sum_imag
        totals = (
            jnp.sum(jnp.sum(twist * centred_rows, axis=0, keepdims=True), axis=1, keepdims=True),
            jnp.sum(jnp.sum(twist, axis=0, keepdims=True) * centred, axis=1, keepdims=True),
        )
        frac_row, frac_col = fractions[j]
        for k in range(2):
            base = jnp.broadcast_to(-4 * math.pi * totals[k], (1, width))
            for n, term in enumerate((base, base * frac_row, base * frac_col)):
                descan_grad[3 * k + n] = term if j == 0 else descan_grad[3 * k + n] + term
        row_start, row_shift, lane = window_place(starts, j, tile_rows, tile_cols, width, fast, slow)
        row_start = pl.multiple_of(row_start, 8)
        parts = (
            ramp_real * sum_real + ramp_imag * sum_imag,
            ramp_real * sum_imag - ramp_imag * sum_real,
        )
        for part in range(2):
            value = jnp.concatenate([parts[part], jnp.zeros((8, width), F32)], axis=0)
            value = pltpu.roll(value, row_shift, 0)
            value = jnp.concatenate([value, jnp.zeros((high, ext_cols - width), F32)], axis=1)
            gradient_ref[part, pl.ds(row_start, high), :] += pltpu.roll(value, lane, 1)
    return probe_grad, descan_grad


def put_sums(probe_grad, descan_grad, keep_ref, send_ref, core, width, modes):
    for m in range(modes):
        real, imag = probe_grad[0][m], probe_grad[1][m]
        keep_ref[m * width : (m + 1) * width] = jnp.where(core == 0, real, imag)
        send_ref[m * width : (m + 1) * width] = jnp.where(core == 0, imag, real)
    block = jnp.concatenate(descan_grad + [jnp.zeros((EXTRA - 6, width), F32)], axis=0)
    keep_ref[modes * width :] = block
    send_ref[modes * width :] = block


def updated_probe(probe_ref, mine_ref, other_ref, core, total, width, modes):
    rows = modes * width
    mine, other = mine_ref[:rows], other_ref[...]
    real = probe_ref[0].reshape(rows, width) - PROBE_STEP / total * jnp.where(core == 0, mine, other)
    imag = probe_ref[1].reshape(rows, width) - PROBE_STEP / total * jnp.where(core == 0, other, mine)
    power = jnp.sum(jnp.sum(real * real + imag * imag, axis=0, keepdims=True), axis=1, keepdims=True)
    scale = jnp.sqrt(PROBE_POWER * rows * width / power)
    return real * scale, imag * scale


def halo_blocks(right, left, width):
    rim = width // 2
    low = lane_of(right.shape) < rim
    return jnp.where(low, right, pltpu.roll(left, rim, 1)), jnp.where(low, pltpu.roll(right, rim, 1), left)


def first_kernel(
    sizes, where_ref, starts, descan_ref, object_ref, probe_ref, measured_ref, tables_ref,
    top_ref, bottom_ref, right_refs, left_refs,
    extended_ref, gradient_ref, strip_right_ref, strip_left_ref, keep_ref, send_ref, wave_ref, far_ref,
):
    tile_rows, tile_cols, width, modes, count, n_fast, n_slow = sizes
    fast, slow = where_ref[0], where_ref[1]
    rim = width // 2
    for part in range(2):
        extended_ref[part, rim : rim + tile_rows, :tile_cols] = object_ref[part]
        extended_ref[part, :rim, :tile_cols] = top_ref[part]
        extended_ref[part, rim + tile_rows :, :tile_cols] = bottom_ref[part]
    at = 0
    for right, left in zip(right_refs, left_refs):
        real, imag = halo_blocks(right[...], left[...], width)
        extended_ref[0, at : at + right.shape[0], tile_cols:] = real
        extended_ref[1, at : at + right.shape[0], tile_cols:] = imag
        at += right.shape[0]
    descan_rows = [jnp.full((1, width), descan_ref[k, n], F32) for k in range(2) for n in range(3)]
    probe = tuple(probe_ref[part].reshape(modes * width, width) for part in range(2))
    probe_grad, descan_grad = gradients(
        extended_ref, probe, descan_rows, starts, measured_ref, tables_ref, gradient_ref, wave_ref, far_ref,
        sizes + (fast, slow),
    )
    put_sums(probe_grad, descan_grad, keep_ref, send_ref, lax.rem(fast, 2), width, modes)
    halo = gradient_ref[:, :, tile_cols:]
    low = lane_of(halo.shape) < rim
    strip_right_ref[...] = jnp.where(low, halo, gradient_ref[:, :, tile_cols - width : tile_cols])
    strip_left_ref[...] = jnp.where(low, gradient_ref[:, :, :width], halo)


def add_columns(gradient, right, left, tile_cols, width):
    rim = width // 2
    low = lane_of(right.shape) < rim
    zero = jnp.zeros(right.shape, F32)
    blocks = [gradient[:, :, k : k + width] for k in range(0, tile_cols + width, width)]
    blocks[0] = blocks[0] + jnp.where(low, left, zero)
    blocks[-2] = blocks[-2] + jnp.where(low, zero, right)
    blocks[-1] = blocks[-1] + jnp.where(low, right, left)
    return jnp.concatenate(blocks, axis=2)


def masked(where_ref, right, left, n_slow):
    slow = where_ref[1]
    return (
        jnp.where(slow < n_slow - 1, right, jnp.zeros_like(right)),
        jnp.where(slow > 0, left, jnp.zeros_like(left)),
    )


def rows_kernel(sizes, where_ref, gradient_ref, right_ref, left_ref, up_ref, down_ref):
    tile_rows, tile_cols, width, modes, count, n_fast, n_slow = sizes
    for out_ref, at in ((up_ref, 0), (down_ref, tile_rows)):
        right, left = masked(where_ref, right_ref[:, at : at + width], left_ref[:, at : at + width], n_slow)
        out_ref[...] = add_columns(gradient_ref[:, at : at + width], right, left, tile_cols, width)


def second_kernel(
    sizes, total, where_ref, starts, descan_ref, extended_ref, gradient_in_ref, probe_ref, measured_ref, tables_ref,
    right_ref, left_ref, above_ref, below_ref, mine_ref, other_ref,
    base_ref, up_ref, down_ref, strip_right_ref, strip_left_ref, keep_ref, send_ref, probe_out_ref, descan_out_ref,
    object_ref, gradient_ref, wave_ref, far_ref,
):
    tile_rows, tile_cols, width, modes, count, n_fast, n_slow = sizes
    fast, slow = where_ref[0], where_ref[1]
    core = lax.rem(fast, 2)
    rim = width // 2
    right, left = masked(where_ref, right_ref[...], left_ref[...], n_slow)
    object_ref[...] = extended_ref[...] - OBJECT_STEP * add_columns(
        gradient_in_ref[...], right, left, tile_cols, width
    )
    object_ref[:, :width] -= OBJECT_STEP * above_ref[...]
    object_ref[:, tile_rows:] -= OBJECT_STEP * below_ref[...]
    probe = updated_probe(probe_ref, mine_ref, other_ref, core, total, width, modes)
    probe_out_ref[0] = probe[0].reshape(modes, width, width)
    probe_out_ref[1] = probe[1].reshape(modes, width, width)
    at = modes * width
    descan_rows = [
        descan_ref[k // 3, k % 3] - DESCAN_STEP / total * mine_ref[at + k : at + k + 1] for k in range(6)
    ]
    descan_out_ref[...] = jnp.concatenate(descan_rows + [jnp.zeros((EXTRA - 6, width), F32)], axis=0)
    probe_grad, descan_grad = gradients(
        object_ref, probe, descan_rows, starts, measured_ref, tables_ref, gradient_ref, wave_ref, far_ref,
        sizes + (fast, slow),
    )
    put_sums(probe_grad, descan_grad, keep_ref, send_ref, core, width, modes)
    base_ref[...] = (
        object_ref[:, rim : rim + tile_rows, :tile_cols]
        - OBJECT_STEP * gradient_ref[:, rim : rim + tile_rows, :tile_cols]
    )
    up_ref[...] = gradient_ref[:, :rim, :tile_cols]
    down_ref[...] = gradient_ref[:, rim + tile_rows :, :tile_cols]
    real, imag = gradient_ref[0, :, tile_cols:], gradient_ref[1, :, tile_cols:]
    low = lane_of(real.shape) < rim
    strip_right_ref[...] = jnp.where(low, real, pltpu.roll(imag, rim, 1))
    strip_left_ref[...] = jnp.where(low, pltpu.roll(real, rim, 1), imag)


def edge_blocks(where_ref, right, left, n_slow, width):
    rim = width // 2
    right, left = masked(where_ref, right, left, n_slow)
    low = lane_of(right.shape) < rim
    zero = jnp.zeros(right.shape, F32)
    first = (jnp.where(low, left, zero), jnp.where(low, pltpu.roll(left, rim, 1), zero))
    last = (jnp.where(low, zero, pltpu.roll(right, rim, 1)), jnp.where(low, zero, right))
    return first, last


def last_rows_kernel(sizes, where_ref, up_in_ref, down_in_ref, right_ref, left_ref, up_ref, down_ref):
    tile_rows, tile_cols, width, modes, count, n_fast, n_slow = sizes
    rim = width // 2
    for in_ref, out_ref, at in ((up_in_ref, up_ref, 0), (down_in_ref, down_ref, rim + tile_rows)):
        out_ref[...] = in_ref[...]
        first, last = edge_blocks(where_ref, right_ref[at : at + rim], left_ref[at : at + rim], n_slow, width)
        for part in range(2):
            out_ref[part, :, :width] += first[part]
            out_ref[part, :, tile_cols - width :] += last[part]


def object_kernel(sizes, where_ref, base_ref, right_ref, left_ref, above_ref, below_ref, out_ref):
    tile_rows, tile_cols, width, modes, count, n_fast, n_slow = sizes
    rim = width // 2
    out_ref[...] = base_ref[...]
    first, last = edge_blocks(
        where_ref, right_ref[rim : rim + tile_rows], left_ref[rim : rim + tile_rows], n_slow, width
    )
    for part in range(2):
        out_ref[part, :, :width] -= OBJECT_STEP * first[part]
        out_ref[part, :, tile_cols - width :] -= OBJECT_STEP * last[part]
    out_ref[:, :rim] -= OBJECT_STEP * above_ref[...]
    out_ref[:, tile_rows - rim :] -= OBJECT_STEP * below_ref[...]


def probe_kernel(sizes, total, where_ref, probe_ref, descan_ref, mine_ref, other_ref, probe_out_ref, descan_out_ref):
    tile_rows, tile_cols, width, modes, count, n_fast, n_slow = sizes
    core = lax.rem(where_ref[0], 2)
    real, imag = updated_probe(probe_ref, mine_ref, other_ref, core, total, width, modes)
    probe_out_ref[0] = real.reshape(modes, width, width)
    probe_out_ref[1] = imag.reshape(modes, width, width)
    at = modes * width
    rows = descan_ref[...] - DESCAN_STEP / total * mine_ref[at : at + EXTRA]
    lane = lane_of((1, width))
    for k in range(2):
        values = [rows[3 * k + n : 3 * k + n + 1] for n in range(3)]
        row = jnp.where(lane == 0, values[0], jnp.where(lane == 1, values[1], values[2]))
        descan_out_ref[k : k + 1, :] = row[:, :3]


def call(kernel, outs, scratch, *operands, smem=0):
    return pl.pallas_call(
        kernel,
        out_shape=[jax.ShapeDtypeStruct(shape, F32) for shape in outs],
        in_specs=[SMEM] * smem + [VMEM] * (len(operands) - smem),
        out_specs=[VMEM] * len(outs),
        scratch_shapes=[pltpu.VMEM(shape, F32) for shape in scratch],
        compiler_params=pltpu.CompilerParams(vmem_limit_bytes=LIMIT),
    )(*operands)


def on_device(object_field, probe_modes, descan, scan_positions, amplitudes):
    width = amplitudes.shape[-1]
    rim = width // 2
    modes = probe_modes.shape[1]
    count = scan_positions.shape[1]
    tile_rows, tile_cols = object_field.shape[1:]
    n_fast, n_slow = lax.axis_size("fast"), lax.axis_size("slow")
    total = count * n_fast * n_slow
    sizes = (tile_rows, tile_cols, width, modes, count, n_fast, n_slow)
    fast, slow = lax.axis_index("fast"), lax.axis_index("slow")
    where = jnp.stack([fast, slow]).astype(jnp.int32)
    tables = transform_tables(width)
    ext_rows, ext_cols = tile_rows + width, tile_cols + width
    half_rows = modes * width

    def moved(value, step_fast, step_slow):
        pairs = []
        for f in range(n_fast):
            for s in range(n_slow):
                to_fast, to_slow = f + step_fast, s + step_slow
                if 0 <= to_fast < n_fast and 0 <= to_slow < n_slow:
                    pairs.append((f * n_slow + s, to_fast * n_slow + to_slow))
        return lax.ppermute(value, AXES, pairs)

    def across(to_right, to_left, step_fast):
        if n_slow == 2:
            pairs = [
                (f * 2 + s, (f + step_fast) * 2 + 1 - s)
                for f in range(n_fast)
                for s in range(2)
                if 0 <= f + step_fast < n_fast
            ]
            got = lax.ppermute(jnp.where(slow == 0, to_right, to_left), AXES, pairs)
            return got, got
        return moved(to_left, step_fast, -1), moved(to_right, step_fast, 1)

    def swapped(value, axis, bit):
        return lax.ppermute(value, axis, [(i, i ^ bit) for i in range(lax.axis_size(axis))])

    def summed(keep, send):
        if n_fast & (n_fast - 1) or n_slow & (n_slow - 1) or n_fast < 2:
            core = lax.rem(fast, 2)
            real = lax.psum(jnp.where(core == 0, keep, send), AXES)
            imag = lax.psum(jnp.where(core == 0, send, keep), AXES)
            return jnp.where(core == 0, real, imag), jnp.where(core == 0, imag, real)[:half_rows]
        mine = keep + swapped(send, "fast", 1)
        bit = 1
        while bit < n_slow:
            mine = mine + swapped(mine, "slow", bit)
            bit *= 2
        bit = 2
        while bit < n_fast:
            mine = mine + swapped(mine, "fast", bit)
            bit *= 2
        return mine, swapped(mine[:half_rows], "fast", 1)

    last = object_field[:, :, tile_cols - rim :]
    initial = object_field[:, :, :rim]
    to_right = jnp.concatenate([last[0], last[1]], axis=1)
    to_left = jnp.concatenate([initial[0], initial[1]], axis=1)
    top = moved(object_field[:, tile_rows - rim :], 1, 0)
    bottom = moved(object_field[:, :rim], -1, 0)
    right_mid, left_mid = across(to_right, to_left, 0)
    right_top, left_top = across(to_right[tile_rows - rim :], to_left[tile_rows - rim :], 1)
    right_bottom, left_bottom = across(to_right[:rim], to_left[:rim], -1)

    def first(where_ref, starts, descan_ref, object_ref, probe_ref, measured_ref, tables_ref, top_ref, bottom_ref,
              r0, r1, r2, l0, l1, l2, *rest):
        first_kernel(sizes, where_ref, starts, descan_ref, object_ref, probe_ref, measured_ref, tables_ref,
                     top_ref, bottom_ref, (r0, r1, r2), (l0, l1, l2), *rest)

    scratch = [(count * modes * width, 2 * width), (2 * width, count * modes * width)]
    sums = [(half_rows + EXTRA, width)] * 2
    extended, gradient, strip_right, strip_left, keep, send = call(
        first,
        [(2, ext_rows, ext_cols)] * 2 + [(2, ext_rows, width)] * 2 + sums,
        scratch,
        where, scan_positions, descan, object_field, probe_modes, amplitudes, tables, top, bottom,
        right_top, right_mid, right_bottom, left_top, left_mid, left_bottom,
        smem=3,
    )
    from_right, from_left = across(strip_right, strip_left, 0)
    up, down = call(
        functools.partial(rows_kernel, sizes), [(2, width, ext_cols)] * 2, [],
        where, gradient, from_right, from_left, smem=1,
    )
    above, below = moved(down, 1, 0), moved(up, -1, 0)
    mine, other = summed(keep, send)
    base, up, down, strip_right, strip_left, keep, send, probes, descan_rows = call(
        functools.partial(second_kernel, sizes, total),
        [(2, tile_rows, tile_cols)] + [(2, rim, tile_cols)] * 2 + [(ext_rows, width)] * 2 + sums
        + [probe_modes.shape, (EXTRA, width)],
        [(2, ext_rows, ext_cols)] * 2 + scratch,
        where, scan_positions, descan, extended, gradient, probe_modes, amplitudes, tables,
        from_right, from_left, above, below, mine, other,
        smem=3,
    )
    from_right, from_left = across(strip_right, strip_left, 0)
    up, down = call(
        functools.partial(last_rows_kernel, sizes), [(2, rim, tile_cols)] * 2, [],
        where, up, down, from_right, from_left, smem=1,
    )
    above, below = moved(down, 1, 0), moved(up, -1, 0)
    (objects,) = call(
        functools.partial(object_kernel, sizes), [(2, tile_rows, tile_cols)], [],
        where, base, from_right, from_left, above, below, smem=1,
    )
    mine, other = summed(keep, send)
    probes, descan_out = call(
        functools.partial(probe_kernel, sizes, total), [probe_modes.shape, descan.shape], [],
        where, probes, descan_rows, mine, other, smem=1,
    )
    return objects, probes, descan_out


def solution(mesh):
    placed = (P(None, "fast", "slow"), P(), P(), P(None, "fast", "slow"), P("fast", "slow", None))
    return jax.shard_map(
        on_device,
        mesh=mesh,
        in_specs=placed,
        out_specs=(P(None, "fast", "slow"), P(), P()),
        check_vma=False,
    )
```

profile of v0, /device:TPU:7, one launch (start us, length us, event | category | flops | bytes accessed | tf_op | source)
XLA Modules:
  0.0 102.4 jit_solution(17977567112024401017)
XLA Ops:
  1.7 2.7 %collective-permute-start.1 = (f32[2,64,256]{2,1,0:T(8,128)S(1)}, f32[2,64,256]{2,1,0:T(8,128)S(1)}, u32[]{:S(2)}, u32[]{:S(2)}) collective-permute-start(f32[2,64,256]{2,1,0:T(8,128)S(1)} %get-tuple-element.51), channel_id=1, source_target_pairs={{2,0},{3,1},{4,2},{5,3},{6,4},{7,5},{8,6},{9,7},{10,8},{11,9},{12,... | collective-permute-start | bytes 393224 | tf_op jit(solution)/shard_map/ppermute | solution.py:400
  4.4 3.9 %collective-permute-start = (f32[2,64,256]{2,1,0:T(8,128)S(1)}, f32[2,64,256]{2,1,0:T(8,128)S(1)}, u32[]{:S(2)}, u32[]{:S(2)}) collective-permute-start(f32[2,64,256]{2,1,0:T(8,128)S(1)} %get-tuple-element.52), channel_id=1, source_target_pairs={{0,2},{1,3},{2,4},{3,5},{4,6},{5,7},{6,8},{7,9},{8,10},{9,11},{10,... | collective-permute-start | bytes 393224 | tf_op jit(solution)/shard_map/ppermute | solution.py:400
  8.3 1.2 %slice_bitcast_fusion.2 = (f32[256,64]{1,0:T(8,128)S(1)}, f32[256,64]{1,0:T(8,128)S(1)}, f32[256,64]{1,0:T(8,128)S(1)}, f32[256,64]{1,0:T(8,128)S(1)}) fusion(f32[2,256,256]{2,1,0:T(8,128)} %object_ref.1), kind=kLoop, calls=%fused_computation.4 | loop fusion | bytes 524288 | tf_op jit(solution)/shard_map/squeeze | solution.py:436
  10.1 1.9 %collective-permute-start.4 = (f32[64,128]{1,0:T(8,128)S(1)}, f32[64,128]{1,0:T(8,128)S(1)}, u32[]{:S(2)}, u32[]{:S(2)}) collective-permute-start(f32[64,128]{1,0:T(8,128)S(1)} %get-tuple-element.45), channel_id=1, source_target_pairs={{2,1},{3,0},{4,3},{5,2},{6,5},{7,4},{8,7},{9,6},{10,9},{11,8},{12,... | collective-permute-start | bytes 98312 | tf_op jit(solution)/shard_map/ppermute | solution.py:410
  12.0 5.4 %collective-permute-start.2 = (f32[64,128]{1,0:T(8,128)S(1)}, f32[64,128]{1,0:T(8,128)S(1)}, u32[]{:S(2)}, u32[]{:S(2)}) collective-permute-start(f32[64,128]{1,0:T(8,128)S(1)} %get-tuple-element.46), channel_id=1, source_target_pairs={{0,3},{1,2},{2,5},{3,4},{4,7},{5,6},{6,9},{7,8},{8,11},{9,10},{10,... | collective-permute-start | bytes 98312 | tf_op jit(solution)/shard_map/ppermute | solution.py:410
  18.6 3.2 %shard_map.85 = (f32[2,384,384]{2,1,0:T(8,128)S(1)}, f32[2,384,384]{2,1,0:T(8,128)S(1)}, f32[2,384,128]{2,1,0:T(8,128)S(1)}, f32[2,384,128]{2,1,0:T(8,128)S(1)},...) custom-call(s32[2]{0:T(128)S(1)} %pad_add_fusion.where_ref, s32[2,2,1]{2,1,0:T(2,128)S(1)} %copy.10.starts, ...), custom_call_target="tpu_custom_call" | custom-call | tf_op jit(solution)/shard_map/pallas_call | solution.py:368
  23.3 1.2 %collective-permute-start.9 = (f32[264,128]{1,0:T(8,128)S(1)}, f32[264,128]{1,0:T(8,128)S(1)}, u32[]{:S(2)}, u32[]{:S(2)}) collective-permute-start(f32[264,128]{1,0:T(8,128)S(1)} %add.30), channel_id=1, source_target_pairs={{0,1},{1,0},{2,3},{3,2},{4,5},{5,4},{6,7},{7,6},{8,9},{9,8},{10,11... | collective-permute-start | bytes 405512 | tf_op jit(solution)/shard_map/ppermute | solution.py:415
  24.5 11.3 %collective-permute-done.9 = f32[264,128]{1,0:T(8,128)S(1)} collective-permute-done((f32[264,128]{1,0:T(8,128)S(1)}, f32[264,128]{1,0:T(8,128)S(1)}, u32[]{:S(2)}, u32[]{:S(2)}) %collective-permute-start.9) | collective-permute-done | bytes 135200 | tf_op jit(solution)/shard_map/ppermute | solution.py:415
  36.0 3.8 %collective-permute-done.10 = f32[264,128]{1,0:T(8,128)S(1)} collective-permute-done((f32[264,128]{1,0:T(8,128)S(1)}, f32[264,128]{1,0:T(8,128)S(1)}, u32[]{:S(2)}, u32[]{:S(2)}) %collective-permute-start.10) | collective-permute-done | bytes 135200 | tf_op jit(solution)/shard_map/ppermute | solution.py:415
  39.8 3.7 %collective-permute-start.11 = (f32[264,128]{1,0:T(8,128)S(1)}, f32[264,128]{1,0:T(8,128)S(1)}, u32[]{:S(2)}, u32[]{:S(2)}) collective-permute-start(f32[264,128]{1,0:T(8,128)S(1)} %add.32), channel_id=1, source_target_pairs={{0,8},{2,10},{4,12},{6,14},{8,0},{10,2},{12,4},{14,6},{16,24},{18,... | collective-permute-start | bytes 405512 | tf_op jit(solution)/shard_map/ppermute | solution.py:415
  44.1 4.4 %collective-permute-start.6 = (f32[2,128,384]{2,1,0:T(8,128)S(1)}, f32[2,128,384]{2,1,0:T(8,128)S(1)}, u32[]{:S(2)}, u32[]{:S(2)}) collective-permute-start(f32[2,128,384]{2,1,0:T(8,128)S(1)} %get-tuple-element.28), channel_id=1, source_target_pairs={{0,2},{1,3},{2,4},{3,5},{4,6},{5,7},{6,8},{7,9},{8,10},{9,11},{10,... | collective-permute-start | bytes 1179656 | tf_op jit(solution)/shard_map/ppermute | solution.py:400
  48.5 1.9 %collective-permute-start.7 = (f32[2,128,384]{2,1,0:T(8,128)S(1)}, f32[2,128,384]{2,1,0:T(8,128)S(1)}, u32[]{:S(2)}, u32[]{:S(2)}) collective-permute-start(f32[2,128,384]{2,1,0:T(8,128)S(1)} %get-tuple-element.29), channel_id=1, source_target_pairs={{2,0},{3,1},{4,2},{5,3},{6,4},{7,5},{8,6},{9,7},{10,8},{11,9},{12,... | collective-permute-start | bytes 1179656 | tf_op jit(solution)/shard_map/ppermute | solution.py:400
  50.5 2.8 %collective-permute-start.12 = (f32[264,128]{1,0:T(8,128)S(1)}, f32[264,128]{1,0:T(8,128)S(1)}, u32[]{:S(2)}, u32[]{:S(2)}) collective-permute-start(f32[264,128]{1,0:T(8,128)S(1)} %add.33), channel_id=1, source_target_pairs={{0,16},{2,18},{4,20},{6,22},{8,24},{10,26},{12,28},{14,30},{16,0},... | collective-permute-start | bytes 405512 | tf_op jit(solution)/shard_map/ppermute | solution.py:415
  53.3 6.4 %collective-permute-done.12 = f32[264,128]{1,0:T(8,128)S(1)} collective-permute-done((f32[264,128]{1,0:T(8,128)S(1)}, f32[264,128]{1,0:T(8,128)S(1)}, u32[]{:S(2)}, u32[]{:S(2)}) %collective-permute-start.12) | collective-permute-done | bytes 135200 | tf_op jit(solution)/shard_map/ppermute | solution.py:415
  61.8 3.7 %shard_map.87 = (f32[2,256,256]{2,1,0:T(8,128)S(1)}, f32[2,64,256]{2,1,0:T(8,128)S(1)}, f32[2,64,256]{2,1,0:T(8,128)S(1)}, f32[384,128]{1,0:T(8,128)S(1)}, f32[3...) custom-call(s32[2]{0:T(128)S(1)} %pad_add_fusion.where_ref, ...), custom_call_target="tpu_custom_call" | custom-call | tf_op jit(solution)/shard_map/pallas_call | solution.py:368
  67.3 4.6 %collective-permute-done.18 = f32[264,128]{1,0:T(8,128)S(1)} collective-permute-done((f32[264,128]{1,0:T(8,128)S(1)}, f32[264,128]{1,0:T(8,128)S(1)}, u32[]{:S(2)}, u32[]{:S(2)}) %collective-permute-start.18) | collective-permute-done | bytes 135200 | tf_op jit(solution)/shard_map/ppermute | solution.py:415
  71.9 4.4 %collective-permute-start.19 = (f32[264,128]{1,0:T(8,128)S(1)}, f32[264,128]{1,0:T(8,128)S(1)}, u32[]{:S(2)}, u32[]{:S(2)}) collective-permute-start(f32[264,128]{1,0:T(8,128)S(1)} %add.36), channel_id=1, source_target_pairs={{0,4},{2,6},{4,0},{6,2},{8,12},{10,14},{12,8},{14,10},{16,20},{18,... | collective-permute-start | bytes 405512 | tf_op jit(solution)/shard_map/ppermute | solution.py:415
  76.3 2.7 %collective-permute-done.19 = f32[264,128]{1,0:T(8,128)S(1)} collective-permute-done((f32[264,128]{1,0:T(8,128)S(1)}, f32[264,128]{1,0:T(8,128)S(1)}, u32[]{:S(2)}, u32[]{:S(2)}) %collective-permute-start.19) | collective-permute-done | bytes 135200 | tf_op jit(solution)/shard_map/ppermute | solution.py:415
  79.5 3.5 %collective-permute-done.20 = f32[264,128]{1,0:T(8,128)S(1)} collective-permute-done((f32[264,128]{1,0:T(8,128)S(1)}, f32[264,128]{1,0:T(8,128)S(1)}, u32[]{:S(2)}, u32[]{:S(2)}) %collective-permute-start.20) | collective-permute-done | bytes 135200 | tf_op jit(solution)/shard_map/ppermute | solution.py:415
  84.4 7.9 %collective-permute-start.15 = (f32[2,64,256]{2,1,0:T(8,128)S(1)}, f32[2,64,256]{2,1,0:T(8,128)S(1)}, u32[]{:S(2)}, u32[]{:S(2)}) collective-permute-start(f32[2,64,256]{2,1,0:T(8,128)S(1)} %get-tuple-element.37), channel_id=1, source_target_pairs={{0,2},{1,3},{2,4},{3,5},{4,6},{5,7},{6,8},{7,9},{8,10},{9,11},{10,... | collective-permute-start | bytes 393224 | tf_op jit(solution)/shard_map/ppermute | solution.py:400
  92.3 1.9 %collective-permute-start.16 = (f32[2,64,256]{2,1,0:T(8,128)S(1)}, f32[2,64,256]{2,1,0:T(8,128)S(1)}, u32[]{:S(2)}, u32[]{:S(2)}) collective-permute-start(f32[2,64,256]{2,1,0:T(8,128)S(1)} %get-tuple-element.38), channel_id=1, source_target_pairs={{2,0},{3,1},{4,2},{5,3},{6,4},{7,5},{8,6},{9,7},{10,8},{11,9},{12,... | collective-permute-start | bytes 393224 | tf_op jit(solution)/shard_map/ppermute | solution.py:400
  94.3 5.1 %collective-permute-done.16.below_ref = f32[2,64,256]{2,1,0:T(8,128)S(1)} collective-permute-done((f32[2,64,256]{2,1,0:T(8,128)S(1)}, f32[2,64,256]{2,1,0:T(8,128)S(1)}, u32[]{:S(2)}, u32[]{:S(2)}) %collective-permute-start.16) | collective-permute-done | bytes 131104 | tf_op jit(solution)/shard_map/ppermute | solution.py:400
  99.5 1.5 %shard_map.89 = f32[2,256,256]{2,1,0:T(8,128)} custom-call(s32[2]{0:T(128)S(1)} %pad_add_fusion.where_ref, f32[2,256,256]{2,1,0:T(8,128)S(1)} %get-tuple-element.32.base_ref, f32[384,128]{1,0:T(8,128)S(1)} %collective-permute-done.14.right_ref.left_ref, f32[384,128]{1,0:T(8,128)S(1)} %collective-permute-done.14.right_ref.left_ref, ...), custom_call_target="tpu_custom_call" | custom-call | tf_op jit(solution)/shard_map/pallas_call | solution.py:368
  100.9 1.4 %shard_map.90 = (f32[2,2,128,128]{3,2,1,0:T(8,128)}, f32[2,3]{1,0:T(2,128)}) custom-call(s32[2]{0:T(128)S(1)} %pad_add_fusion.where_ref, f32[2,2,128,128]{3,2,1,0:T(8,128)S(1)} %get-tuple-element.39.probe_ref, f32[8,128]{1,0:T(8,128)S(1)} %get-tuple-element.40.descan_ref, f32[264,128]{1,0:T(8,128)S(1)} %add.39.mine_ref, ...), custom_call_target="tpu_custom_call" | custom-call | tf_op jit(solution)/shard_map/pallas_call | solution.py:368
  (60 shorter events, 10.7 us)
Async XLA Ops:
  1.6 16.9 %copy-start = (f32[2,256,256]{2,1,0:T(8,128)S(1)}, f32[2,256,256]{2,1,0:T(8,128)}, u32[]{:S(2)}) copy-start(f32[2,256,256]{2,1,0:T(8,128)} %object_ref.1) | copy-start | bytes 1572868
  1.7 16.8 %collective-permute-start.1 = (f32[2,64,256]{2,1,0:T(8,128)S(1)}, f32[2,64,256]{2,1,0:T(8,128)S(1)}, u32[]{:S(2)}, u32[]{:S(2)}) collective-permute-start(f32[2,64,256]{2,1,0:T(8,128)S(1)} %get-tuple-element.51), channel_id=1, source_target_pairs={{2,0},{3,1},{4,2},{5,3},{6,4},{7,5},{8,6},{9,7},{10,8},{11,9},{12,... | collective-permute-start | bytes 393224 | tf_op jit(solution)/shard_map/ppermute | solution.py:400
  4.4 14.1 %collective-permute-start = (f32[2,64,256]{2,1,0:T(8,128)S(1)}, f32[2,64,256]{2,1,0:T(8,128)S(1)}, u32[]{:S(2)}, u32[]{:S(2)}) collective-permute-start(f32[2,64,256]{2,1,0:T(8,128)S(1)} %get-tuple-element.52), channel_id=1, source_target_pairs={{0,2},{1,3},{2,4},{3,5},{4,6},{5,7},{6,8},{7,9},{8,10},{9,11},{10,... | collective-permute-start | bytes 393224 | tf_op jit(solution)/shard_map/ppermute | solution.py:400
  9.7 8.8 %collective-permute-start.3 = (f32[256,128]{1,0:T(8,128)S(1)}, f32[256,128]{1,0:T(8,128)S(1)}, u32[]{:S(2)}, u32[]{:S(2)}) collective-permute-start(f32[256,128]{1,0:T(8,128)S(1)} %maximum_select_fusion), channel_id=1, source_target_pairs={{0,1},{1,0},{2,3},{3,2},{4,5},{5,4},{6,7},{7,6},{8,9},{9,8},{10,11... | collective-permute-start | bytes 393224 | tf_op jit(solution)/shard_map/ppermute | solution.py:410
  10.1 7.6 %collective-permute-start.4 = (f32[64,128]{1,0:T(8,128)S(1)}, f32[64,128]{1,0:T(8,128)S(1)}, u32[]{:S(2)}, u32[]{:S(2)}) collective-permute-start(f32[64,128]{1,0:T(8,128)S(1)} %get-tuple-element.45), channel_id=1, source_target_pairs={{2,1},{3,0},{4,3},{5,2},{6,5},{7,4},{8,7},{9,6},{10,9},{11,8},{12,... | collective-permute-start | bytes 98312 | tf_op jit(solution)/shard_map/ppermute | solution.py:410
  12.0 6.5 %collective-permute-start.2 = (f32[64,128]{1,0:T(8,128)S(1)}, f32[64,128]{1,0:T(8,128)S(1)}, u32[]{:S(2)}, u32[]{:S(2)}) collective-permute-start(f32[64,128]{1,0:T(8,128)S(1)} %get-tuple-element.46), channel_id=1, source_target_pairs={{0,3},{1,2},{2,5},{3,4},{4,7},{5,6},{6,9},{7,8},{8,11},{9,10},{10,... | collective-permute-start | bytes 98312 | tf_op jit(solution)/shard_map/ppermute | solution.py:410
  21.8 1.4 %collective-permute-start.8 = (f32[264,128]{1,0:T(8,128)S(1)}, f32[264,128]{1,0:T(8,128)S(1)}, u32[]{:S(2)}, u32[]{:S(2)}) collective-permute-start(f32[264,128]{1,0:T(8,128)S(1)} %get-tuple-element.31), channel_id=1, source_target_pairs={{0,2},{2,0},{4,6},{6,4},{8,10},{10,8},{12,14},{14,12},{16,18},{18,... | collective-permute-start | bytes 405512 | tf_op jit(solution)/shard_map/ppermute | solution.py:415
  22.3 21.2 %collective-permute-start.5 = (f32[2,384,128]{2,1,0:T(8,128)S(1)}, f32[2,384,128]{2,1,0:T(8,128)S(1)}, u32[]{:S(2)}, u32[]{:S(2)}) collective-permute-start(f32[2,384,128]{2,1,0:T(8,128)S(1)} %broadcast_select_fusion), channel_id=1, source_target_pairs={{0,1},{1,0},{2,3},{3,2},{4,5},{5,4},{6,7},{7,6},{8,9},{9,8},{10,11... | collective-permute-start | bytes 1179656 | tf_op jit(solution)/shard_map/ppermute | solution.py:410
  23.3 12.6 %collective-permute-start.9 = (f32[264,128]{1,0:T(8,128)S(1)}, f32[264,128]{1,0:T(8,128)S(1)}, u32[]{:S(2)}, u32[]{:S(2)}) collective-permute-start(f32[264,128]{1,0:T(8,128)S(1)} %add.30), channel_id=1, source_target_pairs={{0,1},{1,0},{2,3},{3,2},{4,5},{5,4},{6,7},{7,6},{8,9},{9,8},{10,11... | collective-permute-start | bytes 405512 | tf_op jit(solution)/shard_map/ppermute | solution.py:415
  35.9 3.9 %collective-permute-start.10 = (f32[264,128]{1,0:T(8,128)S(1)}, f32[264,128]{1,0:T(8,128)S(1)}, u32[]{:S(2)}, u32[]{:S(2)}) collective-permute-start(f32[264,128]{1,0:T(8,128)S(1)} %add.31), channel_id=1, source_target_pairs={{0,4},{2,6},{4,0},{6,2},{8,12},{10,14},{12,8},{14,10},{16,20},{18,... | collective-permute-start | bytes 405512 | tf_op jit(solution)/shard_map/ppermute | solution.py:415
  39.8 10.6 %collective-permute-start.11 = (f32[264,128]{1,0:T(8,128)S(1)}, f32[264,128]{1,0:T(8,128)S(1)}, u32[]{:S(2)}, u32[]{:S(2)}) collective-permute-start(f32[264,128]{1,0:T(8,128)S(1)} %add.32), channel_id=1, source_target_pairs={{0,8},{2,10},{4,12},{6,14},{8,0},{10,2},{12,4},{14,6},{16,24},{18,... | collective-permute-start | bytes 405512 | tf_op jit(solution)/shard_map/ppermute | solution.py:415
  44.1 16.7 %collective-permute-start.6 = (f32[2,128,384]{2,1,0:T(8,128)S(1)}, f32[2,128,384]{2,1,0:T(8,128)S(1)}, u32[]{:S(2)}, u32[]{:S(2)}) collective-permute-start(f32[2,128,384]{2,1,0:T(8,128)S(1)} %get-tuple-element.28), channel_id=1, source_target_pairs={{0,2},{1,3},{2,4},{3,5},{4,6},{5,7},{6,8},{7,9},{8,10},{9,11},{10,... | collective-permute-start | bytes 1179656 | tf_op jit(solution)/shard_map/ppermute | solution.py:400
  48.5 12.3 %collective-permute-start.7 = (f32[2,128,384]{2,1,0:T(8,128)S(1)}, f32[2,128,384]{2,1,0:T(8,128)S(1)}, u32[]{:S(2)}, u32[]{:S(2)}) collective-permute-start(f32[2,128,384]{2,1,0:T(8,128)S(1)} %get-tuple-element.29), channel_id=1, source_target_pairs={{2,0},{3,1},{4,2},{5,3},{6,4},{7,5},{8,6},{9,7},{10,8},{11,9},{12,... | collective-permute-start | bytes 1179656 | tf_op jit(solution)/shard_map/ppermute | solution.py:400
  50.5 9.2 %collective-permute-start.12 = (f32[264,128]{1,0:T(8,128)S(1)}, f32[264,128]{1,0:T(8,128)S(1)}, u32[]{:S(2)}, u32[]{:S(2)}) collective-permute-start(f32[264,128]{1,0:T(8,128)S(1)} %add.33), channel_id=1, source_target_pairs={{0,16},{2,18},{4,20},{6,22},{8,24},{10,26},{12,28},{14,30},{16,0},... | collective-permute-start | bytes 405512 | tf_op jit(solution)/shard_map/ppermute | solution.py:415
  59.7 2.1 %collective-permute-start.13 = (f32[256,128]{1,0:T(8,128)S(1)}, f32[256,128]{1,0:T(8,128)S(1)}, u32[]{:S(2)}, u32[]{:S(2)}) collective-permute-start(f32[256,128]{1,0:T(8,128)S(1)} %slice.62), channel_id=1, source_target_pairs={{0,2},{2,0},{4,6},{6,4},{8,10},{10,8},{12,14},{14,12},{16,18},{18,... | collective-permute-start | bytes 393224 | tf_op jit(solution)/shard_map/ppermute | solution.py:415
  65.5 1.4 %collective-permute-start.17 = (f32[264,128]{1,0:T(8,128)S(1)}, f32[264,128]{1,0:T(8,128)S(1)}, u32[]{:S(2)}, u32[]{:S(2)}) collective-permute-start(f32[264,128]{1,0:T(8,128)S(1)} %get-tuple-element.42), channel_id=1, source_target_pairs={{0,2},{2,0},{4,6},{6,4},{8,10},{10,8},{12,14},{14,12},{16,18},{18,... | collective-permute-start | bytes 405512 | tf_op jit(solution)/shard_map/ppermute | solution.py:415
  67.0 4.9 %collective-permute-start.18 = (f32[264,128]{1,0:T(8,128)S(1)}, f32[264,128]{1,0:T(8,128)S(1)}, u32[]{:S(2)}, u32[]{:S(2)}) collective-permute-start(f32[264,128]{1,0:T(8,128)S(1)} %add.35), channel_id=1, source_target_pairs={{0,1},{1,0},{2,3},{3,2},{4,5},{5,4},{6,7},{7,6},{8,9},{9,8},{10,11... | collective-permute-start | bytes 405512 | tf_op jit(solution)/shard_map/ppermute | solution.py:415
  71.9 7.2 %collective-permute-start.19 = (f32[264,128]{1,0:T(8,128)S(1)}, f32[264,128]{1,0:T(8,128)S(1)}, u32[]{:S(2)}, u32[]{:S(2)}) collective-permute-start(f32[264,128]{1,0:T(8,128)S(1)} %add.36), channel_id=1, source_target_pairs={{0,4},{2,6},{4,0},{6,2},{8,12},{10,14},{12,8},{14,10},{16,20},{18,... | collective-permute-start | bytes 405512 | tf_op jit(solution)/shard_map/ppermute | solution.py:415
  79.1 3.9 %collective-permute-start.20 = (f32[264,128]{1,0:T(8,128)S(1)}, f32[264,128]{1,0:T(8,128)S(1)}, u32[]{:S(2)}, u32[]{:S(2)}) collective-permute-start(f32[264,128]{1,0:T(8,128)S(1)} %add.37), channel_id=1, source_target_pairs={{0,8},{2,10},{4,12},{6,14},{8,0},{10,2},{12,4},{14,6},{16,24},{18,... | collective-permute-start | bytes 405512 | tf_op jit(solution)/shard_map/ppermute | solution.py:415
  79.2 4.6 %collective-permute-start.14 = (f32[384,128]{1,0:T(8,128)S(1)}, f32[384,128]{1,0:T(8,128)S(1)}, u32[]{:S(2)}, u32[]{:S(2)}) collective-permute-start(f32[384,128]{1,0:T(8,128)S(1)} %broadcast_select_fusion.1), channel_id=1, source_target_pairs={{0,1},{1,0},{2,3},{3,2},{4,5},{5,4},{6,7},{7,6},{8,9},{9,8},{10,11... | collective-permute-start | bytes 589832 | tf_op jit(solution)/shard_map/ppermute | solution.py:410
  83.0 11.2 %collective-permute-start.21 = (f32[264,128]{1,0:T(8,128)S(1)}, f32[264,128]{1,0:T(8,128)S(1)}, u32[]{:S(2)}, u32[]{:S(2)}) collective-permute-start(f32[264,128]{1,0:T(8,128)S(1)} %add.38), channel_id=1, source_target_pairs={{0,16},{2,18},{4,20},{6,22},{8,24},{10,26},{12,28},{14,30},{16,0},... | collective-permute-start | bytes 405512 | tf_op jit(solution)/shard_map/ppermute | solution.py:415
  84.4 9.9 %collective-permute-start.15 = (f32[2,64,256]{2,1,0:T(8,128)S(1)}, f32[2,64,256]{2,1,0:T(8,128)S(1)}, u32[]{:S(2)}, u32[]{:S(2)}) collective-permute-start(f32[2,64,256]{2,1,0:T(8,128)S(1)} %get-tuple-element.37), channel_id=1, source_target_pairs={{0,2},{1,3},{2,4},{3,5},{4,6},{5,7},{6,8},{7,9},{8,10},{9,11},{10,... | collective-permute-start | bytes 393224 | tf_op jit(solution)/shard_map/ppermute | solution.py:400
  92.3 7.2 %collective-permute-start.16 = (f32[2,64,256]{2,1,0:T(8,128)S(1)}, f32[2,64,256]{2,1,0:T(8,128)S(1)}, u32[]{:S(2)}, u32[]{:S(2)}) collective-permute-start(f32[2,64,256]{2,1,0:T(8,128)S(1)} %get-tuple-element.38), channel_id=1, source_target_pairs={{2,0},{3,1},{4,2},{5,3},{6,4},{7,5},{8,6},{9,7},{10,8},{11,9},{12,... | collective-permute-start | bytes 393224 | tf_op jit(solution)/shard_map/ppermute | solution.py:400
  94.3 6.7 %collective-permute-start.22 = (f32[256,128]{1,0:T(8,128)S(1)}, f32[256,128]{1,0:T(8,128)S(1)}, u32[]{:S(2)}, u32[]{:S(2)}) collective-permute-start(f32[256,128]{1,0:T(8,128)S(1)} %slice.63), channel_id=1, source_target_pairs={{0,2},{2,0},{4,6},{6,4},{8,10},{10,8},{12,14},{14,12},{16,18},{18,... | collective-permute-start | bytes 393224 | tf_op jit(solution)/shard_map/ppermute | solution.py:415
  (5 other events, 83.4 us)
where the time goes:
time: 103 us; the launch traced here: 102 us
  starting transfers between devices  46.3 us (45%)
  waiting for transfers between devices  41 us (40%)
  Pallas kernels  11.2 us (11%)
  local copies, waits for them, and re-layouts  2.38 us (2%)
    ppermute x12, waiting for transfers between devices, swapped(): lax.ppermute(value, axis, [(i, i ^ bit) for i in range(lax.axis_size(axis...  34.4 us
    ppermute x6, starting transfers between devices, moved(): return lax.ppermute(value, AXES, pairs)  22.7 us
    ppermute x12, starting transfers between devices, swapped(): lax.ppermute(value, axis, [(i, i ^ bit) for i in range(lax.axis_size(axis...  14.8 us
    pallas_call x6, Pallas kernels, call(): pl.pallas_call(kernel, out_shape=[jax.ShapeDtypeStruct(shape, F32) for sh...  11.2 us
    ppermute x5, starting transfers between devices, across(): got = lax.ppermute(jnp.where(slow == 0, to_right, to_left), AXES, pairs)  8.91 us
    ppermute x6, waiting for transfers between devices, moved(): return lax.ppermute(value, AXES, pairs)  5.13 us
  transfers between devices with their start and end apart: 23, of which 11 were waited for; matrix products, arithmetic and copies ran while one was open for 2% of the time, Pallas kernels for 3%

commit v1 on v0

--- a/solution.py
+++ b/solution.py
@@ -14,14 +14,15 @@
 DESCAN_STEP = 0.02
 FLOOR_LEVEL = 0.25
 PROBE_POWER = 0.5
-LANES = 128
 EXTRA = 8
 AXES = ("fast", "slow")
 F32 = jnp.float32
 BF16 = jnp.bfloat16
 VMEM = pl.BlockSpec(memory_space=pltpu.VMEM)
 SMEM = pl.BlockSpec(memory_space=pltpu.SMEM)
+HBM = pl.BlockSpec(memory_space=pltpu.HBM)
 LIMIT = 40 * 1024 * 1024
+WORK = 2_000_000_000
 
 
 def transform_tables(width):
@@ -58,8 +59,8 @@
 
 def window_place(starts, j, tile_rows, tile_cols, width, fast, slow):
     rim = width // 2
-    row = starts[0, j, 0] - fast * tile_rows + rim
-    col = starts[1, j, 0] - slow * tile_cols
+    row = starts[0, 0, j] - fast * tile_rows + rim
+    col = starts[1, 0, j] - slow * tile_cols
     lane = jnp.where(col < 0, col + tile_cols + width, col)
     block = jnp.minimum(row // 8, (tile_rows + width - width - 8) // 8)
     return block * 8, row - block * 8, lane
@@ -80,8 +81,8 @@
     fractions = []
     phases = []
     for j in range(count):
-        frac_row = jnp.full((1, width), starts[0, j, 0], jnp.int32).astype(F32) / (tile_rows * n_fast)
-        frac_col = jnp.full((1, width), starts[1, j, 0], jnp.int32).astype(F32) / (tile_cols * n_slow)
+        frac_row = jnp.full((1, width), starts[0, 0, j], jnp.int32).astype(F32) / (tile_rows * n_fast)
+        frac_col = jnp.full((1, width), starts[1, 0, j], jnp.int32).astype(F32) / (tile_cols * n_slow)
         fractions.append((frac_row, frac_col))
         for k in range(2):
             d = descan_rows[3 * k : 3 * k + 3]
@@ -190,6 +191,16 @@
     return probe_grad, descan_grad
 
 
+def pick(parity, when_even, when_odd):
+    return jnp.where(parity == 0, when_even, when_odd)
+
+
+def both_sides(parity, even_ref, odd_ref, index=Ellipsis):
+    even = even_ref[index]
+    odd = jnp.zeros_like(even) if odd_ref is None else odd_ref[index]
+    return pick(parity, even, odd), pick(parity, odd, even)
+
+
 def put_sums(probe_grad, descan_grad, keep_ref, send_ref, core, width, modes):
     for m in range(modes):
         real, imag = probe_grad[0][m], probe_grad[1][m]
@@ -216,35 +227,72 @@
     return jnp.where(low, right, pltpu.roll(left, rim, 1)), jnp.where(low, pltpu.roll(right, rim, 1), left)
 
 
+def pack_kernel(sizes, where_ref, object_ref, extended_ref, rows_even_ref, rows_odd_ref, *rest):
+    tile_rows, tile_cols, width, modes, count, n_fast, n_slow = sizes
+    rim = width // 2
+    *rest, semaphore = rest
+    inner = extended_ref.at[:, rim : rim + tile_rows, :tile_cols]
+    copy = pltpu.make_async_copy(object_ref, inner, semaphore)
+    copy.start()
+    copy.wait()
+    fast, slow = lax.rem(where_ref[0], 2), lax.rem(where_ref[1], 2)
+    initial, final = extended_ref[:, rim:width, :tile_cols], extended_ref[:, tile_rows : rim + tile_rows, :tile_cols]
+    rows_even_ref[...] = pick(fast, final, initial)
+    rows_odd_ref[...] = pick(fast, initial, final)
+    low = lane_of((tile_rows, width)) < rim
+    end = extended_ref[:, rim : rim + tile_rows, tile_cols - width : tile_cols]
+    start = extended_ref[:, rim : rim + tile_rows, :width]
+    to_right = jnp.where(low, pltpu.roll(end[0], rim, 1), end[1])
+    to_left = jnp.where(low, start[0], pltpu.roll(start[1], rim, 1))
+    strips = (pick(slow, to_right, to_left), pick(slow, to_left, to_right))
+    for k in range(len(rest) // 3):
+        strip = strips[k]
+        rest[3 * k][...] = strip
+        rest[3 * k + 1][...] = pick(fast, strip[tile_rows - rim :], strip[:rim])
+        rest[3 * k + 2][...] = pick(fast, strip[:rim], strip[tile_rows - rim :])
+
+
 def first_kernel(
-    sizes, where_ref, starts, descan_ref, object_ref, probe_ref, measured_ref, tables_ref,
-    top_ref, bottom_ref, right_refs, left_refs,
-    extended_ref, gradient_ref, strip_right_ref, strip_left_ref, keep_ref, send_ref, wave_ref, far_ref,
+    sizes, info, starts, descan_ref, extended_in_ref, probe_ref, measured_ref, tables_ref,
+    rows_even_ref, rows_odd_ref, halos,
+    extended_ref, gradient_ref, strips, keep_ref, send_ref, wave_ref, far_ref,
 ):
     tile_rows, tile_cols, width, modes, count, n_fast, n_slow = sizes
-    fast, slow = where_ref[0], where_ref[1]
-    rim = width // 2
-    for part in range(2):
-        extended_ref[part, rim : rim + tile_rows, :tile_cols] = object_ref[part]
-        extended_ref[part, :rim, :tile_cols] = top_ref[part]
-        extended_ref[part, rim + tile_rows :, :tile_cols] = bottom_ref[part]
-    at = 0
-    for right, left in zip(right_refs, left_refs):
-        real, imag = halo_blocks(right[...], left[...], width)
-        extended_ref[0, at : at + right.shape[0], tile_cols:] = real
-        extended_ref[1, at : at + right.shape[0], tile_cols:] = imag
-        at += right.shape[0]
-    descan_rows = [jnp.full((1, width), descan_ref[k, n], F32) for k in range(2) for n in range(3)]
+    fast, slow = info[0], info[1]
+    core = lax.rem(fast, 2)
+    rim = width // 2
+    below, above = both_sides(core, rows_even_ref, rows_odd_ref)
+    extended_ref[:, :rim, :tile_cols] = above
+    extended_ref[:, rim + tile_rows :, :tile_cols] = below
+    columns = []
+    for middle_ref, even_ref, odd_ref in halos:
+        after, before = both_sides(core, even_ref, odd_ref)
+        columns.append(((0, before), (rim, middle_ref[...]), (rim + tile_rows, after)))
+    for piece in range(3):
+        at, even = columns[0][piece]
+        odd = columns[-1][piece][1]
+        real, imag = halo_blocks(pick(lax.rem(slow, 2), even, odd), pick(lax.rem(slow, 2), odd, even), width)
+        extended_ref[0, at : at + even.shape[0], tile_cols:] = real
+        extended_ref[1, at : at + even.shape[0], tile_cols:] = imag
+    descan_rows = [jnp.full((1, width), descan_ref[k // 3, k % 3], F32) for k in range(6)]
     probe = tuple(probe_ref[part].reshape(modes * width, width) for part in range(2))
     probe_grad, descan_grad = gradients(
         extended_ref, probe, descan_rows, starts, measured_ref, tables_ref, gradient_ref, wave_ref, far_ref,
         sizes + (fast, slow),
     )
-    put_sums(probe_grad, descan_grad, keep_ref, send_ref, lax.rem(fast, 2), width, modes)
+    put_sums(probe_grad, descan_grad, keep_ref, send_ref, core, width, modes)
     halo = gradient_ref[:, :, tile_cols:]
     low = lane_of(halo.shape) < rim
-    strip_right_ref[...] = jnp.where(low, halo, gradient_ref[:, :, tile_cols - width : tile_cols])
-    strip_left_ref[...] = jnp.where(low, gradient_ref[:, :, :width], halo)
+    to_right = jnp.where(low, halo, gradient_ref[:, :, tile_cols - width : tile_cols])
+    to_left = jnp.where(low, gradient_ref[:, :, :width], halo)
+    put_strips(slow, to_right, to_left, strips)
+
+
+def put_strips(place, to_next, to_previous, refs):
+    parity = lax.rem(place, 2)
+    refs[0][...] = pick(parity, to_next, to_previous)
+    if len(refs) > 1:
+        refs[1][...] = pick(parity, to_previous, to_next)
 
 
 def add_columns(gradient, right, left, tile_cols, width):
@@ -258,37 +306,34 @@
     return jnp.concatenate(blocks, axis=2)
 
 
-def masked(where_ref, right, left, n_slow):
-    slow = where_ref[1]
-    return (
-        jnp.where(slow < n_slow - 1, right, jnp.zeros_like(right)),
-        jnp.where(slow > 0, left, jnp.zeros_like(left)),
-    )
-
-
-def rows_kernel(sizes, where_ref, gradient_ref, right_ref, left_ref, up_ref, down_ref):
-    tile_rows, tile_cols, width, modes, count, n_fast, n_slow = sizes
-    for out_ref, at in ((up_ref, 0), (down_ref, tile_rows)):
-        right, left = masked(where_ref, right_ref[:, at : at + width], left_ref[:, at : at + width], n_slow)
-        out_ref[...] = add_columns(gradient_ref[:, at : at + width], right, left, tile_cols, width)
+def rows_kernel(sizes, where_ref, gradient_ref, columns, token_ref, even_ref, odd_ref):
+    tile_rows, tile_cols, width, modes, count, n_fast, n_slow = sizes
+    slow = lax.rem(where_ref[1], 2)
+    edges = []
+    for at in (0, tile_rows):
+        index = (slice(None), slice(at, at + width))
+        right, left = both_sides(slow, *columns, index)
+        edges.append(add_columns(gradient_ref[index], right, left, tile_cols, width))
+    put_strips(where_ref[0], edges[1], edges[0], (even_ref, odd_ref))
 
 
 def second_kernel(
     sizes, total, where_ref, starts, descan_ref, extended_ref, gradient_in_ref, probe_ref, measured_ref, tables_ref,
-    right_ref, left_ref, above_ref, below_ref, mine_ref, other_ref,
-    base_ref, up_ref, down_ref, strip_right_ref, strip_left_ref, keep_ref, send_ref, probe_out_ref, descan_out_ref,
+    columns, rows_even_ref, rows_odd_ref, mine_ref, other_ref,
+    base_ref, up_ref, down_ref, strips, keep_ref, send_ref, probe_out_ref, descan_out_ref,
     object_ref, gradient_ref, wave_ref, far_ref,
 ):
     tile_rows, tile_cols, width, modes, count, n_fast, n_slow = sizes
     fast, slow = where_ref[0], where_ref[1]
     core = lax.rem(fast, 2)
     rim = width // 2
-    right, left = masked(where_ref, right_ref[...], left_ref[...], n_slow)
+    right, left = both_sides(lax.rem(slow, 2), *columns)
     object_ref[...] = extended_ref[...] - OBJECT_STEP * add_columns(
         gradient_in_ref[...], right, left, tile_cols, width
     )
-    object_ref[:, :width] -= OBJECT_STEP * above_ref[...]
-    object_ref[:, tile_rows:] -= OBJECT_STEP * below_ref[...]
+    below, above = both_sides(core, rows_even_ref, rows_odd_ref)
+    object_ref[:, :width] -= OBJECT_STEP * above
+    object_ref[:, tile_rows:] -= OBJECT_STEP * below
     probe = updated_probe(probe_ref, mine_ref, other_ref, core, total, width, modes)
     probe_out_ref[0] = probe[0].reshape(modes, width, width)
     probe_out_ref[1] = probe[1].reshape(modes, width, width)
@@ -310,13 +355,14 @@
     down_ref[...] = gradient_ref[:, rim + tile_rows :, :tile_cols]
     real, imag = gradient_ref[0, :, tile_cols:], gradient_ref[1, :, tile_cols:]
     low = lane_of(real.shape) < rim
-    strip_right_ref[...] = jnp.where(low, real, pltpu.roll(imag, rim, 1))
-    strip_left_ref[...] = jnp.where(low, pltpu.roll(real, rim, 1), imag)
-
-
-def edge_blocks(where_ref, right, left, n_slow, width):
-    rim = width // 2
-    right, left = masked(where_ref, right, left, n_slow)
+    to_right = jnp.where(low, real, pltpu.roll(imag, rim, 1))
+    to_left = jnp.where(low, pltpu.roll(real, rim, 1), imag)
+    put_strips(slow, to_right, to_left, strips)
+
+
+def edge_blocks(slow, columns, rows, width):
+    rim = width // 2
+    right, left = both_sides(lax.rem(slow, 2), *columns, rows)
     low = lane_of(right.shape) < rim
     zero = jnp.zeros(right.shape, F32)
     first = (jnp.where(low, left, zero), jnp.where(low, pltpu.roll(left, rim, 1), zero))
@@ -324,29 +370,33 @@
     return first, last
 
 
-def last_rows_kernel(sizes, where_ref, up_in_ref, down_in_ref, right_ref, left_ref, up_ref, down_ref):
-    tile_rows, tile_cols, width, modes, count, n_fast, n_slow = sizes
-    rim = width // 2
-    for in_ref, out_ref, at in ((up_in_ref, up_ref, 0), (down_in_ref, down_ref, rim + tile_rows)):
-        out_ref[...] = in_ref[...]
-        first, last = edge_blocks(where_ref, right_ref[at : at + rim], left_ref[at : at + rim], n_slow, width)
+def last_rows_kernel(sizes, where_ref, up_ref, down_ref, columns, token_ref, even_ref, odd_ref):
+    tile_rows, tile_cols, width, modes, count, n_fast, n_slow = sizes
+    rim = width // 2
+    edges = []
+    for in_ref, at in ((up_ref, 0), (down_ref, rim + tile_rows)):
+        first, last = edge_blocks(where_ref[1], columns, slice(at, at + rim), width)
+        rows = []
         for part in range(2):
-            out_ref[part, :, :width] += first[part]
-            out_ref[part, :, tile_cols - width :] += last[part]
-
-
-def object_kernel(sizes, where_ref, base_ref, right_ref, left_ref, above_ref, below_ref, out_ref):
+            blocks = [in_ref[part, :, k : k + width] for k in range(0, tile_cols, width)]
+            blocks[0] = blocks[0] + first[part]
+            blocks[-1] = blocks[-1] + last[part]
+            rows.append(jnp.concatenate(blocks, axis=1))
+        edges.append(jnp.stack(rows))
+    put_strips(where_ref[0], edges[1], edges[0], (even_ref, odd_ref))
+
+
+def object_kernel(sizes, where_ref, base_ref, columns, rows_even_ref, rows_odd_ref, out_ref):
     tile_rows, tile_cols, width, modes, count, n_fast, n_slow = sizes
     rim = width // 2
     out_ref[...] = base_ref[...]
-    first, last = edge_blocks(
-        where_ref, right_ref[rim : rim + tile_rows], left_ref[rim : rim + tile_rows], n_slow, width
-    )
+    first, last = edge_blocks(where_ref[1], columns, slice(rim, rim + tile_rows), width)
     for part in range(2):
         out_ref[part, :, :width] -= OBJECT_STEP * first[part]
         out_ref[part, :, tile_cols - width :] -= OBJECT_STEP * last[part]
-    out_ref[:, :rim] -= OBJECT_STEP * above_ref[...]
-    out_ref[:, tile_rows - rim :] -= OBJECT_STEP * below_ref[...]
+    below, above = both_sides(lax.rem(where_ref[0], 2), rows_even_ref, rows_odd_ref)
+    out_ref[:, :rim] -= OBJECT_STEP * above
+    out_ref[:, tile_rows - rim :] -= OBJECT_STEP * below
 
 
 def probe_kernel(sizes, total, where_ref, probe_ref, descan_ref, mine_ref, other_ref, probe_out_ref, descan_out_ref):
@@ -364,14 +414,17 @@
         descan_out_ref[k : k + 1, :] = row[:, :3]
 
 
-def call(kernel, outs, scratch, *operands, smem=0):
+def call(kernel, outs, scratch, *operands, smem=0, hbm=False, semaphores=(), aliases=None, work=0):
     return pl.pallas_call(
         kernel,
-        out_shape=[jax.ShapeDtypeStruct(shape, F32) for shape in outs],
-        in_specs=[SMEM] * smem + [VMEM] * (len(operands) - smem),
+        out_shape=[out if isinstance(out, jax.ShapeDtypeStruct) else jax.ShapeDtypeStruct(out, F32) for out in outs],
+        in_specs=[SMEM] * smem + [HBM if hbm else VMEM] * (len(operands) - smem),
         out_specs=[VMEM] * len(outs),
-        scratch_shapes=[pltpu.VMEM(shape, F32) for shape in scratch],
+        scratch_shapes=[pltpu.VMEM(shape, F32) for shape in scratch]
+        + [pltpu.SemaphoreType.DMA(shape) for shape in semaphores],
+        input_output_aliases=aliases or {},
         compiler_params=pltpu.CompilerParams(vmem_limit_bytes=LIMIT),
+        cost_estimate=pl.CostEstimate(flops=work, bytes_accessed=work // 100, transcendentals=0) if work else None,
     )(*operands)
 
 
@@ -386,103 +439,126 @@
     sizes = (tile_rows, tile_cols, width, modes, count, n_fast, n_slow)
     fast, slow = lax.axis_index("fast"), lax.axis_index("slow")
     where = jnp.stack([fast, slow]).astype(jnp.int32)
+    starts = scan_positions.transpose(0, 2, 1)
     tables = transform_tables(width)
     ext_rows, ext_cols = tile_rows + width, tile_cols + width
     half_rows = modes * width
-
-    def moved(value, step_fast, step_slow):
+    swaps = 1 if n_slow == 2 else 2
+
+    def partner(place, odd, length):
+        other = place ^ 1 if not odd else ((place + 1) ^ 1) - 1
+        return other if 0 <= other < length else None
+
+    def exchanged(value, fast_swap=None, slow_swap=None):
         pairs = []
         for f in range(n_fast):
             for s in range(n_slow):
-                to_fast, to_slow = f + step_fast, s + step_slow
-                if 0 <= to_fast < n_fast and 0 <= to_slow < n_slow:
+                to_fast = f if fast_swap is None else partner(f, fast_swap, n_fast)
+                to_slow = s if slow_swap is None else partner(s, slow_swap, n_slow)
+                if to_fast is not None and to_slow is not None:
                     pairs.append((f * n_slow + s, to_fast * n_slow + to_slow))
         return lax.ppermute(value, AXES, pairs)
 
-    def across(to_right, to_left, step_fast):
-        if n_slow == 2:
-            pairs = [
-                (f * 2 + s, (f + step_fast) * 2 + 1 - s)
-                for f in range(n_fast)
-                for s in range(2)
-                if 0 <= f + step_fast < n_fast
-            ]
-            got = lax.ppermute(jnp.where(slow == 0, to_right, to_left), AXES, pairs)
-            return got, got
-        return moved(to_left, step_fast, -1), moved(to_right, step_fast, 1)
-
     def swapped(value, axis, bit):
         return lax.ppermute(value, axis, [(i, i ^ bit) for i in range(lax.axis_size(axis))])
 
-    def summed(keep, send):
-        if n_fast & (n_fast - 1) or n_slow & (n_slow - 1) or n_fast < 2:
+    assert n_fast >= 4 and n_slow >= 2 and not n_fast % 2 and not n_slow % 2
+    regular = not (n_fast & (n_fast - 1) or n_slow & (n_slow - 1))
+    fast_bits = [1 << k for k in range(1, n_fast.bit_length() - 1)]
+    slow_bits = [1 << k for k in range(n_slow.bit_length() - 1)]
+
+    def sum_begun(keep, send):
+        mine = keep + swapped(send, "fast", 1)
+        if regular:
+            for bit in fast_bits[:-1]:
+                mine = mine + swapped(mine, "fast", bit)
+        return mine
+
+    def sum_ended(mine):
+        if regular:
+            mine = mine + swapped(mine, "fast", fast_bits[-1])
+            for bit in slow_bits:
+                mine = mine + swapped(mine, "slow", bit)
+        else:
             core = lax.rem(fast, 2)
-            real = lax.psum(jnp.where(core == 0, keep, send), AXES)
-            imag = lax.psum(jnp.where(core == 0, send, keep), AXES)
-            return jnp.where(core == 0, real, imag), jnp.where(core == 0, imag, real)[:half_rows]
-        mine = keep + swapped(send, "fast", 1)
-        bit = 1
-        while bit < n_slow:
-            mine = mine + swapped(mine, "slow", bit)
-            bit *= 2
-        bit = 2
-        while bit < n_fast:
-            mine = mine + swapped(mine, "fast", bit)
-            bit *= 2
+            every = lax.psum(jnp.where(jnp.arange(2)[:, None, None] == core, mine, 0.0), AXES) * 0.5
+            mine = lax.dynamic_index_in_dim(every, core, keepdims=False)
         return mine, swapped(mine[:half_rows], "fast", 1)
 
-    last = object_field[:, :, tile_cols - rim :]
-    initial = object_field[:, :, :rim]
-    to_right = jnp.concatenate([last[0], last[1]], axis=1)
-    to_left = jnp.concatenate([initial[0], initial[1]], axis=1)
-    top = moved(object_field[:, tile_rows - rim :], 1, 0)
-    bottom = moved(object_field[:, :rim], -1, 0)
-    right_mid, left_mid = across(to_right, to_left, 0)
-    right_top, left_top = across(to_right[tile_rows - rim :], to_left[tile_rows - rim :], 1)
-    right_bottom, left_bottom = across(to_right[:rim], to_left[:rim], -1)
-
-    def first(where_ref, starts, descan_ref, object_ref, probe_ref, measured_ref, tables_ref, top_ref, bottom_ref,
-              r0, r1, r2, l0, l1, l2, *rest):
-        first_kernel(sizes, where_ref, starts, descan_ref, object_ref, probe_ref, measured_ref, tables_ref,
-                     top_ref, bottom_ref, (r0, r1, r2), (l0, l1, l2), *rest)
+    def pairwise(refs):
+        return refs if swaps == 2 else (refs[0], None)
+
+    extended, rows_even, rows_odd, *packed = call(
+        functools.partial(pack_kernel, sizes),
+        [(2, ext_rows, ext_cols)] + [(2, rim, tile_cols)] * 2
+        + [(tile_rows, width), (rim, width), (rim, width)] * swaps, [],
+        where, object_field, smem=1, hbm=True, semaphores=[()], work=WORK,
+    )
+    halos = []
+    rows_odd = exchanged(rows_odd, 1)
+    for k in range(swaps):
+        corner_odd = exchanged(packed[3 * k + 2], 1, k)
+        middle = exchanged(packed[3 * k], None, k)
+        halos += [middle, exchanged(packed[3 * k + 1], 0, k), corner_odd]
+    rows_even = exchanged(rows_even, 0)
+    def first(info_ref, starts_ref, descan_ref, extended_ref, probe_ref, measured_ref, tables_ref, *rest):
+        halo_refs = [rest[2 + 3 * k : 5 + 3 * k] for k in range(swaps)]
+        extended_out_ref, gradient_ref, *rest_out = rest[2 + 3 * swaps :]
+        first_kernel(sizes, info_ref, starts_ref, descan_ref, extended_ref, probe_ref, measured_ref, tables_ref,
+                     *rest[:2], halo_refs, extended_out_ref, gradient_ref, rest_out[:swaps], *rest_out[swaps:])
 
     scratch = [(count * modes * width, 2 * width), (2 * width, count * modes * width)]
     sums = [(half_rows + EXTRA, width)] * 2
-    extended, gradient, strip_right, strip_left, keep, send = call(
+    extended, gradient, *strips, keep, send = call(
         first,
-        [(2, ext_rows, ext_cols)] * 2 + [(2, ext_rows, width)] * 2 + sums,
+        [(2, ext_rows, ext_cols)] * 2 + [(2, ext_rows, width)] * swaps + sums,
         scratch,
-        where, scan_positions, descan, object_field, probe_modes, amplitudes, tables, top, bottom,
-        right_top, right_mid, right_bottom, left_top, left_mid, left_bottom,
-        smem=3,
-    )
-    from_right, from_left = across(strip_right, strip_left, 0)
-    up, down = call(
-        functools.partial(rows_kernel, sizes), [(2, width, ext_cols)] * 2, [],
-        where, gradient, from_right, from_left, smem=1,
-    )
-    above, below = moved(down, 1, 0), moved(up, -1, 0)
-    mine, other = summed(keep, send)
-    base, up, down, strip_right, strip_left, keep, send, probes, descan_rows = call(
-        functools.partial(second_kernel, sizes, total),
-        [(2, tile_rows, tile_cols)] + [(2, rim, tile_cols)] * 2 + [(ext_rows, width)] * 2 + sums
+        where, starts, descan, extended, probe_modes, amplitudes, tables, rows_even, rows_odd, *halos,
+        smem=3, aliases={3: 0},
+    )
+    columns = [exchanged(strip, None, k) for k, strip in enumerate(strips)]
+    mine = sum_begun(keep, send)
+
+    def rows(where_ref, gradient_ref, *rest):
+        rows_kernel(sizes, where_ref, gradient_ref, pairwise(rest[:swaps]), *rest[swaps:])
+
+    rows_even, rows_odd = call(rows, [(2, width, ext_cols)] * 2, [], where, gradient, *columns, mine, smem=1)
+    rows_odd = exchanged(rows_odd, 1)
+    rows_even = exchanged(rows_even, 0)
+    mine, other = sum_ended(mine)
+
+    def second(where_ref, starts_ref, descan_ref, extended_ref, gradient_ref, probe_ref, measured_ref, tables_ref, *rest):
+        base_ref, up_ref, down_ref, *rest_out = rest[swaps + 4 :]
+        second_kernel(sizes, total, where_ref, starts_ref, descan_ref, extended_ref, gradient_ref, probe_ref,
+                      measured_ref, tables_ref, pairwise(rest[:swaps]), *rest[swaps : swaps + 4],
+                      base_ref, up_ref, down_ref, rest_out[:swaps], *rest_out[swaps:])
+
+    base, up, down, *strips, keep, send, probes, descan_rows = call(
+        second,
+        [(2, tile_rows, tile_cols)] + [(2, rim, tile_cols)] * 2 + [(ext_rows, width)] * swaps + sums
         + [probe_modes.shape, (EXTRA, width)],
         [(2, ext_rows, ext_cols)] * 2 + scratch,
-        where, scan_positions, descan, extended, gradient, probe_modes, amplitudes, tables,
-        from_right, from_left, above, below, mine, other,
+        where, starts, descan, extended, gradient, probe_modes, amplitudes, tables,
+        *columns, rows_even, rows_odd, mine, other,
         smem=3,
     )
-    from_right, from_left = across(strip_right, strip_left, 0)
-    up, down = call(
-        functools.partial(last_rows_kernel, sizes), [(2, rim, tile_cols)] * 2, [],
-        where, up, down, from_right, from_left, smem=1,
-    )
-    above, below = moved(down, 1, 0), moved(up, -1, 0)
+    columns = [exchanged(strip, None, k) for k, strip in enumerate(strips)]
+    mine = sum_begun(keep, send)
+
+    def last_rows(where_ref, up_ref, down_ref, *rest):
+        last_rows_kernel(sizes, where_ref, up_ref, down_ref, pairwise(rest[:swaps]), *rest[swaps:])
+
+    rows_even, rows_odd = call(last_rows, [(2, rim, tile_cols)] * 2, [], where, up, down, *columns, mine, smem=1)
+    rows_odd = exchanged(rows_odd, 1)
+    rows_even = exchanged(rows_even, 0)
+    mine, other = sum_ended(mine)
+
+    def objects_of(where_ref, base_ref, *rest):
+        object_kernel(sizes, where_ref, base_ref, pairwise(rest[:swaps]), *rest[swaps:])
+
     (objects,) = call(
-        functools.partial(object_kernel, sizes), [(2, tile_rows, tile_cols)], [],
-        where, base, from_right, from_left, above, below, smem=1,
-    )
-    mine, other = summed(keep, send)
+        objects_of, [(2, tile_rows, tile_cols)], [], where, base, *columns, rows_even, rows_odd, smem=1,
+    )
     probes, descan_out = call(
         functools.partial(probe_kernel, sizes, total), [probe_modes.shape, descan.shape], [],
         where, probes, descan_rows, mine, other, smem=1,

time: 103 us -> 84.8 us (0.82)
  the two profiles are of different devices: /device:TPU:7 before, /device:TPU:1 now
where the time goes in v1:
time: 84.8 us; the launch traced here: 84.6 us
  starting transfers between devices  39 us (46%)
  waiting for transfers between devices  31.3 us (37%)
  Pallas kernels  12 us (14%)
  local copies, waits for them, and re-layouts  1.08 us (1%)
  between operations  0.86 us (1%)
    ppermute x12, waiting for transfers between devices, swapped(): lax.ppermute(value, axis, [(i, i ^ bit) for i in range(lax.axis_size(axis...  24.8 us
    ppermute x11, starting transfers between devices, exchanged(): return lax.ppermute(value, AXES, pairs)  20.8 us
    ppermute x12, starting transfers between devices, swapped(): lax.ppermute(value, axis, [(i, i ^ bit) for i in range(lax.axis_size(axis...  18.3 us
    pallas_call x7, Pallas kernels, call(): pl.pallas_call(kernel, out_shape=[out if isinstance(out, jax.ShapeDtypeSt...  12 us
    ppermute x11, waiting for transfers between devices, exchanged(): return lax.ppermute(value, AXES, pairs)  6.48 us
  transfers between devices with their start and end apart: 23, of which 11 were waited for; matrix products, arithmetic and copies ran while one was open for 0% of the time, Pallas kernels for 3%

profile of v1, /device:TPU:1, one launch (start us, length us, event | category | flops | bytes accessed | tf_op | source)
XLA Modules:
  0.0 84.6 jit_solution(11812668351333495093)
XLA Ops:
  2.6 4.5 %collective-permute-start.1 = (f32[2,64,256]{2,1,0:T(8,128)S(1)}, f32[2,64,256]{2,1,0:T(8,128)S(1)}, u32[]{:S(2)}, u32[]{:S(2)}) collective-permute-start(f32[2,64,256]{2,1,0:T(8,128)S(1)} %get-tuple-element.30), channel_id=1, source_target_pairs={{2,4},{3,5},{4,2},{5,3},{6,8},{7,9},{8,6},{9,7},{10,12},{11,13},{1... | collective-permute-start | bytes 393224 | tf_op jit(solution)/shard_map/ppermute | solution.py:460
  8.4 4.6 %collective-permute-start.4 = (f32[64,128]{1,0:T(8,128)S(1)}, f32[64,128]{1,0:T(8,128)S(1)}, u32[]{:S(2)}, u32[]{:S(2)}) collective-permute-start(f32[64,128]{1,0:T(8,128)S(1)} %get-tuple-element.33), channel_id=1, source_target_pairs={{2,5},{3,4},{4,3},{5,2},{6,9},{7,8},{8,7},{9,6},{10,13},{11,12},{1... | collective-permute-start | bytes 98312 | tf_op jit(solution)/shard_map/ppermute | solution.py:460
  13.0 1.6 %collective-permute-done.4.rest_4_ = f32[64,128]{1,0:T(8,128)S(1)} collective-permute-done((f32[64,128]{1,0:T(8,128)S(1)}, f32[64,128]{1,0:T(8,128)S(1)}, u32[]{:S(2)}, u32[]{:S(2)}) %collective-permute-start.4) | collective-permute-done | bytes 32800 | tf_op jit(solution)/shard_map/ppermute | solution.py:460
  14.7 3.2 %shard_map.86 = (f32[2,384,384]{2,1,0:T(8,128)S(1)}, f32[2,384,384]{2,1,0:T(8,128)S(1)}, f32[2,384,128]{2,1,0:T(8,128)S(1)}, f32[264,128]{1,0:T(8,128)S(1)}, f32[264,128]{1,0:T(8,128)S(1)}) custom-call(s32[2]{0:T(128)S(1)} %pad_add_fusion.where_ref.info_ref, s32[2,1,2]{2,1,0:T(1,128)S(1)} %bitcast.5, ...), custom_call_target="tpu_custom_call", output_to_operand_aliasing={{0}: (3, {})} | custom-call | tf_op jit(solution)/shard_map/pallas_call | solution.py:418
  19.3 2.1 %collective-permute-start.7 = (f32[264,128]{1,0:T(8,128)S(1)}, f32[264,128]{1,0:T(8,128)S(1)}, u32[]{:S(2)}, u32[]{:S(2)}) collective-permute-start(f32[264,128]{1,0:T(8,128)S(1)} %add.30), channel_id=1, source_target_pairs={{0,4},{2,6},{4,0},{6,2},{8,12},{10,14},{12,8},{14,10},{16,20},{18,... | collective-permute-start | bytes 405512 | tf_op jit(solution)/shard_map/ppermute | solution.py:463
  21.5 3.5 %collective-permute-done.7 = f32[264,128]{1,0:T(8,128)S(1)} collective-permute-done((f32[264,128]{1,0:T(8,128)S(1)}, f32[264,128]{1,0:T(8,128)S(1)}, u32[]{:S(2)}, u32[]{:S(2)}) %collective-permute-start.7) | collective-permute-done | bytes 135200 | tf_op jit(solution)/shard_map/ppermute | solution.py:463
  24.9 2.1 %collective-permute-start.8 = (f32[264,128]{1,0:T(8,128)S(1)}, f32[264,128]{1,0:T(8,128)S(1)}, u32[]{:S(2)}, u32[]{:S(2)}) collective-permute-start(f32[264,128]{1,0:T(8,128)S(1)} %add.31), channel_id=1, source_target_pairs={{0,8},{2,10},{4,12},{6,14},{8,0},{10,2},{12,4},{14,6},{16,24},{18,... | collective-permute-start | bytes 405512 | tf_op jit(solution)/shard_map/ppermute | solution.py:463
  27.1 2.7 %collective-permute-done.8 = f32[264,128]{1,0:T(8,128)S(1)} collective-permute-done((f32[264,128]{1,0:T(8,128)S(1)}, f32[264,128]{1,0:T(8,128)S(1)}, u32[]{:S(2)}, u32[]{:S(2)}) %collective-permute-start.8) | collective-permute-done | bytes 135200 | tf_op jit(solution)/shard_map/ppermute | solution.py:463
  29.8 2.5 %collective-permute-start.11 = (f32[264,128]{1,0:T(8,128)S(1)}, f32[264,128]{1,0:T(8,128)S(1)}, u32[]{:S(2)}, u32[]{:S(2)}) collective-permute-start(f32[264,128]{1,0:T(8,128)S(1)} %add.32.rest_1_), channel_id=1, source_target_pairs={{0,16},{2,18},{4,20},{6,22},{8,24},{10,26},{12,28},{14,30},{16,0},... | collective-permute-start | bytes 405512 | tf_op jit(solution)/shard_map/ppermute | solution.py:463
  33.0 2.4 %collective-permute-start.9 = (f32[2,128,384]{2,1,0:T(8,128)S(1)}, f32[2,128,384]{2,1,0:T(8,128)S(1)}, u32[]{:S(2)}, u32[]{:S(2)}) collective-permute-start(f32[2,128,384]{2,1,0:T(8,128)S(1)} %get-tuple-element.39), channel_id=1, source_target_pairs={{0,2},{1,3},{2,0},{3,1},{4,6},{5,7},{6,4},{7,5},{8,10},{9,11},{10,... | collective-permute-start | bytes 1179656 | tf_op jit(solution)/shard_map/ppermute | solution.py:460
  35.4 2.4 %collective-permute-start.10 = (f32[2,128,384]{2,1,0:T(8,128)S(1)}, f32[2,128,384]{2,1,0:T(8,128)S(1)}, u32[]{:S(2)}, u32[]{:S(2)}) collective-permute-start(f32[2,128,384]{2,1,0:T(8,128)S(1)} %get-tuple-element.40), channel_id=1, source_target_pairs={{2,4},{3,5},{4,2},{5,3},{6,8},{7,9},{8,6},{9,7},{10,12},{11,13},{1... | collective-permute-start | bytes 1179656 | tf_op jit(solution)/shard_map/ppermute | solution.py:460
  39.0 2.7 %collective-permute-done.12 = f32[264,128]{1,0:T(8,128)S(1)} collective-permute-done((f32[264,128]{1,0:T(8,128)S(1)}, f32[264,128]{1,0:T(8,128)S(1)}, u32[]{:S(2)}, u32[]{:S(2)}) %collective-permute-start.12) | collective-permute-done | bytes 135200 | tf_op jit(solution)/shard_map/ppermute | solution.py:463
  41.8 3.2 %collective-permute-start.13 = (f32[256,128]{1,0:T(8,128)S(1)}, f32[256,128]{1,0:T(8,128)S(1)}, u32[]{:S(2)}, u32[]{:S(2)}) collective-permute-start(f32[256,128]{1,0:T(8,128)S(1)} %slice.8), channel_id=1, source_target_pairs={{0,2},{2,0},{4,6},{6,4},{8,10},{10,8},{12,14},{14,12},{16,18},{18,... | collective-permute-start | bytes 393224 | tf_op jit(solution)/shard_map/ppermute | solution.py:463
  45.0 1.8 %collective-permute-done.10.rest_2_ = f32[2,128,384]{2,1,0:T(8,128)S(1)} collective-permute-done((f32[2,128,384]{2,1,0:T(8,128)S(1)}, f32[2,128,384]{2,1,0:T(8,128)S(1)}, u32[]{:S(2)}, u32[]{:S(2)}) %collective-permute-start.10) | collective-permute-done | bytes 393248 | tf_op jit(solution)/shard_map/ppermute | solution.py:460
  46.7 3.8 %shard_map.88 = (f32[2,256,256]{2,1,0:T(8,128)S(1)}, f32[2,64,256]{2,1,0:T(8,128)S(1)}, f32[2,64,256]{2,1,0:T(8,128)S(1)}, f32[384,128]{1,0:T(8,128)S(1)}, f32[2...) custom-call(s32[2]{0:T(128)S(1)} %pad_add_fusion.where_ref.info_ref, ...), custom_call_target="tpu_custom_call" | custom-call | tf_op jit(solution)/shard_map/pallas_call | solution.py:418
  52.0 2.3 %collective-permute-start.16 = (f32[264,128]{1,0:T(8,128)S(1)}, f32[264,128]{1,0:T(8,128)S(1)}, u32[]{:S(2)}, u32[]{:S(2)}) collective-permute-start(f32[264,128]{1,0:T(8,128)S(1)} %add.35), channel_id=1, source_target_pairs={{0,4},{2,6},{4,0},{6,2},{8,12},{10,14},{12,8},{14,10},{16,20},{18,... | collective-permute-start | bytes 405512 | tf_op jit(solution)/shard_map/ppermute | solution.py:463
  54.3 3.7 %collective-permute-done.16 = f32[264,128]{1,0:T(8,128)S(1)} collective-permute-done((f32[264,128]{1,0:T(8,128)S(1)}, f32[264,128]{1,0:T(8,128)S(1)}, u32[]{:S(2)}, u32[]{:S(2)}) %collective-permute-start.16) | collective-permute-done | bytes 135200 | tf_op jit(solution)/shard_map/ppermute | solution.py:463
  58.0 2.4 %collective-permute-start.17 = (f32[264,128]{1,0:T(8,128)S(1)}, f32[264,128]{1,0:T(8,128)S(1)}, u32[]{:S(2)}, u32[]{:S(2)}) collective-permute-start(f32[264,128]{1,0:T(8,128)S(1)} %add.36), channel_id=1, source_target_pairs={{0,8},{2,10},{4,12},{6,14},{8,0},{10,2},{12,4},{14,6},{16,24},{18,... | collective-permute-start | bytes 405512 | tf_op jit(solution)/shard_map/ppermute | solution.py:463
  60.4 3.0 %collective-permute-done.17 = f32[264,128]{1,0:T(8,128)S(1)} collective-permute-done((f32[264,128]{1,0:T(8,128)S(1)}, f32[264,128]{1,0:T(8,128)S(1)}, u32[]{:S(2)}, u32[]{:S(2)}) %collective-permute-start.17) | collective-permute-done | bytes 135200 | tf_op jit(solution)/shard_map/ppermute | solution.py:463
  64.6 7.6 %collective-permute-done.20 = f32[264,128]{1,0:T(8,128)S(1)} collective-permute-done((f32[264,128]{1,0:T(8,128)S(1)}, f32[264,128]{1,0:T(8,128)S(1)}, u32[]{:S(2)}, u32[]{:S(2)}) %collective-permute-start.20) | collective-permute-done | bytes 135200 | tf_op jit(solution)/shard_map/ppermute | solution.py:463
  73.9 1.5 %collective-permute-start.18 = (f32[2,64,256]{2,1,0:T(8,128)S(1)}, f32[2,64,256]{2,1,0:T(8,128)S(1)}, u32[]{:S(2)}, u32[]{:S(2)}) collective-permute-start(f32[2,64,256]{2,1,0:T(8,128)S(1)} %get-tuple-element.47), channel_id=1, source_target_pairs={{0,2},{1,3},{2,0},{3,1},{4,6},{5,7},{6,4},{7,5},{8,10},{9,11},{10,... | collective-permute-start | bytes 393224 | tf_op jit(solution)/shard_map/ppermute | solution.py:460
  75.4 1.9 %collective-permute-start.19 = (f32[2,64,256]{2,1,0:T(8,128)S(1)}, f32[2,64,256]{2,1,0:T(8,128)S(1)}, u32[]{:S(2)}, u32[]{:S(2)}) collective-permute-start(f32[2,64,256]{2,1,0:T(8,128)S(1)} %get-tuple-element.48), channel_id=1, source_target_pairs={{2,4},{3,5},{4,2},{5,3},{6,8},{7,9},{8,6},{9,7},{10,12},{11,13},{1... | collective-permute-start | bytes 393224 | tf_op jit(solution)/shard_map/ppermute | solution.py:460
  78.5 3.1 %collective-permute-done.19.rest_2_ = f32[2,64,256]{2,1,0:T(8,128)S(1)} collective-permute-done((f32[2,64,256]{2,1,0:T(8,128)S(1)}, f32[2,64,256]{2,1,0:T(8,128)S(1)}, u32[]{:S(2)}, u32[]{:S(2)}) %collective-permute-start.19) | collective-permute-done | bytes 131104 | tf_op jit(solution)/shard_map/ppermute | solution.py:460
  81.6 1.5 %shard_map.90 = f32[2,256,256]{2,1,0:T(8,128)} custom-call(s32[2]{0:T(128)S(1)} %pad_add_fusion.where_ref.info_ref, f32[2,256,256]{2,1,0:T(8,128)S(1)} %get-tuple-element.41.base_ref, f32[384,128]{1,0:T(8,128)S(1)} %collective-permute-done.14.rest_0_, f32[2,64,256]{2,1,0:T(8,128)S(1)} %collective-permute-done.18.rest_1_, ...), custom_call_target="tpu_custom_call" | custom-call | tf_op jit(solution)/shard_map/pallas_call | solution.py:418
  (54 shorter events, 13.6 us)
Async XLA Ops:
  1.8 12.9 %copy-start.4 = (f32[2,3]{1,0:T(2,128)S(1)}, f32[2,3]{1,0:T(2,128)}, u32[]{:S(2)}) copy-start(f32[2,3]{1,0:T(2,128)} %descan_ref.3) | copy-start | bytes 76
  2.5 12.1 %collective-permute-start = (f32[2,64,256]{2,1,0:T(8,128)S(1)}, f32[2,64,256]{2,1,0:T(8,128)S(1)}, u32[]{:S(2)}, u32[]{:S(2)}) collective-permute-start(f32[2,64,256]{2,1,0:T(8,128)S(1)} %get-tuple-element.29), channel_id=1, source_target_pairs={{0,2},{1,3},{2,0},{3,1},{4,6},{5,7},{6,4},{7,5},{8,10},{9,11},{10,... | collective-permute-start | bytes 393224 | tf_op jit(solution)/shard_map/ppermute | solution.py:460
  2.6 12.0 %collective-permute-start.1 = (f32[2,64,256]{2,1,0:T(8,128)S(1)}, f32[2,64,256]{2,1,0:T(8,128)S(1)}, u32[]{:S(2)}, u32[]{:S(2)}) collective-permute-start(f32[2,64,256]{2,1,0:T(8,128)S(1)} %get-tuple-element.30), channel_id=1, source_target_pairs={{2,4},{3,5},{4,2},{5,3},{6,8},{7,9},{8,6},{9,7},{10,12},{11,13},{1... | collective-permute-start | bytes 393224 | tf_op jit(solution)/shard_map/ppermute | solution.py:460
  7.1 7.5 %collective-permute-start.2 = (f32[256,128]{1,0:T(8,128)S(1)}, f32[256,128]{1,0:T(8,128)S(1)}, u32[]{:S(2)}, u32[]{:S(2)}) collective-permute-start(f32[256,128]{1,0:T(8,128)S(1)} %get-tuple-element.31), channel_id=1, source_target_pairs={{0,1},{1,0},{2,3},{3,2},{4,5},{5,4},{6,7},{7,6},{8,9},{9,8},{10,11... | collective-permute-start | bytes 393224 | tf_op jit(solution)/shard_map/ppermute | solution.py:460
  8.4 4.6 %collective-permute-start.3 = (f32[64,128]{1,0:T(8,128)S(1)}, f32[64,128]{1,0:T(8,128)S(1)}, u32[]{:S(2)}, u32[]{:S(2)}) collective-permute-start(f32[64,128]{1,0:T(8,128)S(1)} %get-tuple-element.32), channel_id=1, source_target_pairs={{0,3},{1,2},{2,1},{3,0},{4,7},{5,6},{6,5},{7,4},{8,11},{9,10},{10,... | collective-permute-start | bytes 98312 | tf_op jit(solution)/shard_map/ppermute | solution.py:460
  8.4 6.2 %collective-permute-start.4 = (f32[64,128]{1,0:T(8,128)S(1)}, f32[64,128]{1,0:T(8,128)S(1)}, u32[]{:S(2)}, u32[]{:S(2)}) collective-permute-start(f32[64,128]{1,0:T(8,128)S(1)} %get-tuple-element.33), channel_id=1, source_target_pairs={{2,5},{3,4},{4,3},{5,2},{6,9},{7,8},{8,7},{9,6},{10,13},{11,12},{1... | collective-permute-start | bytes 98312 | tf_op jit(solution)/shard_map/ppermute | solution.py:460
  17.9 1.4 %collective-permute-start.6 = (f32[264,128]{1,0:T(8,128)S(1)}, f32[264,128]{1,0:T(8,128)S(1)}, u32[]{:S(2)}, u32[]{:S(2)}) collective-permute-start(f32[264,128]{1,0:T(8,128)S(1)} %get-tuple-element.38), channel_id=1, source_target_pairs={{0,2},{2,0},{4,6},{6,4},{8,10},{10,8},{12,14},{14,12},{16,18},{18,... | collective-permute-start | bytes 405512 | tf_op jit(solution)/shard_map/ppermute | solution.py:463
  18.0 14.3 %collective-permute-start.5 = (f32[2,384,128]{2,1,0:T(8,128)S(1)}, f32[2,384,128]{2,1,0:T(8,128)S(1)}, u32[]{:S(2)}, u32[]{:S(2)}) collective-permute-start(f32[2,384,128]{2,1,0:T(8,128)S(1)} %get-tuple-element.36), channel_id=1, source_target_pairs={{0,1},{1,0},{2,3},{3,2},{4,5},{5,4},{6,7},{7,6},{8,9},{9,8},{10,11... | collective-permute-start | bytes 1179656 | tf_op jit(solution)/shard_map/ppermute | solution.py:460
  19.3 5.6 %collective-permute-start.7 = (f32[264,128]{1,0:T(8,128)S(1)}, f32[264,128]{1,0:T(8,128)S(1)}, u32[]{:S(2)}, u32[]{:S(2)}) collective-permute-start(f32[264,128]{1,0:T(8,128)S(1)} %add.30), channel_id=1, source_target_pairs={{0,4},{2,6},{4,0},{6,2},{8,12},{10,14},{12,8},{14,10},{16,20},{18,... | collective-permute-start | bytes 405512 | tf_op jit(solution)/shard_map/ppermute | solution.py:463
  24.9 4.9 %collective-permute-start.8 = (f32[264,128]{1,0:T(8,128)S(1)}, f32[264,128]{1,0:T(8,128)S(1)}, u32[]{:S(2)}, u32[]{:S(2)}) collective-permute-start(f32[264,128]{1,0:T(8,128)S(1)} %add.31), channel_id=1, source_target_pairs={{0,8},{2,10},{4,12},{6,14},{8,0},{10,2},{12,4},{14,6},{16,24},{18,... | collective-permute-start | bytes 405512 | tf_op jit(solution)/shard_map/ppermute | solution.py:463
  29.8 8.0 %collective-permute-start.11 = (f32[264,128]{1,0:T(8,128)S(1)}, f32[264,128]{1,0:T(8,128)S(1)}, u32[]{:S(2)}, u32[]{:S(2)}) collective-permute-start(f32[264,128]{1,0:T(8,128)S(1)} %add.32.rest_1_), channel_id=1, source_target_pairs={{0,16},{2,18},{4,20},{6,22},{8,24},{10,26},{12,28},{14,30},{16,0},... | collective-permute-start | bytes 405512 | tf_op jit(solution)/shard_map/ppermute | solution.py:463
  33.0 12.0 %collective-permute-start.9 = (f32[2,128,384]{2,1,0:T(8,128)S(1)}, f32[2,128,384]{2,1,0:T(8,128)S(1)}, u32[]{:S(2)}, u32[]{:S(2)}) collective-permute-start(f32[2,128,384]{2,1,0:T(8,128)S(1)} %get-tuple-element.39), channel_id=1, source_target_pairs={{0,2},{1,3},{2,0},{3,1},{4,6},{5,7},{6,4},{7,5},{8,10},{9,11},{10,... | collective-permute-start | bytes 1179656 | tf_op jit(solution)/shard_map/ppermute | solution.py:460
  35.4 11.3 %collective-permute-start.10 = (f32[2,128,384]{2,1,0:T(8,128)S(1)}, f32[2,128,384]{2,1,0:T(8,128)S(1)}, u32[]{:S(2)}, u32[]{:S(2)}) collective-permute-start(f32[2,128,384]{2,1,0:T(8,128)S(1)} %get-tuple-element.40), channel_id=1, source_target_pairs={{2,4},{3,5},{4,2},{5,3},{6,8},{7,9},{8,6},{9,7},{10,12},{11,13},{1... | collective-permute-start | bytes 1179656 | tf_op jit(solution)/shard_map/ppermute | solution.py:460
  37.8 3.9 %collective-permute-start.12 = (f32[264,128]{1,0:T(8,128)S(1)}, f32[264,128]{1,0:T(8,128)S(1)}, u32[]{:S(2)}, u32[]{:S(2)}) collective-permute-start(f32[264,128]{1,0:T(8,128)S(1)} %add.33), channel_id=1, source_target_pairs={{0,1},{1,0},{2,3},{3,2},{4,5},{5,4},{6,7},{7,6},{8,9},{9,8},{10,11... | collective-permute-start | bytes 405512 | tf_op jit(solution)/shard_map/ppermute | solution.py:463
  41.8 4.9 %collective-permute-start.13 = (f32[256,128]{1,0:T(8,128)S(1)}, f32[256,128]{1,0:T(8,128)S(1)}, u32[]{:S(2)}, u32[]{:S(2)}) collective-permute-start(f32[256,128]{1,0:T(8,128)S(1)} %slice.8), channel_id=1, source_target_pairs={{0,2},{2,0},{4,6},{6,4},{8,10},{10,8},{12,14},{14,12},{16,18},{18,... | collective-permute-start | bytes 393224 | tf_op jit(solution)/shard_map/ppermute | solution.py:463
  50.6 1.4 %collective-permute-start.15 = (f32[264,128]{1,0:T(8,128)S(1)}, f32[264,128]{1,0:T(8,128)S(1)}, u32[]{:S(2)}, u32[]{:S(2)}) collective-permute-start(f32[264,128]{1,0:T(8,128)S(1)} %get-tuple-element.46), channel_id=1, source_target_pairs={{0,2},{2,0},{4,6},{6,4},{8,10},{10,8},{12,14},{14,12},{16,18},{18,... | collective-permute-start | bytes 405512 | tf_op jit(solution)/shard_map/ppermute | solution.py:463
  52.0 6.0 %collective-permute-start.16 = (f32[264,128]{1,0:T(8,128)S(1)}, f32[264,128]{1,0:T(8,128)S(1)}, u32[]{:S(2)}, u32[]{:S(2)}) collective-permute-start(f32[264,128]{1,0:T(8,128)S(1)} %add.35), channel_id=1, source_target_pairs={{0,4},{2,6},{4,0},{6,2},{8,12},{10,14},{12,8},{14,10},{16,20},{18,... | collective-permute-start | bytes 405512 | tf_op jit(solution)/shard_map/ppermute | solution.py:463
  58.0 5.4 %collective-permute-start.17 = (f32[264,128]{1,0:T(8,128)S(1)}, f32[264,128]{1,0:T(8,128)S(1)}, u32[]{:S(2)}, u32[]{:S(2)}) collective-permute-start(f32[264,128]{1,0:T(8,128)S(1)} %add.36), channel_id=1, source_target_pairs={{0,8},{2,10},{4,12},{6,14},{8,0},{10,2},{12,4},{14,6},{16,24},{18,... | collective-permute-start | bytes 405512 | tf_op jit(solution)/shard_map/ppermute | solution.py:463
  63.4 8.7 %collective-permute-start.20 = (f32[264,128]{1,0:T(8,128)S(1)}, f32[264,128]{1,0:T(8,128)S(1)}, u32[]{:S(2)}, u32[]{:S(2)}) collective-permute-start(f32[264,128]{1,0:T(8,128)S(1)} %add.37.rest_1_), channel_id=1, source_target_pairs={{0,16},{2,18},{4,20},{6,22},{8,24},{10,26},{12,28},{14,30},{16,0},... | collective-permute-start | bytes 405512 | tf_op jit(solution)/shard_map/ppermute | solution.py:463
  63.5 9.7 %collective-permute-start.14 = (f32[384,128]{1,0:T(8,128)S(1)}, f32[384,128]{1,0:T(8,128)S(1)}, u32[]{:S(2)}, u32[]{:S(2)}) collective-permute-start(f32[384,128]{1,0:T(8,128)S(1)} %get-tuple-element.42), channel_id=1, source_target_pairs={{0,1},{1,0},{2,3},{3,2},{4,5},{5,4},{6,7},{7,6},{8,9},{9,8},{10,11... | collective-permute-start | bytes 589832 | tf_op jit(solution)/shard_map/ppermute | solution.py:460
  72.2 5.1 %collective-permute-start.21 = (f32[264,128]{1,0:T(8,128)S(1)}, f32[264,128]{1,0:T(8,128)S(1)}, u32[]{:S(2)}, u32[]{:S(2)}) collective-permute-start(f32[264,128]{1,0:T(8,128)S(1)} %add.38), channel_id=1, source_target_pairs={{0,1},{1,0},{2,3},{3,2},{4,5},{5,4},{6,7},{7,6},{8,9},{9,8},{10,11... | collective-permute-start | bytes 405512 | tf_op jit(solution)/shard_map/ppermute | solution.py:463
  73.9 4.6 %collective-permute-start.18 = (f32[2,64,256]{2,1,0:T(8,128)S(1)}, f32[2,64,256]{2,1,0:T(8,128)S(1)}, u32[]{:S(2)}, u32[]{:S(2)}) collective-permute-start(f32[2,64,256]{2,1,0:T(8,128)S(1)} %get-tuple-element.47), channel_id=1, source_target_pairs={{0,2},{1,3},{2,0},{3,1},{4,6},{5,7},{6,4},{7,5},{8,10},{9,11},{10,... | collective-permute-start | bytes 393224 | tf_op jit(solution)/shard_map/ppermute | solution.py:460
  75.4 6.3 %collective-permute-start.19 = (f32[2,64,256]{2,1,0:T(8,128)S(1)}, f32[2,64,256]{2,1,0:T(8,128)S(1)}, u32[]{:S(2)}, u32[]{:S(2)}) collective-permute-start(f32[2,64,256]{2,1,0:T(8,128)S(1)} %get-tuple-element.48), channel_id=1, source_target_pairs={{2,4},{3,5},{4,2},{5,3},{6,8},{7,9},{8,6},{9,7},{10,12},{11,13},{1... | collective-permute-start | bytes 393224 | tf_op jit(solution)/shard_map/ppermute | solution.py:460
  77.3 5.8 %collective-permute-start.22 = (f32[256,128]{1,0:T(8,128)S(1)}, f32[256,128]{1,0:T(8,128)S(1)}, u32[]{:S(2)}, u32[]{:S(2)}) collective-permute-start(f32[256,128]{1,0:T(8,128)S(1)} %slice.9), channel_id=1, source_target_pairs={{0,2},{2,0},{4,6},{6,4},{8,10},{10,8},{12,14},{14,12},{16,18},{18,... | collective-permute-start | bytes 393224 | tf_op jit(solution)/shard_map/ppermute | solution.py:463
  (5 other events, 52.5 us)

commit v2 on v1

--- a/solution.py
+++ b/solution.py
@@ -211,11 +211,45 @@
     send_ref[modes * width :] = block
 
 
-def updated_probe(probe_ref, mine_ref, other_ref, core, total, width, modes):
+def put_quarters(probe_grad, descan_grad, mine_ref, beside_ref, send_ref, core, slow, width, modes):
     rows = modes * width
-    mine, other = mine_ref[:rows], other_ref[...]
-    real = probe_ref[0].reshape(rows, width) - PROBE_STEP / total * jnp.where(core == 0, mine, other)
-    imag = probe_ref[1].reshape(rows, width) - PROBE_STEP / total * jnp.where(core == 0, other, mine)
+    real, imag = jnp.concatenate(probe_grad[0], axis=0), jnp.concatenate(probe_grad[1], axis=0)
+    keep, send = pick(core, real, imag), pick(core, imag, real)
+    half = rows // 2
+    block = jnp.concatenate(descan_grad + [jnp.zeros((EXTRA - 6, width), F32)], axis=0)
+    low, high = keep[:half], keep[half:]
+    mine_ref[:half] = pick(slow, low, high)
+    mine_ref[half:] = block
+    beside_ref[:half] = pick(slow, high, low)
+    beside_ref[half:] = block
+    low, high = send[:half], send[half:]
+    send_ref[0, :half] = pick(slow, low, high)
+    send_ref[0, half:] = block
+    send_ref[1, :half] = pick(slow, high, low)
+    send_ref[1, half:] = block
+
+
+def of_halves(halves, core, slow, rows):
+    mine, other = halves[0][:rows], halves[1][...]
+    return pick(core, mine, other), pick(core, other, mine)
+
+
+def of_quarters(quarters, core, slow, rows):
+    part = rows // 2
+    values = [quarters[0][:part], quarters[1][...], quarters[2][:part], quarters[2][part:]]
+    sums = []
+    for own, beside in (
+        (pick(core, values[0], values[2]), pick(core, values[1], values[3])),
+        (pick(core, values[2], values[0]), pick(core, values[3], values[1])),
+    ):
+        sums.append(jnp.concatenate([pick(slow, own, beside), pick(slow, beside, own)], axis=0))
+    return sums
+
+
+def updated_probe(probe_ref, sums, total, width, modes):
+    rows = modes * width
+    real = probe_ref[0].reshape(rows, width) - PROBE_STEP / total * sums[0]
+    imag = probe_ref[1].reshape(rows, width) - PROBE_STEP / total * sums[1]
     power = jnp.sum(jnp.sum(real * real + imag * imag, axis=0, keepdims=True), axis=1, keepdims=True)
     scale = jnp.sqrt(PROBE_POWER * rows * width / power)
     return real * scale, imag * scale
@@ -320,7 +354,7 @@
 def second_kernel(
     sizes, total, where_ref, starts, descan_ref, extended_ref, gradient_in_ref, probe_ref, measured_ref, tables_ref,
     columns, rows_even_ref, rows_odd_ref, mine_ref, other_ref,
-    base_ref, up_ref, down_ref, strips, keep_ref, send_ref, probe_out_ref, descan_out_ref,
+    base_ref, up_ref, down_ref, strips, own_ref, beside_ref, send_ref, probe_out_ref, descan_out_ref,
     object_ref, gradient_ref, wave_ref, far_ref,
 ):
     tile_rows, tile_cols, width, modes, count, n_fast, n_slow = sizes
@@ -334,7 +368,8 @@
     below, above = both_sides(core, rows_even_ref, rows_odd_ref)
     object_ref[:, :width] -= OBJECT_STEP * above
     object_ref[:, tile_rows:] -= OBJECT_STEP * below
-    probe = updated_probe(probe_ref, mine_ref, other_ref, core, total, width, modes)
+    sums = of_halves((mine_ref, other_ref), core, slow, modes * width)
+    probe = updated_probe(probe_ref, sums, total, width, modes)
     probe_out_ref[0] = probe[0].reshape(modes, width, width)
     probe_out_ref[1] = probe[1].reshape(modes, width, width)
     at = modes * width
@@ -346,7 +381,7 @@
         object_ref, probe, descan_rows, starts, measured_ref, tables_ref, gradient_ref, wave_ref, far_ref,
         sizes + (fast, slow),
     )
-    put_sums(probe_grad, descan_grad, keep_ref, send_ref, core, width, modes)
+    put_quarters(probe_grad, descan_grad, own_ref, beside_ref, send_ref, core, lax.rem(slow, 2), width, modes)
     base_ref[...] = (
         object_ref[:, rim : rim + tile_rows, :tile_cols]
         - OBJECT_STEP * gradient_ref[:, rim : rim + tile_rows, :tile_cols]
@@ -370,9 +405,10 @@
     return first, last
 
 
-def last_rows_kernel(sizes, where_ref, up_ref, down_ref, columns, token_ref, even_ref, odd_ref):
+def last_rows_kernel(sizes, where_ref, up_ref, down_ref, columns, mine_ref, arrived_ref, even_ref, odd_ref, sum_ref):
     tile_rows, tile_cols, width, modes, count, n_fast, n_slow = sizes
     rim = width // 2
+    sum_ref[...] = mine_ref[...] + arrived_ref[...]
     edges = []
     for in_ref, at in ((up_ref, 0), (down_ref, rim + tile_rows)):
         first, last = edge_blocks(where_ref[1], columns, slice(at, at + rim), width)
@@ -386,6 +422,12 @@
     put_strips(where_ref[0], edges[1], edges[0], (even_ref, odd_ref))
 
 
+def join_kernel(own_ref, beside_ref, *rest):
+    rows = own_ref.shape[0]
+    rest[-1][:rows] = own_ref[...]
+    rest[-1][rows:] = beside_ref[...]
+
+
 def object_kernel(sizes, where_ref, base_ref, columns, rows_even_ref, rows_odd_ref, out_ref):
     tile_rows, tile_cols, width, modes, count, n_fast, n_slow = sizes
     rim = width // 2
@@ -399,14 +441,15 @@
     out_ref[:, tile_rows - rim :] -= OBJECT_STEP * below
 
 
-def probe_kernel(sizes, total, where_ref, probe_ref, descan_ref, mine_ref, other_ref, probe_out_ref, descan_out_ref):
+def probe_kernel(sizes, total, where_ref, probe_ref, descan_ref, quarters, probe_out_ref, descan_out_ref):
     tile_rows, tile_cols, width, modes, count, n_fast, n_slow = sizes
-    core = lax.rem(where_ref[0], 2)
-    real, imag = updated_probe(probe_ref, mine_ref, other_ref, core, total, width, modes)
+    core, slow = lax.rem(where_ref[0], 2), lax.rem(where_ref[1], 2)
+    sums = of_quarters(quarters, core, slow, modes * width)
+    real, imag = updated_probe(probe_ref, sums, total, width, modes)
     probe_out_ref[0] = real.reshape(modes, width, width)
     probe_out_ref[1] = imag.reshape(modes, width, width)
-    at = modes * width
-    rows = descan_ref[...] - DESCAN_STEP / total * mine_ref[at : at + EXTRA]
+    at = modes * width // 2
+    rows = descan_ref[...] - DESCAN_STEP / total * quarters[0][at : at + EXTRA]
     lane = lane_of((1, width))
     for k in range(2):
         values = [rows[3 * k + n : 3 * k + n + 1] for n in range(3)]
@@ -533,9 +576,10 @@
                       measured_ref, tables_ref, pairwise(rest[:swaps]), *rest[swaps : swaps + 4],
                       base_ref, up_ref, down_ref, rest_out[:swaps], *rest_out[swaps:])
 
-    base, up, down, *strips, keep, send, probes, descan_rows = call(
+    part = (half_rows // 2 + EXTRA, width)
+    base, up, down, *strips, mine, beside, send, probes, descan_rows = call(
         second,
-        [(2, tile_rows, tile_cols)] + [(2, rim, tile_cols)] * 2 + [(ext_rows, width)] * swaps + sums
+        [(2, tile_rows, tile_cols)] + [(2, rim, tile_cols)] * 2 + [(ext_rows, width)] * swaps + [part, part, (2, *part)]
         + [probe_modes.shape, (EXTRA, width)],
         [(2, ext_rows, ext_cols)] * 2 + scratch,
         where, starts, descan, extended, gradient, probe_modes, amplitudes, tables,
@@ -543,15 +587,30 @@
         smem=3,
     )
     columns = [exchanged(strip, None, k) for k, strip in enumerate(strips)]
-    mine = sum_begun(keep, send)
+    core_part = swapped(send, "fast", 1)
+    mine = mine + core_part[0] + swapped(beside + core_part[1], "slow", 1)
+    steps = [("fast", bit) for bit in fast_bits] + [("slow", bit) for bit in slow_bits[1:]]
 
     def last_rows(where_ref, up_ref, down_ref, *rest):
         last_rows_kernel(sizes, where_ref, up_ref, down_ref, pairwise(rest[:swaps]), *rest[swaps:])
 
-    rows_even, rows_odd = call(last_rows, [(2, rim, tile_cols)] * 2, [], where, up, down, *columns, mine, smem=1)
+    arrived = swapped(mine, *steps[0]) if regular else jnp.zeros_like(mine)
+    rows_even, rows_odd, mine = call(
+        last_rows, [(2, rim, tile_cols)] * 2 + [part], [], where, up, down, *columns, mine, arrived, smem=1,
+    )
     rows_odd = exchanged(rows_odd, 1)
     rows_even = exchanged(rows_even, 0)
-    mine, other = sum_ended(mine)
+    if regular:
+        for step in steps[1:]:
+            mine = mine + swapped(mine, *step)
+    else:
+        place = 2 * lax.rem(fast, 2) + lax.rem(slow, 2)
+        every = lax.psum(jnp.where(jnp.arange(4)[:, None, None] == place, mine, 0.0), AXES)
+        mine = lax.dynamic_index_in_dim(every, place, keepdims=False)
+    own = mine[: half_rows // 2]
+    beside = swapped(own, "slow", 1)
+    (both,) = call(join_kernel, [(half_rows, width)], [], own, beside, rows_even, rows_odd)
+    other = swapped(both, "fast", 1)
 
     def objects_of(where_ref, base_ref, *rest):
         object_kernel(sizes, where_ref, base_ref, pairwise(rest[:swaps]), *rest[swaps:])
@@ -559,9 +618,13 @@
     (objects,) = call(
         objects_of, [(2, tile_rows, tile_cols)], [], where, base, *columns, rows_even, rows_odd, smem=1,
     )
+
+    def probe_of(where_ref, probe_ref, descan_ref, q0, q1, q2, *outs):
+        probe_kernel(sizes, total, where_ref, probe_ref, descan_ref, (q0, q1, q2), *outs)
+
     probes, descan_out = call(
-        functools.partial(probe_kernel, sizes, total), [probe_modes.shape, descan.shape], [],
-        where, probes, descan_rows, mine, other, smem=1,
+        probe_of, [probe_modes.shape, descan.shape], [],
+        where, probes, descan_rows, mine, beside, other, smem=1,
     )
     return objects, probes, descan_out
 

time: 84.8 us -> 81.1 us (0.956)
  the two profiles are of different devices: /device:TPU:1 before, /device:TPU:7 now
where the time goes in v2:
time: 81.1 us; the launch traced here: 79.6 us
  starting transfers between devices  36.5 us (45%)
  waiting for transfers between devices  28.9 us (36%)
  Pallas kernels  12 us (15%)
  local copies, waits for them, and re-layouts  1.08 us (1%)
  between operations  0.87 us (1%)
    ppermute x11, starting transfers between devices, exchanged(): return lax.ppermute(value, AXES, pairs)  23.2 us
    ppermute x13, waiting for transfers between devices, swapped(): lax.ppermute(value, axis, [(i, i ^ bit) for i in range(lax.axis_size(axis...  18.4 us
    ppermute x13, starting transfers between devices, swapped(): lax.ppermute(value, axis, [(i, i ^ bit) for i in range(lax.axis_size(axis...  13.3 us
    pallas_call x8, Pallas kernels, call(): pl.pallas_call(kernel, out_shape=[out if isinstance(out, jax.ShapeDtypeSt...  12 us
    ppermute x11, waiting for transfers between devices, exchanged(): return lax.ppermute(value, AXES, pairs)  10.6 us
  transfers between devices with their start and end apart: 24, of which 13 were waited for; matrix products, arithmetic and copies ran while one was open for 0% of the time, Pallas kernels for 3%

profile of v2, /device:TPU:7, one launch (start us, length us, event | category | flops | bytes accessed | tf_op | source)
XLA Modules:
  0.0 79.6 jit_solution(702697162530775753)
XLA Ops:
  3.2 3.0 %collective-permute-start.1 = (f32[2,64,256]{2,1,0:T(8,128)S(1)}, f32[2,64,256]{2,1,0:T(8,128)S(1)}, u32[]{:S(2)}, u32[]{:S(2)}) collective-permute-start(f32[2,64,256]{2,1,0:T(8,128)S(1)} %get-tuple-element.32), channel_id=1, source_target_pairs={{2,4},{3,5},{4,2},{5,3},{6,8},{7,9},{8,6},{9,7},{10,12},{11,13},{1... | collective-permute-start | bytes 393224 | tf_op jit(solution)/shard_map/ppermute | solution.py:503
  7.5 3.8 %collective-permute-start.4 = (f32[64,128]{1,0:T(8,128)S(1)}, f32[64,128]{1,0:T(8,128)S(1)}, u32[]{:S(2)}, u32[]{:S(2)}) collective-permute-start(f32[64,128]{1,0:T(8,128)S(1)} %get-tuple-element.35), channel_id=1, source_target_pairs={{2,5},{3,4},{4,3},{5,2},{6,9},{7,8},{8,7},{9,6},{10,13},{11,12},{1... | collective-permute-start | bytes 98312 | tf_op jit(solution)/shard_map/ppermute | solution.py:503
  11.3 1.2 %collective-permute-done.3.rest_3_ = f32[64,128]{1,0:T(8,128)S(1)} collective-permute-done((f32[64,128]{1,0:T(8,128)S(1)}, f32[64,128]{1,0:T(8,128)S(1)}, u32[]{:S(2)}, u32[]{:S(2)}) %collective-permute-start.3) | collective-permute-done | bytes 32800 | tf_op jit(solution)/shard_map/ppermute | solution.py:503
  12.4 2.0 %collective-permute-done.4.rest_4_ = f32[64,128]{1,0:T(8,128)S(1)} collective-permute-done((f32[64,128]{1,0:T(8,128)S(1)}, f32[64,128]{1,0:T(8,128)S(1)}, u32[]{:S(2)}, u32[]{:S(2)}) %collective-permute-start.4) | collective-permute-done | bytes 32800 | tf_op jit(solution)/shard_map/ppermute | solution.py:503
  14.6 3.2 %shard_map.86 = (f32[2,384,384]{2,1,0:T(8,128)S(1)}, f32[2,384,384]{2,1,0:T(8,128)S(1)}, f32[2,384,128]{2,1,0:T(8,128)S(1)}, f32[264,128]{1,0:T(8,128)S(1)}, f32[264,128]{1,0:T(8,128)S(1)}) custom-call(s32[2]{0:T(128)S(1)} %pad_add_fusion.where_ref.info_ref, s32[2,1,2]{2,1,0:T(1,128)S(1)} %bitcast.15, ...), custom_call_target="tpu_custom_call", output_to_operand_aliasing={{0}: (3, {})} | custom-call | tf_op jit(solution)/shard_map/pallas_call | solution.py:461
  19.3 5.0 %collective-permute-done.7 = f32[264,128]{1,0:T(8,128)S(1)} collective-permute-done((f32[264,128]{1,0:T(8,128)S(1)}, f32[264,128]{1,0:T(8,128)S(1)}, u32[]{:S(2)}, u32[]{:S(2)}) %collective-permute-start.7) | collective-permute-done | bytes 135200 | tf_op jit(solution)/shard_map/ppermute | solution.py:506
  24.3 1.4 %collective-permute-start.8 = (f32[264,128]{1,0:T(8,128)S(1)}, f32[264,128]{1,0:T(8,128)S(1)}, u32[]{:S(2)}, u32[]{:S(2)}) collective-permute-start(f32[264,128]{1,0:T(8,128)S(1)} %add.31), channel_id=1, source_target_pairs={{0,8},{2,10},{4,12},{6,14},{8,0},{10,2},{12,4},{14,6},{16,24},{18,... | collective-permute-start | bytes 405512 | tf_op jit(solution)/shard_map/ppermute | solution.py:506
  25.7 2.9 %collective-permute-done.8 = f32[264,128]{1,0:T(8,128)S(1)} collective-permute-done((f32[264,128]{1,0:T(8,128)S(1)}, f32[264,128]{1,0:T(8,128)S(1)}, u32[]{:S(2)}, u32[]{:S(2)}) %collective-permute-start.8) | collective-permute-done | bytes 135200 | tf_op jit(solution)/shard_map/ppermute | solution.py:506
  28.6 2.4 %collective-permute-start.11 = (f32[264,128]{1,0:T(8,128)S(1)}, f32[264,128]{1,0:T(8,128)S(1)}, u32[]{:S(2)}, u32[]{:S(2)}) collective-permute-start(f32[264,128]{1,0:T(8,128)S(1)} %add.32.rest_1_), channel_id=1, source_target_pairs={{0,16},{2,18},{4,20},{6,22},{8,24},{10,26},{12,28},{14,30},{16,0},... | collective-permute-start | bytes 405512 | tf_op jit(solution)/shard_map/ppermute | solution.py:506
  31.6 2.2 %collective-permute-start.9 = (f32[2,128,384]{2,1,0:T(8,128)S(1)}, f32[2,128,384]{2,1,0:T(8,128)S(1)}, u32[]{:S(2)}, u32[]{:S(2)}) collective-permute-start(f32[2,128,384]{2,1,0:T(8,128)S(1)} %get-tuple-element.41), channel_id=1, source_target_pairs={{0,2},{1,3},{2,0},{3,1},{4,6},{5,7},{6,4},{7,5},{8,10},{9,11},{10,... | collective-permute-start | bytes 1179656 | tf_op jit(solution)/shard_map/ppermute | solution.py:503
  33.8 3.5 %collective-permute-start.10 = (f32[2,128,384]{2,1,0:T(8,128)S(1)}, f32[2,128,384]{2,1,0:T(8,128)S(1)}, u32[]{:S(2)}, u32[]{:S(2)}) collective-permute-start(f32[2,128,384]{2,1,0:T(8,128)S(1)} %get-tuple-element.42), channel_id=1, source_target_pairs={{2,4},{3,5},{4,2},{5,3},{6,8},{7,9},{8,6},{9,7},{10,12},{11,13},{1... | collective-permute-start | bytes 1179656 | tf_op jit(solution)/shard_map/ppermute | solution.py:503
  37.9 3.7 %collective-permute-done.12 = f32[264,128]{1,0:T(8,128)S(1)} collective-permute-done((f32[264,128]{1,0:T(8,128)S(1)}, f32[264,128]{1,0:T(8,128)S(1)}, u32[]{:S(2)}, u32[]{:S(2)}) %collective-permute-start.12) | collective-permute-done | bytes 135200 | tf_op jit(solution)/shard_map/ppermute | solution.py:506
  41.6 2.0 %collective-permute-start.13 = (f32[256,128]{1,0:T(8,128)S(1)}, f32[256,128]{1,0:T(8,128)S(1)}, u32[]{:S(2)}, u32[]{:S(2)}) collective-permute-start(f32[256,128]{1,0:T(8,128)S(1)} %slice.16), channel_id=1, source_target_pairs={{0,2},{2,0},{4,6},{6,4},{8,10},{10,8},{12,14},{14,12},{16,18},{18,... | collective-permute-start | bytes 393224 | tf_op jit(solution)/shard_map/ppermute | solution.py:506
  44.6 3.8 %shard_map.88 = (f32[2,256,256]{2,1,0:T(8,128)S(1)}, f32[2,64,256]{2,1,0:T(8,128)S(1)}, f32[2,64,256]{2,1,0:T(8,128)S(1)}, f32[384,128]{1,0:T(8,128)S(1)}, f32[1...) custom-call(s32[2]{0:T(128)S(1)} %pad_add_fusion.where_ref.info_ref,, ...), custom_call_target="tpu_custom_call" | custom-call | tf_op jit(solution)/shard_map/pallas_call | solution.py:461
  48.5 2.6 %collective-permute-start.15 = (f32[2,136,128]{2,1,0:T(8,128)S(1)}, f32[2,136,128]{2,1,0:T(8,128)S(1)}, u32[]{:S(2)}, u32[]{:S(2)}) collective-permute-start(f32[2,136,128]{2,1,0:T(8,128)S(1)} %get-tuple-element.48), channel_id=1, source_target_pairs={{0,2},{2,0},{4,6},{6,4},{8,10},{10,8},{12,14},{14,12},{16,18},{18,... | collective-permute-start | bytes 417800 | tf_op jit(solution)/shard_map/ppermute | solution.py:506
  53.6 1.7 %collective-permute-done.16 = f32[136,128]{1,0:T(8,128)S(1)} collective-permute-done((f32[136,128]{1,0:T(8,128)S(1)}, f32[136,128]{1,0:T(8,128)S(1)}, u32[]{:S(2)}, u32[]{:S(2)}) %collective-permute-start.16) | collective-permute-done | bytes 69664 | tf_op jit(solution)/shard_map/ppermute | solution.py:506
  55.4 4.4 %collective-permute-done.14.rest_0_ = f32[384,128]{1,0:T(8,128)S(1)} collective-permute-done((f32[384,128]{1,0:T(8,128)S(1)}, f32[384,128]{1,0:T(8,128)S(1)}, u32[]{:S(2)}, u32[]{:S(2)}) %collective-permute-start.14) | collective-permute-done | bytes 196640 | tf_op jit(solution)/shard_map/ppermute | solution.py:503
  61.1 2.5 %collective-permute-done.20 = f32[136,128]{1,0:T(8,128)S(1)} collective-permute-done((f32[136,128]{1,0:T(8,128)S(1)}, f32[136,128]{1,0:T(8,128)S(1)}, u32[]{:S(2)}, u32[]{:S(2)}) %collective-permute-start.20) | collective-permute-done | bytes 69664 | tf_op jit(solution)/shard_map/ppermute | solution.py:506
  64.0 3.4 %collective-permute-start.18 = (f32[2,64,256]{2,1,0:T(8,128)S(1)}, f32[2,64,256]{2,1,0:T(8,128)S(1)}, u32[]{:S(2)}, u32[]{:S(2)}) collective-permute-start(f32[2,64,256]{2,1,0:T(8,128)S(1)} %get-tuple-element.50), channel_id=1, source_target_pairs={{0,2},{1,3},{2,0},{3,1},{4,6},{5,7},{6,4},{7,5},{8,10},{9,11},{10,... | collective-permute-start | bytes 393224 | tf_op jit(solution)/shard_map/ppermute | solution.py:503
  67.4 3.8 %collective-permute-start.19 = (f32[2,64,256]{2,1,0:T(8,128)S(1)}, f32[2,64,256]{2,1,0:T(8,128)S(1)}, u32[]{:S(2)}, u32[]{:S(2)}) collective-permute-start(f32[2,64,256]{2,1,0:T(8,128)S(1)} %get-tuple-element.51), channel_id=1, source_target_pairs={{2,4},{3,5},{4,2},{5,3},{6,8},{7,9},{8,6},{9,7},{10,12},{11,13},{1... | collective-permute-start | bytes 393224 | tf_op jit(solution)/shard_map/ppermute | solution.py:503
  71.8 2.7 %collective-permute-done.19.rest_2_.rest_1_ = f32[2,64,256]{2,1,0:T(8,128)S(1)} collective-permute-done((f32[2,64,256]{2,1,0:T(8,128)S(1)}, f32[2,64,256]{2,1,0:T(8,128)S(1)}, u32[]{:S(2)}, u32[]{:S(2)}) %collective-permute-start.19) | collective-permute-done | bytes 131104 | tf_op jit(solution)/shard_map/ppermute | solution.py:503
  74.6 2.1 %collective-permute-start.23 = (f32[256,128]{1,0:T(8,128)S(1)}, f32[256,128]{1,0:T(8,128)S(1)}, u32[]{:S(2)}, u32[]{:S(2)}) collective-permute-start(f32[256,128]{1,0:T(8,128)S(1)} %shard_map.91), channel_id=1, source_target_pairs={{0,2},{2,0},{4,6},{6,4},{8,10},{10,8},{12,14},{14,12},{16,18},{18,... | collective-permute-start | bytes 393224 | tf_op jit(solution)/shard_map/ppermute | solution.py:506
  76.7 1.5 %shard_map.90 = f32[2,256,256]{2,1,0:T(8,128)} custom-call(s32[2]{0:T(128)S(1)} %pad_add_fusion.where_ref.info_ref, f32[2,256,256]{2,1,0:T(8,128)S(1)} %get-tuple-element.43.base_ref, f32[384,128]{1,0:T(8,128)S(1)} %collective-permute-done.14.rest_0_, f32[2,64,256]{2,1,0:T(8,128)S(1)} %collective-permute-done.18.rest_1_.rest_0_, ...), custom_call_target="tpu_custom_call" | custom-call | tf_op jit(solution)/shard_map/pallas_call | solution.py:461
  78.2 1.4 %shard_map.92 = (f32[2,2,128,128]{3,2,1,0:T(8,128)}, f32[2,3]{1,0:T(2,128)}) custom-call(s32[2]{0:T(128)S(1)} %pad_add_fusion.where_ref.info_ref, f32[2,2,128,128]{3,2,1,0:T(8,128)S(1)} %get-tuple-element.52.probe_ref, f32[8,128]{1,0:T(8,128)S(1)} %get-tuple-element.53.descan_ref, f32[136,128]{1,0:T(8,128)S(1)} %add.39.q0, ...), custom_call_target="tpu_custom_call" | custom-call | tf_op jit(solution)/shard_map/pallas_call | solution.py:461
  (56 shorter events, 12.6 us)
Async XLA Ops:
  2.5 12.0 %collective-permute-start = (f32[2,64,256]{2,1,0:T(8,128)S(1)}, f32[2,64,256]{2,1,0:T(8,128)S(1)}, u32[]{:S(2)}, u32[]{:S(2)}) collective-permute-start(f32[2,64,256]{2,1,0:T(8,128)S(1)} %get-tuple-element.31), channel_id=1, source_target_pairs={{0,2},{1,3},{2,0},{3,1},{4,6},{5,7},{6,4},{7,5},{8,10},{9,11},{10,... | collective-permute-start | bytes 393224 | tf_op jit(solution)/shard_map/ppermute | solution.py:503
  3.2 11.2 %collective-permute-start.1 = (f32[2,64,256]{2,1,0:T(8,128)S(1)}, f32[2,64,256]{2,1,0:T(8,128)S(1)}, u32[]{:S(2)}, u32[]{:S(2)}) collective-permute-start(f32[2,64,256]{2,1,0:T(8,128)S(1)} %get-tuple-element.32), channel_id=1, source_target_pairs={{2,4},{3,5},{4,2},{5,3},{6,8},{7,9},{8,6},{9,7},{10,12},{11,13},{1... | collective-permute-start | bytes 393224 | tf_op jit(solution)/shard_map/ppermute | solution.py:503
  6.3 8.2 %collective-permute-start.2 = (f32[256,128]{1,0:T(8,128)S(1)}, f32[256,128]{1,0:T(8,128)S(1)}, u32[]{:S(2)}, u32[]{:S(2)}) collective-permute-start(f32[256,128]{1,0:T(8,128)S(1)} %get-tuple-element.33), channel_id=1, source_target_pairs={{0,1},{1,0},{2,3},{3,2},{4,5},{5,4},{6,7},{7,6},{8,9},{9,8},{10,11... | collective-permute-start | bytes 393224 | tf_op jit(solution)/shard_map/ppermute | solution.py:503
  6.6 5.8 %collective-permute-start.3 = (f32[64,128]{1,0:T(8,128)S(1)}, f32[64,128]{1,0:T(8,128)S(1)}, u32[]{:S(2)}, u32[]{:S(2)}) collective-permute-start(f32[64,128]{1,0:T(8,128)S(1)} %get-tuple-element.34), channel_id=1, source_target_pairs={{0,3},{1,2},{2,1},{3,0},{4,7},{5,6},{6,5},{7,4},{8,11},{9,10},{10,... | collective-permute-start | bytes 98312 | tf_op jit(solution)/shard_map/ppermute | solution.py:503
  7.5 7.0 %collective-permute-start.4 = (f32[64,128]{1,0:T(8,128)S(1)}, f32[64,128]{1,0:T(8,128)S(1)}, u32[]{:S(2)}, u32[]{:S(2)}) collective-permute-start(f32[64,128]{1,0:T(8,128)S(1)} %get-tuple-element.35), channel_id=1, source_target_pairs={{2,5},{3,4},{4,3},{5,2},{6,9},{7,8},{8,7},{9,6},{10,13},{11,12},{1... | collective-permute-start | bytes 98312 | tf_op jit(solution)/shard_map/ppermute | solution.py:503
  17.8 1.4 %collective-permute-start.6 = (f32[264,128]{1,0:T(8,128)S(1)}, f32[264,128]{1,0:T(8,128)S(1)}, u32[]{:S(2)}, u32[]{:S(2)}) collective-permute-start(f32[264,128]{1,0:T(8,128)S(1)} %get-tuple-element.40), channel_id=1, source_target_pairs={{0,2},{2,0},{4,6},{6,4},{8,10},{10,8},{12,14},{14,12},{16,18},{18,... | collective-permute-start | bytes 405512 | tf_op jit(solution)/shard_map/ppermute | solution.py:506
  17.9 13.1 %collective-permute-start.5 = (f32[2,384,128]{2,1,0:T(8,128)S(1)}, f32[2,384,128]{2,1,0:T(8,128)S(1)}, u32[]{:S(2)}, u32[]{:S(2)}) collective-permute-start(f32[2,384,128]{2,1,0:T(8,128)S(1)} %get-tuple-element.38), channel_id=1, source_target_pairs={{0,1},{1,0},{2,3},{3,2},{4,5},{5,4},{6,7},{7,6},{8,9},{9,8},{10,11... | collective-permute-start | bytes 1179656 | tf_op jit(solution)/shard_map/ppermute | solution.py:503
  19.2 5.1 %collective-permute-start.7 = (f32[264,128]{1,0:T(8,128)S(1)}, f32[264,128]{1,0:T(8,128)S(1)}, u32[]{:S(2)}, u32[]{:S(2)}) collective-permute-start(f32[264,128]{1,0:T(8,128)S(1)} %add.30), channel_id=1, source_target_pairs={{0,4},{2,6},{4,0},{6,2},{8,12},{10,14},{12,8},{14,10},{16,20},{18,... | collective-permute-start | bytes 405512 | tf_op jit(solution)/shard_map/ppermute | solution.py:506
  24.3 4.2 %collective-permute-start.8 = (f32[264,128]{1,0:T(8,128)S(1)}, f32[264,128]{1,0:T(8,128)S(1)}, u32[]{:S(2)}, u32[]{:S(2)}) collective-permute-start(f32[264,128]{1,0:T(8,128)S(1)} %add.31), channel_id=1, source_target_pairs={{0,8},{2,10},{4,12},{6,14},{8,0},{10,2},{12,4},{14,6},{16,24},{18,... | collective-permute-start | bytes 405512 | tf_op jit(solution)/shard_map/ppermute | solution.py:506
  28.6 8.8 %collective-permute-start.11 = (f32[264,128]{1,0:T(8,128)S(1)}, f32[264,128]{1,0:T(8,128)S(1)}, u32[]{:S(2)}, u32[]{:S(2)}) collective-permute-start(f32[264,128]{1,0:T(8,128)S(1)} %add.32.rest_1_), channel_id=1, source_target_pairs={{0,16},{2,18},{4,20},{6,22},{8,24},{10,26},{12,28},{14,30},{16,0},... | collective-permute-start | bytes 405512 | tf_op jit(solution)/shard_map/ppermute | solution.py:506
  31.6 12.0 %collective-permute-start.9 = (f32[2,128,384]{2,1,0:T(8,128)S(1)}, f32[2,128,384]{2,1,0:T(8,128)S(1)}, u32[]{:S(2)}, u32[]{:S(2)}) collective-permute-start(f32[2,128,384]{2,1,0:T(8,128)S(1)} %get-tuple-element.41), channel_id=1, source_target_pairs={{0,2},{1,3},{2,0},{3,1},{4,6},{5,7},{6,4},{7,5},{8,10},{9,11},{10,... | collective-permute-start | bytes 1179656 | tf_op jit(solution)/shard_map/ppermute | solution.py:503
  33.8 10.1 %collective-permute-start.10 = (f32[2,128,384]{2,1,0:T(8,128)S(1)}, f32[2,128,384]{2,1,0:T(8,128)S(1)}, u32[]{:S(2)}, u32[]{:S(2)}) collective-permute-start(f32[2,128,384]{2,1,0:T(8,128)S(1)} %get-tuple-element.42), channel_id=1, source_target_pairs={{2,4},{3,5},{4,2},{5,3},{6,8},{7,9},{8,6},{9,7},{10,12},{11,13},{1... | collective-permute-start | bytes 1179656 | tf_op jit(solution)/shard_map/ppermute | solution.py:503
  37.4 4.2 %collective-permute-start.12 = (f32[264,128]{1,0:T(8,128)S(1)}, f32[264,128]{1,0:T(8,128)S(1)}, u32[]{:S(2)}, u32[]{:S(2)}) collective-permute-start(f32[264,128]{1,0:T(8,128)S(1)} %add.33), channel_id=1, source_target_pairs={{0,1},{1,0},{2,3},{3,2},{4,5},{5,4},{6,7},{7,6},{8,9},{9,8},{10,11... | collective-permute-start | bytes 405512 | tf_op jit(solution)/shard_map/ppermute | solution.py:506
  41.6 3.0 %collective-permute-start.13 = (f32[256,128]{1,0:T(8,128)S(1)}, f32[256,128]{1,0:T(8,128)S(1)}, u32[]{:S(2)}, u32[]{:S(2)}) collective-permute-start(f32[256,128]{1,0:T(8,128)S(1)} %slice.16), channel_id=1, source_target_pairs={{0,2},{2,0},{4,6},{6,4},{8,10},{10,8},{12,14},{14,12},{16,18},{18,... | collective-permute-start | bytes 393224 | tf_op jit(solution)/shard_map/ppermute | solution.py:506
  48.5 3.6 %collective-permute-start.15 = (f32[2,136,128]{2,1,0:T(8,128)S(1)}, f32[2,136,128]{2,1,0:T(8,128)S(1)}, u32[]{:S(2)}, u32[]{:S(2)}) collective-permute-start(f32[2,136,128]{2,1,0:T(8,128)S(1)} %get-tuple-element.48), channel_id=1, source_target_pairs={{0,2},{2,0},{4,6},{6,4},{8,10},{10,8},{12,14},{14,12},{16,18},{18,... | collective-permute-start | bytes 417800 | tf_op jit(solution)/shard_map/ppermute | solution.py:506
  52.1 3.2 %collective-permute-start.16 = (f32[136,128]{1,0:T(8,128)S(1)}, f32[136,128]{1,0:T(8,128)S(1)}, u32[]{:S(2)}, u32[]{:S(2)}) collective-permute-start(f32[136,128]{1,0:T(8,128)S(1)} %fusion), channel_id=1, source_target_pairs={{0,1},{1,0},{2,3},{3,2},{4,5},{5,4},{6,7},{7,6},{8,9},{9,8},{10,11... | collective-permute-start | bytes 208904 | tf_op jit(solution)/shard_map/ppermute | solution.py:506
  52.5 7.3 %collective-permute-start.14 = (f32[384,128]{1,0:T(8,128)S(1)}, f32[384,128]{1,0:T(8,128)S(1)}, u32[]{:S(2)}, u32[]{:S(2)}) collective-permute-start(f32[384,128]{1,0:T(8,128)S(1)} %get-tuple-element.44), channel_id=1, source_target_pairs={{0,1},{1,0},{2,3},{3,2},{4,5},{5,4},{6,7},{7,6},{8,9},{9,8},{10,11... | collective-permute-start | bytes 589832 | tf_op jit(solution)/shard_map/ppermute | solution.py:503
  55.3 4.4 %collective-permute-start.17 = (f32[136,128]{1,0:T(8,128)S(1)}, f32[136,128]{1,0:T(8,128)S(1)}, u32[]{:S(2)}, u32[]{:S(2)}) collective-permute-start(f32[136,128]{1,0:T(8,128)S(1)} %fusion.2.rest_1_), channel_id=1, source_target_pairs={{0,4},{2,6},{4,0},{6,2},{8,12},{10,14},{12,8},{14,10},{16,20},{18,... | collective-permute-start | bytes 208904 | tf_op jit(solution)/shard_map/ppermute | solution.py:506
  60.4 3.2 %collective-permute-start.20 = (f32[136,128]{1,0:T(8,128)S(1)}, f32[136,128]{1,0:T(8,128)S(1)}, u32[]{:S(2)}, u32[]{:S(2)}) collective-permute-start(f32[136,128]{1,0:T(8,128)S(1)} %get-tuple-element.54), channel_id=1, source_target_pairs={{0,8},{2,10},{4,12},{6,14},{8,0},{10,2},{12,4},{14,6},{16,24},{18,... | collective-permute-start | bytes 208904 | tf_op jit(solution)/shard_map/ppermute | solution.py:506
  63.7 7.5 %collective-permute-start.21 = (f32[136,128]{1,0:T(8,128)S(1)}, f32[136,128]{1,0:T(8,128)S(1)}, u32[]{:S(2)}, u32[]{:S(2)}) collective-permute-start(f32[136,128]{1,0:T(8,128)S(1)} %add.38), channel_id=1, source_target_pairs={{0,16},{2,18},{4,20},{6,22},{8,24},{10,26},{12,28},{14,30},{16,0},... | collective-permute-start | bytes 208904 | tf_op jit(solution)/shard_map/ppermute | solution.py:506
  64.0 7.8 %collective-permute-start.18 = (f32[2,64,256]{2,1,0:T(8,128)S(1)}, f32[2,64,256]{2,1,0:T(8,128)S(1)}, u32[]{:S(2)}, u32[]{:S(2)}) collective-permute-start(f32[2,64,256]{2,1,0:T(8,128)S(1)} %get-tuple-element.50), channel_id=1, source_target_pairs={{0,2},{1,3},{2,0},{3,1},{4,6},{5,7},{6,4},{7,5},{8,10},{9,11},{10,... | collective-permute-start | bytes 393224 | tf_op jit(solution)/shard_map/ppermute | solution.py:503
  67.4 7.2 %collective-permute-start.19 = (f32[2,64,256]{2,1,0:T(8,128)S(1)}, f32[2,64,256]{2,1,0:T(8,128)S(1)}, u32[]{:S(2)}, u32[]{:S(2)}) collective-permute-start(f32[2,64,256]{2,1,0:T(8,128)S(1)} %get-tuple-element.51), channel_id=1, source_target_pairs={{2,4},{3,5},{4,2},{5,3},{6,8},{7,9},{8,6},{9,7},{10,12},{11,13},{1... | collective-permute-start | bytes 393224 | tf_op jit(solution)/shard_map/ppermute | solution.py:503
  71.2 3.3 %collective-permute-start.22 = (f32[128,128]{1,0:T(8,128)S(1)}, f32[128,128]{1,0:T(8,128)S(1)}, u32[]{:S(2)}, u32[]{:S(2)}) collective-permute-start(f32[128,128]{1,0:T(8,128)S(1)} %slice.19.own_ref), channel_id=1, source_target_pairs={{0,1},{1,0},{2,3},{3,2},{4,5},{5,4},{6,7},{7,6},{8,9},{9,8},{10,11... | collective-permute-start | bytes 196616 | tf_op jit(solution)/shard_map/ppermute | solution.py:506
  74.6 3.6 %collective-permute-start.23 = (f32[256,128]{1,0:T(8,128)S(1)}, f32[256,128]{1,0:T(8,128)S(1)}, u32[]{:S(2)}, u32[]{:S(2)}) collective-permute-start(f32[256,128]{1,0:T(8,128)S(1)} %shard_map.91), channel_id=1, source_target_pairs={{0,2},{2,0},{4,6},{6,4},{8,10},{10,8},{12,14},{14,12},{16,18},{18,... | collective-permute-start | bytes 393224 | tf_op jit(solution)/shard_map/ppermute | solution.py:506
  (6 other events, 64.9 us)

commit v3 on v2

--- a/solution.py
+++ b/solution.py
@@ -261,7 +261,7 @@
     return jnp.where(low, right, pltpu.roll(left, rim, 1)), jnp.where(low, pltpu.roll(right, rim, 1), left)
 
 
-def pack_kernel(sizes, where_ref, object_ref, extended_ref, rows_even_ref, rows_odd_ref, *rest):
+def pack_kernel(sizes, object_ref, extended_ref, rows_even_ref, rows_odd_ref, *rest):
     tile_rows, tile_cols, width, modes, count, n_fast, n_slow = sizes
     rim = width // 2
     *rest, semaphore = rest
@@ -269,7 +269,7 @@
     copy = pltpu.make_async_copy(object_ref, inner, semaphore)
     copy.start()
     copy.wait()
-    fast, slow = lax.rem(where_ref[0], 2), lax.rem(where_ref[1], 2)
+    fast, slow = lax.rem(lax.axis_index("fast"), 2), lax.rem(lax.axis_index("slow"), 2)
     initial, final = extended_ref[:, rim:width, :tile_cols], extended_ref[:, tile_rows : rim + tile_rows, :tile_cols]
     rows_even_ref[...] = pick(fast, final, initial)
     rows_odd_ref[...] = pick(fast, initial, final)
@@ -287,12 +287,12 @@
 
 
 def first_kernel(
-    sizes, info, starts, descan_ref, extended_in_ref, probe_ref, measured_ref, tables_ref,
+    sizes, starts, descan_ref, extended_in_ref, probe_ref, measured_ref, tables_ref,
     rows_even_ref, rows_odd_ref, halos,
     extended_ref, gradient_ref, strips, keep_ref, send_ref, wave_ref, far_ref,
 ):
     tile_rows, tile_cols, width, modes, count, n_fast, n_slow = sizes
-    fast, slow = info[0], info[1]
+    fast, slow = lax.axis_index("fast"), lax.axis_index("slow")
     core = lax.rem(fast, 2)
     rim = width // 2
     below, above = both_sides(core, rows_even_ref, rows_odd_ref)
@@ -308,7 +308,7 @@
         real, imag = halo_blocks(pick(lax.rem(slow, 2), even, odd), pick(lax.rem(slow, 2), odd, even), width)
         extended_ref[0, at : at + even.shape[0], tile_cols:] = real
         extended_ref[1, at : at + even.shape[0], tile_cols:] = imag
-    descan_rows = [jnp.full((1, width), descan_ref[k // 3, k % 3], F32) for k in range(6)]
+    descan_rows = [jnp.broadcast_to(descan_ref[k // 3 : k // 3 + 1, k % 3 : k % 3 + 1], (1, width)) for k in range(6)]
     probe = tuple(probe_ref[part].reshape(modes * width, width) for part in range(2))
     probe_grad, descan_grad = gradients(
         extended_ref, probe, descan_rows, starts, measured_ref, tables_ref, gradient_ref, wave_ref, far_ref,
@@ -340,25 +340,55 @@
     return jnp.concatenate(blocks, axis=2)
 
 
-def rows_kernel(sizes, where_ref, gradient_ref, columns, token_ref, even_ref, odd_ref):
-    tile_rows, tile_cols, width, modes, count, n_fast, n_slow = sizes
-    slow = lax.rem(where_ref[1], 2)
-    edges = []
-    for at in (0, tile_rows):
-        index = (slice(None), slice(at, at + width))
-        right, left = both_sides(slow, *columns, index)
-        edges.append(add_columns(gradient_ref[index], right, left, tile_cols, width))
-    put_strips(where_ref[0], edges[1], edges[0], (even_ref, odd_ref))
+def toward_next(odd):
+    return lax.rem(lax.axis_index("fast"), 2) == (1 if odd else 0)
+
+
+def packed_halo(halo):
+    rim = halo.shape[-1] // 2
+    low = lane_of(halo.shape[1:]) < rim
+    return jnp.where(low, halo[0], pltpu.roll(halo[1], rim, 1)), jnp.where(low, pltpu.roll(halo[0], rim, 1), halo[1])
+
+
+def rows_shape(sizes):
+    tile_rows, tile_cols, width, modes, count, n_fast, n_slow = sizes
+    return (width, 2 * tile_cols + width) if n_slow == 2 else (2, width, tile_cols + width)
+
+
+def rows_of(sizes, value):
+    tile_rows, tile_cols, width, modes, count, n_fast, n_slow = sizes
+    if n_slow > 2:
+        return value[0], value[1]
+    real, imag = halo_blocks(value[:, 2 * tile_cols :], value[:, 2 * tile_cols :], width)
+    return (
+        jnp.concatenate([value[:, :tile_cols], real], axis=1),
+        jnp.concatenate([value[:, tile_cols : 2 * tile_cols], imag], axis=1),
+    )
+
+
+def rows_kernel(sizes, odd, gradient_ref, columns, token_ref, out_ref):
+    tile_rows, tile_cols, width, modes, count, n_fast, n_slow = sizes
+    slow = lax.rem(lax.axis_index("slow"), 2)
+    at = pl.multiple_of(jnp.where(toward_next(odd), tile_rows, 0), 8)
+    index = (slice(None), pl.ds(at, width))
+    right, left = both_sides(slow, *columns, index)
+    value = add_columns(gradient_ref[index], right, left, tile_cols, width)
+    if n_slow > 2:
+        out_ref[...] = value
+        return
+    out_ref[:, :tile_cols] = value[0, :, :tile_cols]
+    out_ref[:, tile_cols : 2 * tile_cols] = value[1, :, :tile_cols]
+    out_ref[:, 2 * tile_cols :] = pick(slow, *packed_halo(value[:, :, tile_cols:]))
 
 
 def second_kernel(
-    sizes, total, where_ref, starts, descan_ref, extended_ref, gradient_in_ref, probe_ref, measured_ref, tables_ref,
+    sizes, total, starts, descan_ref, extended_ref, gradient_in_ref, probe_ref, measured_ref, tables_ref,
     columns, rows_even_ref, rows_odd_ref, mine_ref, other_ref,
     base_ref, up_ref, down_ref, strips, own_ref, beside_ref, send_ref, probe_out_ref, descan_out_ref,
     object_ref, gradient_ref, wave_ref, far_ref,
 ):
     tile_rows, tile_cols, width, modes, count, n_fast, n_slow = sizes
-    fast, slow = where_ref[0], where_ref[1]
+    fast, slow = lax.axis_index("fast"), lax.axis_index("slow")
     core = lax.rem(fast, 2)
     rim = width // 2
     right, left = both_sides(lax.rem(slow, 2), *columns)
@@ -366,15 +396,18 @@
         gradient_in_ref[...], right, left, tile_cols, width
     )
     below, above = both_sides(core, rows_even_ref, rows_odd_ref)
-    object_ref[:, :width] -= OBJECT_STEP * above
-    object_ref[:, tile_rows:] -= OBJECT_STEP * below
+    above, below = rows_of(sizes, above), rows_of(sizes, below)
+    for part in range(2):
+        object_ref[part, :width] -= OBJECT_STEP * above[part]
+        object_ref[part, tile_rows:] -= OBJECT_STEP * below[part]
     sums = of_halves((mine_ref, other_ref), core, slow, modes * width)
     probe = updated_probe(probe_ref, sums, total, width, modes)
     probe_out_ref[0] = probe[0].reshape(modes, width, width)
     probe_out_ref[1] = probe[1].reshape(modes, width, width)
     at = modes * width
     descan_rows = [
-        descan_ref[k // 3, k % 3] - DESCAN_STEP / total * mine_ref[at + k : at + k + 1] for k in range(6)
+        descan_ref[k // 3 : k // 3 + 1, k % 3 : k % 3 + 1] - DESCAN_STEP / total * mine_ref[at + k : at + k + 1]
+        for k in range(6)
     ]
     descan_out_ref[...] = jnp.concatenate(descan_rows + [jnp.zeros((EXTRA - 6, width), F32)], axis=0)
     probe_grad, descan_grad = gradients(
@@ -405,21 +438,20 @@
     return first, last
 
 
-def last_rows_kernel(sizes, where_ref, up_ref, down_ref, columns, mine_ref, arrived_ref, even_ref, odd_ref, sum_ref):
-    tile_rows, tile_cols, width, modes, count, n_fast, n_slow = sizes
-    rim = width // 2
-    sum_ref[...] = mine_ref[...] + arrived_ref[...]
-    edges = []
-    for in_ref, at in ((up_ref, 0), (down_ref, rim + tile_rows)):
-        first, last = edge_blocks(where_ref[1], columns, slice(at, at + rim), width)
-        rows = []
-        for part in range(2):
-            blocks = [in_ref[part, :, k : k + width] for k in range(0, tile_cols, width)]
-            blocks[0] = blocks[0] + first[part]
-            blocks[-1] = blocks[-1] + last[part]
-            rows.append(jnp.concatenate(blocks, axis=1))
-        edges.append(jnp.stack(rows))
-    put_strips(where_ref[0], edges[1], edges[0], (even_ref, odd_ref))
+def last_rows_kernel(sizes, odd, up_ref, down_ref, columns, mine_ref, *rest):
+    tile_rows, tile_cols, width, modes, count, n_fast, n_slow = sizes
+    rim = width // 2
+    out_ref = rest[-1]
+    if odd:
+        arrived_ref, sum_ref, out_ref = rest
+        sum_ref[...] = mine_ref[...] + arrived_ref[...]
+    following = toward_next(odd)
+    at = pl.multiple_of(jnp.where(following, rim + tile_rows, 0), 8)
+    out_ref[...] = jnp.where(following, down_ref[...], up_ref[...])
+    first, last = edge_blocks(lax.axis_index("slow"), columns, pl.ds(at, rim), width)
+    for part in range(2):
+        out_ref[part, :, :width] += first[part]
+        out_ref[part, :, tile_cols - width :] += last[part]
 
 
 def join_kernel(own_ref, beside_ref, *rest):
@@ -428,22 +460,22 @@
     rest[-1][rows:] = beside_ref[...]
 
 
-def object_kernel(sizes, where_ref, base_ref, columns, rows_even_ref, rows_odd_ref, out_ref):
+def object_kernel(sizes, base_ref, columns, rows_even_ref, rows_odd_ref, out_ref):
     tile_rows, tile_cols, width, modes, count, n_fast, n_slow = sizes
     rim = width // 2
     out_ref[...] = base_ref[...]
-    first, last = edge_blocks(where_ref[1], columns, slice(rim, rim + tile_rows), width)
+    first, last = edge_blocks(lax.axis_index("slow"), columns, slice(rim, rim + tile_rows), width)
     for part in range(2):
         out_ref[part, :, :width] -= OBJECT_STEP * first[part]
         out_ref[part, :, tile_cols - width :] -= OBJECT_STEP * last[part]
-    below, above = both_sides(lax.rem(where_ref[0], 2), rows_even_ref, rows_odd_ref)
+    below, above = both_sides(lax.rem(lax.axis_index("fast"), 2), rows_even_ref, rows_odd_ref)
     out_ref[:, :rim] -= OBJECT_STEP * above
     out_ref[:, tile_rows - rim :] -= OBJECT_STEP * below
 
 
-def probe_kernel(sizes, total, where_ref, probe_ref, descan_ref, quarters, probe_out_ref, descan_out_ref):
-    tile_rows, tile_cols, width, modes, count, n_fast, n_slow = sizes
-    core, slow = lax.rem(where_ref[0], 2), lax.rem(where_ref[1], 2)
+def probe_kernel(sizes, total, probe_ref, descan_ref, quarters, probe_out_ref, descan_out_ref):
+    tile_rows, tile_cols, width, modes, count, n_fast, n_slow = sizes
+    core, slow = lax.rem(lax.axis_index("fast"), 2), lax.rem(lax.axis_index("slow"), 2)
     sums = of_quarters(quarters, core, slow, modes * width)
     real, imag = updated_probe(probe_ref, sums, total, width, modes)
     probe_out_ref[0] = real.reshape(modes, width, width)
@@ -481,7 +513,6 @@
     total = count * n_fast * n_slow
     sizes = (tile_rows, tile_cols, width, modes, count, n_fast, n_slow)
     fast, slow = lax.axis_index("fast"), lax.axis_index("slow")
-    where = jnp.stack([fast, slow]).astype(jnp.int32)
     starts = scan_positions.transpose(0, 2, 1)
     tables = transform_tables(width)
     ext_rows, ext_cols = tile_rows + width, tile_cols + width
@@ -517,9 +548,11 @@
                 mine = mine + swapped(mine, "fast", bit)
         return mine
 
+    def fast_ended(mine):
+        return mine + swapped(mine, "fast", fast_bits[-1]) if regular else mine
+
     def sum_ended(mine):
         if regular:
-            mine = mine + swapped(mine, "fast", fast_bits[-1])
             for bit in slow_bits:
                 mine = mine + swapped(mine, "slow", bit)
         else:
@@ -535,7 +568,7 @@
         functools.partial(pack_kernel, sizes),
         [(2, ext_rows, ext_cols)] + [(2, rim, tile_cols)] * 2
         + [(tile_rows, width), (rim, width), (rim, width)] * swaps, [],
-        where, object_field, smem=1, hbm=True, semaphores=[()], work=WORK,
+        object_field, hbm=True, semaphores=[()], work=WORK,
     )
     halos = []
     rows_odd = exchanged(rows_odd, 1)
@@ -544,10 +577,10 @@
         middle = exchanged(packed[3 * k], None, k)
         halos += [middle, exchanged(packed[3 * k + 1], 0, k), corner_odd]
     rows_even = exchanged(rows_even, 0)
-    def first(info_ref, starts_ref, descan_ref, extended_ref, probe_ref, measured_ref, tables_ref, *rest):
+    def first(starts_ref, descan_ref, extended_ref, probe_ref, measured_ref, tables_ref, *rest):
         halo_refs = [rest[2 + 3 * k : 5 + 3 * k] for k in range(swaps)]
         extended_out_ref, gradient_ref, *rest_out = rest[2 + 3 * swaps :]
-        first_kernel(sizes, info_ref, starts_ref, descan_ref, extended_ref, probe_ref, measured_ref, tables_ref,
+        first_kernel(sizes, starts_ref, descan_ref, extended_ref, probe_ref, measured_ref, tables_ref,
                      *rest[:2], halo_refs, extended_out_ref, gradient_ref, rest_out[:swaps], *rest_out[swaps:])
 
     scratch = [(count * modes * width, 2 * width), (2 * width, count * modes * width)]
@@ -556,23 +589,26 @@
         first,
         [(2, ext_rows, ext_cols)] * 2 + [(2, ext_rows, width)] * swaps + sums,
         scratch,
-        where, starts, descan, extended, probe_modes, amplitudes, tables, rows_even, rows_odd, *halos,
-        smem=3, aliases={3: 0},
+        starts, descan, extended, probe_modes, amplitudes, tables, rows_even, rows_odd, *halos,
+        smem=1, aliases={2: 0},
     )
     columns = [exchanged(strip, None, k) for k, strip in enumerate(strips)]
     mine = sum_begun(keep, send)
 
-    def rows(where_ref, gradient_ref, *rest):
-        rows_kernel(sizes, where_ref, gradient_ref, pairwise(rest[:swaps]), *rest[swaps:])
-
-    rows_even, rows_odd = call(rows, [(2, width, ext_cols)] * 2, [], where, gradient, *columns, mine, smem=1)
-    rows_odd = exchanged(rows_odd, 1)
-    rows_even = exchanged(rows_even, 0)
+    def rows(odd, gradient_ref, *rest):
+        rows_kernel(sizes, odd, gradient_ref, pairwise(rest[:swaps]), *rest[swaps:])
+
+    def rows_for(odd, token):
+        return call(functools.partial(rows, odd), [rows_shape(sizes)], [], gradient, *columns, token)[0]
+
+    rows_odd = exchanged(rows_for(True, mine), 1)
+    rows_even = exchanged(rows_for(False, mine), 0)
+    mine = fast_ended(mine)
     mine, other = sum_ended(mine)
 
-    def second(where_ref, starts_ref, descan_ref, extended_ref, gradient_ref, probe_ref, measured_ref, tables_ref, *rest):
+    def second(starts_ref, descan_ref, extended_ref, gradient_ref, probe_ref, measured_ref, tables_ref, *rest):
         base_ref, up_ref, down_ref, *rest_out = rest[swaps + 4 :]
-        second_kernel(sizes, total, where_ref, starts_ref, descan_ref, extended_ref, gradient_ref, probe_ref,
+        second_kernel(sizes, total, starts_ref, descan_ref, extended_ref, gradient_ref, probe_ref,
                       measured_ref, tables_ref, pairwise(rest[:swaps]), *rest[swaps : swaps + 4],
                       base_ref, up_ref, down_ref, rest_out[:swaps], *rest_out[swaps:])
 
@@ -582,24 +618,23 @@
         [(2, tile_rows, tile_cols)] + [(2, rim, tile_cols)] * 2 + [(ext_rows, width)] * swaps + [part, part, (2, *part)]
         + [probe_modes.shape, (EXTRA, width)],
         [(2, ext_rows, ext_cols)] * 2 + scratch,
-        where, starts, descan, extended, gradient, probe_modes, amplitudes, tables,
+        starts, descan, extended, gradient, probe_modes, amplitudes, tables,
         *columns, rows_even, rows_odd, mine, other,
-        smem=3,
+        smem=1,
     )
     columns = [exchanged(strip, None, k) for k, strip in enumerate(strips)]
     core_part = swapped(send, "fast", 1)
     mine = mine + core_part[0] + swapped(beside + core_part[1], "slow", 1)
     steps = [("fast", bit) for bit in fast_bits] + [("slow", bit) for bit in slow_bits[1:]]
 
-    def last_rows(where_ref, up_ref, down_ref, *rest):
-        last_rows_kernel(sizes, where_ref, up_ref, down_ref, pairwise(rest[:swaps]), *rest[swaps:])
+    def last_rows(odd, up_ref, down_ref, *rest):
+        last_rows_kernel(sizes, odd, up_ref, down_ref, pairwise(rest[:swaps]), *rest[swaps:])
 
     arrived = swapped(mine, *steps[0]) if regular else jnp.zeros_like(mine)
-    rows_even, rows_odd, mine = call(
-        last_rows, [(2, rim, tile_cols)] * 2 + [part], [], where, up, down, *columns, mine, arrived, smem=1,
+    mine, rows_odd = call(
+        functools.partial(last_rows, True), [part, (2, rim, tile_cols)], [], up, down, *columns, mine, arrived,
     )
     rows_odd = exchanged(rows_odd, 1)
-    rows_even = exchanged(rows_even, 0)
     if regular:
         for step in steps[1:]:
             mine = mine + swapped(mine, *step)
@@ -607,24 +642,28 @@
         place = 2 * lax.rem(fast, 2) + lax.rem(slow, 2)
         every = lax.psum(jnp.where(jnp.arange(4)[:, None, None] == place, mine, 0.0), AXES)
         mine = lax.dynamic_index_in_dim(every, place, keepdims=False)
+    (rows_even,) = call(
+        functools.partial(last_rows, False), [(2, rim, tile_cols)], [], up, down, *columns, mine,
+    )
+    rows_even = exchanged(rows_even, 0)
     own = mine[: half_rows // 2]
     beside = swapped(own, "slow", 1)
     (both,) = call(join_kernel, [(half_rows, width)], [], own, beside, rows_even, rows_odd)
     other = swapped(both, "fast", 1)
 
-    def objects_of(where_ref, base_ref, *rest):
-        object_kernel(sizes, where_ref, base_ref, pairwise(rest[:swaps]), *rest[swaps:])
+    def objects_of(base_ref, *rest):
+        object_kernel(sizes, base_ref, pairwise(rest[:swaps]), *rest[swaps:])
 
     (objects,) = call(
-        objects_of, [(2, tile_rows, tile_cols)], [], where, base, *columns, rows_even, rows_odd, smem=1,
-    )
-
-    def probe_of(where_ref, probe_ref, descan_ref, q0, q1, q2, *outs):
-        probe_kernel(sizes, total, where_ref, probe_ref, descan_ref, (q0, q1, q2), *outs)
+        objects_of, [(2, tile_rows, tile_cols)], [], base, *columns, rows_even, rows_odd,
+    )
+
+    def probe_of(probe_ref, descan_ref, q0, q1, q2, *outs):
+        probe_kernel(sizes, total, probe_ref, descan_ref, (q0, q1, q2), *outs)
 
     probes, descan_out = call(
         probe_of, [probe_modes.shape, descan.shape], [],
-        where, probes, descan_rows, mine, beside, other, smem=1,
+        probes, descan_rows, mine, beside, other,
     )
     return objects, probes, descan_out
 

time: 81.1 us -> 77.4 us (0.954)
  Pallas kernels: 12 us -> 9.25 us
  starting transfers between devices: 36.5 us -> 35.3 us
  waiting for transfers between devices: 28.9 us -> 29.8 us
    pallas_call x8 -> x10, Pallas kernels: 12 us -> 9.25 us  [call(): pl.pallas_call(kernel, out_shape=[out if isinstance(out, jax.ShapeDtypeSt...]
    ppermute x13, waiting for transfers between devices: 18.4 us -> 20.3 us  [swapped(): lax.ppermute(value, axis, [(i, i ^ bit) for i in range(lax.axis_size(axis...]
    ppermute x13, starting transfers between devices: 13.3 us -> 12.1 us  [swapped(): lax.ppermute(value, axis, [(i, i ^ bit) for i in range(lax.axis_size(axis...]
    ppermute x11, waiting for transfers between devices: 10.6 us -> 9.54 us  [exchanged(): return lax.ppermute(value, AXES, pairs)]
  transfers between devices with their start and end apart: 24 -> 24, of which waited for: 13 -> 13; matrix products, arithmetic and copies ran while one was open for 0% -> 0% of each run, Pallas kernels for 3% -> 2%
where the time goes in v3:
time: 77.4 us; the launch traced here: 76.5 us
  starting transfers between devices  35.3 us (46%)
  waiting for transfers between devices  29.8 us (39%)
  Pallas kernels  9.25 us (12%)
  local copies, waits for them, and re-layouts  1.15 us (1%)
  between operations  0.87 us (1%)
    ppermute x11, starting transfers between devices, exchanged(): return lax.ppermute(value, AXES, pairs)  23.2 us
    ppermute x13, waiting for transfers between devices, swapped(): lax.ppermute(value, axis, [(i, i ^ bit) for i in range(lax.axis_size(axis...  20.3 us
    ppermute x13, starting transfers between devices, swapped(): lax.ppermute(value, axis, [(i, i ^ bit) for i in range(lax.axis_size(axis...  12.1 us
    ppermute x11, waiting for transfers between devices, exchanged(): return lax.ppermute(value, AXES, pairs)  9.54 us
    pallas_call x10, Pallas kernels, call(): pl.pallas_call(kernel, out_shape=[out if isinstance(out, jax.ShapeDtypeSt...  9.25 us
  transfers between devices with their start and end apart: 24, of which 13 were waited for; matrix products, arithmetic and copies ran while one was open for 0% of the time, Pallas kernels for 2%

profile of v3, /device:TPU:7, one launch (start us, length us, event | category | flops | bytes accessed | tf_op | source)
XLA Modules:
  0.0 76.5 jit_solution(6695494935752216681)
XLA Ops:
  0.7 1.1 %copy-done.5 = f32[2,256,256]{2,1,0:T(8,128)S(1)} copy-done((f32[2,256,256]{2,1,0:T(8,128)S(1)}, f32[2,256,256]{2,1,0:T(8,128)}, u32[]{:S(2)}) %copy-start.5) | copy-done | bytes 524312
  2.7 3.0 %collective-permute-start.1 = (f32[2,64,256]{2,1,0:T(8,128)S(1)}, f32[2,64,256]{2,1,0:T(8,128)S(1)}, u32[]{:S(2)}, u32[]{:S(2)}) collective-permute-start(f32[2,64,256]{2,1,0:T(8,128)S(1)} %get-tuple-element.29), channel_id=1, source_target_pairs={{2,4},{3,5},{4,2},{5,3},{6,8},{7,9},{8,6},{9,7},{10,12},{11,13},{1... | collective-permute-start | bytes 393224 | tf_op jit(solution)/shard_map/ppermute | solution.py:534
  6.9 3.8 %collective-permute-start.4 = (f32[64,128]{1,0:T(8,128)S(1)}, f32[64,128]{1,0:T(8,128)S(1)}, u32[]{:S(2)}, u32[]{:S(2)}) collective-permute-start(f32[64,128]{1,0:T(8,128)S(1)} %get-tuple-element.32), channel_id=1, source_target_pairs={{2,5},{3,4},{4,3},{5,2},{6,9},{7,8},{8,7},{9,6},{10,13},{11,12},{1... | collective-permute-start | bytes 98312 | tf_op jit(solution)/shard_map/ppermute | solution.py:534
  10.7 1.2 %collective-permute-done.3.rest_3_ = f32[64,128]{1,0:T(8,128)S(1)} collective-permute-done((f32[64,128]{1,0:T(8,128)S(1)}, f32[64,128]{1,0:T(8,128)S(1)}, u32[]{:S(2)}, u32[]{:S(2)}) %collective-permute-start.3) | collective-permute-done | bytes 32800 | tf_op jit(solution)/shard_map/ppermute | solution.py:534
  11.9 2.0 %collective-permute-done.4.rest_4_ = f32[64,128]{1,0:T(8,128)S(1)} collective-permute-done((f32[64,128]{1,0:T(8,128)S(1)}, f32[64,128]{1,0:T(8,128)S(1)}, u32[]{:S(2)}, u32[]{:S(2)}) %collective-permute-start.4) | collective-permute-done | bytes 32800 | tf_op jit(solution)/shard_map/ppermute | solution.py:534
  14.0 3.1 %shard_map.86 = (f32[2,384,384]{2,1,0:T(8,128)S(1)}, f32[2,384,384]{2,1,0:T(8,128)S(1)}, f32[2,384,128]{2,1,0:T(8,128)S(1)}, f32[264,128]{1,0:T(8,128)S(1)}, f32[264,128]{1,0:T(8,128)S(1)}) custom-call(s32[2,1,2]{2,1,0:T(1,128)S(1)} %bitcast.13, f32[2,3]{1,0:T(2,128)S(1)} %copy-done.4, ...), custom_call_target="tpu_custom_call", output_to_operand_aliasing={{0}: (2, {})} | custom-call | tf_op jit(solution)/shard_map/pallas_call | solution.py:493
  18.7 5.0 %collective-permute-done.7 = f32[264,128]{1,0:T(8,128)S(1)} collective-permute-done((f32[264,128]{1,0:T(8,128)S(1)}, f32[264,128]{1,0:T(8,128)S(1)}, u32[]{:S(2)}, u32[]{:S(2)}) %collective-permute-start.7) | collective-permute-done | bytes 135200 | tf_op jit(solution)/shard_map/ppermute | solution.py:537
  23.7 1.4 %collective-permute-start.8 = (f32[264,128]{1,0:T(8,128)S(1)}, f32[264,128]{1,0:T(8,128)S(1)}, u32[]{:S(2)}, u32[]{:S(2)}) collective-permute-start(f32[264,128]{1,0:T(8,128)S(1)} %add.31), channel_id=1, source_target_pairs={{0,8},{2,10},{4,12},{6,14},{8,0},{10,2},{12,4},{14,6},{16,24},{18,... | collective-permute-start | bytes 405512 | tf_op jit(solution)/shard_map/ppermute | solution.py:537
  25.1 2.9 %collective-permute-done.8 = f32[264,128]{1,0:T(8,128)S(1)} collective-permute-done((f32[264,128]{1,0:T(8,128)S(1)}, f32[264,128]{1,0:T(8,128)S(1)}, u32[]{:S(2)}, u32[]{:S(2)}) %collective-permute-start.8) | collective-permute-done | bytes 135200 | tf_op jit(solution)/shard_map/ppermute | solution.py:537
  28.0 2.4 %collective-permute-start.11 = (f32[264,128]{1,0:T(8,128)S(1)}, f32[264,128]{1,0:T(8,128)S(1)}, u32[]{:S(2)}, u32[]{:S(2)}) collective-permute-start(f32[264,128]{1,0:T(8,128)S(1)} %add.32.rest_1_), channel_id=1, source_target_pairs={{0,16},{2,18},{4,20},{6,22},{8,24},{10,26},{12,28},{14,30},{16,0},... | collective-permute-start | bytes 405512 | tf_op jit(solution)/shard_map/ppermute | solution.py:537
  30.5 2.2 %collective-permute-start.9 = (f32[128,640]{1,0:T(8,128)S(1)}, f32[128,640]{1,0:T(8,128)S(1)}, u32[]{:S(2)}, u32[]{:S(2)}) collective-permute-start(f32[128,640]{1,0:T(8,128)S(1)} %shard_map.87), channel_id=1, source_target_pairs={{0,2},{1,3},{2,0},{3,1},{4,6},{5,7},{6,4},{7,5},{8,10},{9,11},{10,... | collective-permute-start | bytes 983048 | tf_op jit(solution)/shard_map/ppermute | solution.py:534
  32.8 3.5 %collective-permute-start.10 = (f32[128,640]{1,0:T(8,128)S(1)}, f32[128,640]{1,0:T(8,128)S(1)}, u32[]{:S(2)}, u32[]{:S(2)}) collective-permute-start(f32[128,640]{1,0:T(8,128)S(1)} %shard_map.88), channel_id=1, source_target_pairs={{2,4},{3,5},{4,2},{5,3},{6,8},{7,9},{8,6},{9,7},{10,12},{11,13},{1... | collective-permute-start | bytes 983048 | tf_op jit(solution)/shard_map/ppermute | solution.py:534
  36.9 3.7 %collective-permute-done.12 = f32[264,128]{1,0:T(8,128)S(1)} collective-permute-done((f32[264,128]{1,0:T(8,128)S(1)}, f32[264,128]{1,0:T(8,128)S(1)}, u32[]{:S(2)}, u32[]{:S(2)}) %collective-permute-start.12) | collective-permute-done | bytes 135200 | tf_op jit(solution)/shard_map/ppermute | solution.py:537
  40.6 2.4 %collective-permute-start.13 = (f32[256,128]{1,0:T(8,128)S(1)}, f32[256,128]{1,0:T(8,128)S(1)}, u32[]{:S(2)}, u32[]{:S(2)}) collective-permute-start(f32[256,128]{1,0:T(8,128)S(1)} %slice.16), channel_id=1, source_target_pairs={{0,2},{2,0},{4,6},{6,4},{8,10},{10,8},{12,14},{14,12},{16,18},{18,... | collective-permute-start | bytes 393224 | tf_op jit(solution)/shard_map/ppermute | solution.py:537
  44.0 3.6 %shard_map.89 = (f32[2,256,256]{2,1,0:T(8,128)S(1)}, f32[2,64,256]{2,1,0:T(8,128)S(1)}, f32[2,64,256]{2,1,0:T(8,128)S(1)}, f32[384,128]{1,0:T(8,128)S(1)}, f32[1...) custom-call(s32[2,1,2]{2,1,0:T(1,128)S(1)} %bitcast.14, ...), custom_call_target="tpu_custom_call" | custom-call | tf_op jit(solution)/shard_map/pallas_call | solution.py:493
  48.4 1.0 %collective-permute-done.15 = f32[2,136,128]{2,1,0:T(8,128)S(1)} collective-permute-done((f32[2,136,128]{2,1,0:T(8,128)S(1)}, f32[2,136,128]{2,1,0:T(8,128)S(1)}, u32[]{:S(2)}, u32[]{:S(2)}) %collective-permute-start.15) | collective-permute-done | bytes 139296 | tf_op jit(solution)/shard_map/ppermute | solution.py:537
  49.8 1.1 %collective-permute-start.14 = (f32[384,128]{1,0:T(8,128)S(1)}, f32[384,128]{1,0:T(8,128)S(1)}, u32[]{:S(2)}, u32[]{:S(2)}) collective-permute-start(f32[384,128]{1,0:T(8,128)S(1)} %get-tuple-element.39), channel_id=1, source_target_pairs={{0,1},{1,0},{2,3},{3,2},{4,5},{5,4},{6,7},{7,6},{8,9},{9,8},{10,11... | collective-permute-start | bytes 589832 | tf_op jit(solution)/shard_map/ppermute | solution.py:534
  51.0 1.7 %collective-permute-done.16 = f32[136,128]{1,0:T(8,128)S(1)} collective-permute-done((f32[136,128]{1,0:T(8,128)S(1)}, f32[136,128]{1,0:T(8,128)S(1)}, u32[]{:S(2)}, u32[]{:S(2)}) %collective-permute-start.16) | collective-permute-done | bytes 69664 | tf_op jit(solution)/shard_map/ppermute | solution.py:537
  52.9 4.2 %collective-permute-done.14.rest_0_ = f32[384,128]{1,0:T(8,128)S(1)} collective-permute-done((f32[384,128]{1,0:T(8,128)S(1)}, f32[384,128]{1,0:T(8,128)S(1)}, u32[]{:S(2)}, u32[]{:S(2)}) %collective-permute-start.14) | collective-permute-done | bytes 196640 | tf_op jit(solution)/shard_map/ppermute | solution.py:534
  57.9 2.5 %collective-permute-done.18 = f32[136,128]{1,0:T(8,128)S(1)} collective-permute-done((f32[136,128]{1,0:T(8,128)S(1)}, f32[136,128]{1,0:T(8,128)S(1)}, u32[]{:S(2)}, u32[]{:S(2)}) %collective-permute-start.18) | collective-permute-done | bytes 69664 | tf_op jit(solution)/shard_map/ppermute | solution.py:537
  60.5 2.2 %collective-permute-start.19 = (f32[136,128]{1,0:T(8,128)S(1)}, f32[136,128]{1,0:T(8,128)S(1)}, u32[]{:S(2)}, u32[]{:S(2)}) collective-permute-start(f32[136,128]{1,0:T(8,128)S(1)} %add.38), channel_id=1, source_target_pairs={{0,16},{2,18},{4,20},{6,22},{8,24},{10,26},{12,28},{14,30},{16,0},... | collective-permute-start | bytes 208904 | tf_op jit(solution)/shard_map/ppermute | solution.py:537
  62.6 6.7 %collective-permute-start.21 = (f32[2,64,256]{2,1,0:T(8,128)S(1)}, f32[2,64,256]{2,1,0:T(8,128)S(1)}, u32[]{:S(2)}, u32[]{:S(2)}) collective-permute-start(f32[2,64,256]{2,1,0:T(8,128)S(1)} %get-tuple-element.46), channel_id=1, source_target_pairs={{2,4},{3,5},{4,2},{5,3},{6,8},{7,9},{8,6},{9,7},{10,12},{11,13},{1... | collective-permute-start | bytes 393224 | tf_op jit(solution)/shard_map/ppermute | solution.py:534
  70.0 2.1 %collective-permute-done.21.rest_2_.rest_1_ = f32[2,64,256]{2,1,0:T(8,128)S(1)} collective-permute-done((f32[2,64,256]{2,1,0:T(8,128)S(1)}, f32[2,64,256]{2,1,0:T(8,128)S(1)}, u32[]{:S(2)}, u32[]{:S(2)}) %collective-permute-start.21) | collective-permute-done | bytes 131104 | tf_op jit(solution)/shard_map/ppermute | solution.py:534
  72.0 1.6 %collective-permute-done.22.beside_ref.q1 = f32[128,128]{1,0:T(8,128)S(1)} collective-permute-done((f32[128,128]{1,0:T(8,128)S(1)}, f32[128,128]{1,0:T(8,128)S(1)}, u32[]{:S(2)}, u32[]{:S(2)}) %collective-permute-start.22) | collective-permute-done | bytes 65568 | tf_op jit(solution)/shard_map/ppermute | solution.py:537
  (57 shorter events, 11.2 us)
Async XLA Ops:
  2.0 12.0 %collective-permute-start = (f32[2,64,256]{2,1,0:T(8,128)S(1)}, f32[2,64,256]{2,1,0:T(8,128)S(1)}, u32[]{:S(2)}, u32[]{:S(2)}) collective-permute-start(f32[2,64,256]{2,1,0:T(8,128)S(1)} %get-tuple-element.28), channel_id=1, source_target_pairs={{0,2},{1,3},{2,0},{3,1},{4,6},{5,7},{6,4},{7,5},{8,10},{9,11},{10,... | collective-permute-start | bytes 393224 | tf_op jit(solution)/shard_map/ppermute | solution.py:534
  2.7 11.2 %collective-permute-start.1 = (f32[2,64,256]{2,1,0:T(8,128)S(1)}, f32[2,64,256]{2,1,0:T(8,128)S(1)}, u32[]{:S(2)}, u32[]{:S(2)}) collective-permute-start(f32[2,64,256]{2,1,0:T(8,128)S(1)} %get-tuple-element.29), channel_id=1, source_target_pairs={{2,4},{3,5},{4,2},{5,3},{6,8},{7,9},{8,6},{9,7},{10,12},{11,13},{1... | collective-permute-start | bytes 393224 | tf_op jit(solution)/shard_map/ppermute | solution.py:534
  5.8 8.2 %collective-permute-start.2 = (f32[256,128]{1,0:T(8,128)S(1)}, f32[256,128]{1,0:T(8,128)S(1)}, u32[]{:S(2)}, u32[]{:S(2)}) collective-permute-start(f32[256,128]{1,0:T(8,128)S(1)} %get-tuple-element.30), channel_id=1, source_target_pairs={{0,1},{1,0},{2,3},{3,2},{4,5},{5,4},{6,7},{7,6},{8,9},{9,8},{10,11... | collective-permute-start | bytes 393224 | tf_op jit(solution)/shard_map/ppermute | solution.py:534
  6.1 5.8 %collective-permute-start.3 = (f32[64,128]{1,0:T(8,128)S(1)}, f32[64,128]{1,0:T(8,128)S(1)}, u32[]{:S(2)}, u32[]{:S(2)}) collective-permute-start(f32[64,128]{1,0:T(8,128)S(1)} %get-tuple-element.31), channel_id=1, source_target_pairs={{0,3},{1,2},{2,1},{3,0},{4,7},{5,6},{6,5},{7,4},{8,11},{9,10},{10,... | collective-permute-start | bytes 98312 | tf_op jit(solution)/shard_map/ppermute | solution.py:534
  6.9 7.0 %collective-permute-start.4 = (f32[64,128]{1,0:T(8,128)S(1)}, f32[64,128]{1,0:T(8,128)S(1)}, u32[]{:S(2)}, u32[]{:S(2)}) collective-permute-start(f32[64,128]{1,0:T(8,128)S(1)} %get-tuple-element.32), channel_id=1, source_target_pairs={{2,5},{3,4},{4,3},{5,2},{6,9},{7,8},{8,7},{9,6},{10,13},{11,12},{1... | collective-permute-start | bytes 98312 | tf_op jit(solution)/shard_map/ppermute | solution.py:534
  17.2 1.4 %collective-permute-start.6 = (f32[264,128]{1,0:T(8,128)S(1)}, f32[264,128]{1,0:T(8,128)S(1)}, u32[]{:S(2)}, u32[]{:S(2)}) collective-permute-start(f32[264,128]{1,0:T(8,128)S(1)} %get-tuple-element.37), channel_id=1, source_target_pairs={{0,2},{2,0},{4,6},{6,4},{8,10},{10,8},{12,14},{14,12},{16,18},{18,... | collective-permute-start | bytes 405512 | tf_op jit(solution)/shard_map/ppermute | solution.py:537
  17.3 13.1 %collective-permute-start.5 = (f32[2,384,128]{2,1,0:T(8,128)S(1)}, f32[2,384,128]{2,1,0:T(8,128)S(1)}, u32[]{:S(2)}, u32[]{:S(2)}) collective-permute-start(f32[2,384,128]{2,1,0:T(8,128)S(1)} %get-tuple-element.35), channel_id=1, source_target_pairs={{0,1},{1,0},{2,3},{3,2},{4,5},{5,4},{6,7},{7,6},{8,9},{9,8},{10,11... | collective-permute-start | bytes 1179656 | tf_op jit(solution)/shard_map/ppermute | solution.py:534
  18.6 5.1 %collective-permute-start.7 = (f32[264,128]{1,0:T(8,128)S(1)}, f32[264,128]{1,0:T(8,128)S(1)}, u32[]{:S(2)}, u32[]{:S(2)}) collective-permute-start(f32[264,128]{1,0:T(8,128)S(1)} %add.30), channel_id=1, source_target_pairs={{0,4},{2,6},{4,0},{6,2},{8,12},{10,14},{12,8},{14,10},{16,20},{18,... | collective-permute-start | bytes 405512 | tf_op jit(solution)/shard_map/ppermute | solution.py:537
  23.7 4.2 %collective-permute-start.8 = (f32[264,128]{1,0:T(8,128)S(1)}, f32[264,128]{1,0:T(8,128)S(1)}, u32[]{:S(2)}, u32[]{:S(2)}) collective-permute-start(f32[264,128]{1,0:T(8,128)S(1)} %add.31), channel_id=1, source_target_pairs={{0,8},{2,10},{4,12},{6,14},{8,0},{10,2},{12,4},{14,6},{16,24},{18,... | collective-permute-start | bytes 405512 | tf_op jit(solution)/shard_map/ppermute | solution.py:537
  28.0 8.3 %collective-permute-start.11 = (f32[264,128]{1,0:T(8,128)S(1)}, f32[264,128]{1,0:T(8,128)S(1)}, u32[]{:S(2)}, u32[]{:S(2)}) collective-permute-start(f32[264,128]{1,0:T(8,128)S(1)} %add.32.rest_1_), channel_id=1, source_target_pairs={{0,16},{2,18},{4,20},{6,22},{8,24},{10,26},{12,28},{14,30},{16,0},... | collective-permute-start | bytes 405512 | tf_op jit(solution)/shard_map/ppermute | solution.py:537
  30.5 12.6 %collective-permute-start.9 = (f32[128,640]{1,0:T(8,128)S(1)}, f32[128,640]{1,0:T(8,128)S(1)}, u32[]{:S(2)}, u32[]{:S(2)}) collective-permute-start(f32[128,640]{1,0:T(8,128)S(1)} %shard_map.87), channel_id=1, source_target_pairs={{0,2},{1,3},{2,0},{3,1},{4,6},{5,7},{6,4},{7,5},{8,10},{9,11},{10,... | collective-permute-start | bytes 983048 | tf_op jit(solution)/shard_map/ppermute | solution.py:534
  32.8 10.3 %collective-permute-start.10 = (f32[128,640]{1,0:T(8,128)S(1)}, f32[128,640]{1,0:T(8,128)S(1)}, u32[]{:S(2)}, u32[]{:S(2)}) collective-permute-start(f32[128,640]{1,0:T(8,128)S(1)} %shard_map.88), channel_id=1, source_target_pairs={{2,4},{3,5},{4,2},{5,3},{6,8},{7,9},{8,6},{9,7},{10,12},{11,13},{1... | collective-permute-start | bytes 983048 | tf_op jit(solution)/shard_map/ppermute | solution.py:534
  36.3 4.2 %collective-permute-start.12 = (f32[264,128]{1,0:T(8,128)S(1)}, f32[264,128]{1,0:T(8,128)S(1)}, u32[]{:S(2)}, u32[]{:S(2)}) collective-permute-start(f32[264,128]{1,0:T(8,128)S(1)} %add.33), channel_id=1, source_target_pairs={{0,1},{1,0},{2,3},{3,2},{4,5},{5,4},{6,7},{7,6},{8,9},{9,8},{10,11... | collective-permute-start | bytes 405512 | tf_op jit(solution)/shard_map/ppermute | solution.py:537
  40.6 3.4 %collective-permute-start.13 = (f32[256,128]{1,0:T(8,128)S(1)}, f32[256,128]{1,0:T(8,128)S(1)}, u32[]{:S(2)}, u32[]{:S(2)}) collective-permute-start(f32[256,128]{1,0:T(8,128)S(1)} %slice.16), channel_id=1, source_target_pairs={{0,2},{2,0},{4,6},{6,4},{8,10},{10,8},{12,14},{14,12},{16,18},{18,... | collective-permute-start | bytes 393224 | tf_op jit(solution)/shard_map/ppermute | solution.py:537
  47.7 1.7 %collective-permute-start.15 = (f32[2,136,128]{2,1,0:T(8,128)S(1)}, f32[2,136,128]{2,1,0:T(8,128)S(1)}, u32[]{:S(2)}, u32[]{:S(2)}) collective-permute-start(f32[2,136,128]{2,1,0:T(8,128)S(1)} %get-tuple-element.43), channel_id=1, source_target_pairs={{0,2},{2,0},{4,6},{6,4},{8,10},{10,8},{12,14},{14,12},{16,18},{18,... | collective-permute-start | bytes 417800 | tf_op jit(solution)/shard_map/ppermute | solution.py:537
  49.4 3.2 %collective-permute-start.16 = (f32[136,128]{1,0:T(8,128)S(1)}, f32[136,128]{1,0:T(8,128)S(1)}, u32[]{:S(2)}, u32[]{:S(2)}) collective-permute-start(f32[136,128]{1,0:T(8,128)S(1)} %fusion), channel_id=1, source_target_pairs={{0,1},{1,0},{2,3},{3,2},{4,5},{5,4},{6,7},{7,6},{8,9},{9,8},{10,11... | collective-permute-start | bytes 208904 | tf_op jit(solution)/shard_map/ppermute | solution.py:537
  49.8 7.3 %collective-permute-start.14 = (f32[384,128]{1,0:T(8,128)S(1)}, f32[384,128]{1,0:T(8,128)S(1)}, u32[]{:S(2)}, u32[]{:S(2)}) collective-permute-start(f32[384,128]{1,0:T(8,128)S(1)} %get-tuple-element.39), channel_id=1, source_target_pairs={{0,1},{1,0},{2,3},{3,2},{4,5},{5,4},{6,7},{7,6},{8,9},{9,8},{10,11... | collective-permute-start | bytes 589832 | tf_op jit(solution)/shard_map/ppermute | solution.py:534
  52.7 4.4 %collective-permute-start.17 = (f32[136,128]{1,0:T(8,128)S(1)}, f32[136,128]{1,0:T(8,128)S(1)}, u32[]{:S(2)}, u32[]{:S(2)}) collective-permute-start(f32[136,128]{1,0:T(8,128)S(1)} %fusion.2.rest_1_), channel_id=1, source_target_pairs={{0,4},{2,6},{4,0},{6,2},{8,12},{10,14},{12,8},{14,10},{16,20},{18,... | collective-permute-start | bytes 208904 | tf_op jit(solution)/shard_map/ppermute | solution.py:537
  57.2 3.2 %collective-permute-start.18 = (f32[136,128]{1,0:T(8,128)S(1)}, f32[136,128]{1,0:T(8,128)S(1)}, u32[]{:S(2)}, u32[]{:S(2)}) collective-permute-start(f32[136,128]{1,0:T(8,128)S(1)} %get-tuple-element.45), channel_id=1, source_target_pairs={{0,8},{2,10},{4,12},{6,14},{8,0},{10,2},{12,4},{14,6},{16,24},{18,... | collective-permute-start | bytes 208904 | tf_op jit(solution)/shard_map/ppermute | solution.py:537
  60.5 8.8 %collective-permute-start.19 = (f32[136,128]{1,0:T(8,128)S(1)}, f32[136,128]{1,0:T(8,128)S(1)}, u32[]{:S(2)}, u32[]{:S(2)}) collective-permute-start(f32[136,128]{1,0:T(8,128)S(1)} %add.38), channel_id=1, source_target_pairs={{0,16},{2,18},{4,20},{6,22},{8,24},{10,26},{12,28},{14,30},{16,0},... | collective-permute-start | bytes 208904 | tf_op jit(solution)/shard_map/ppermute | solution.py:537
  62.6 9.4 %collective-permute-start.21 = (f32[2,64,256]{2,1,0:T(8,128)S(1)}, f32[2,64,256]{2,1,0:T(8,128)S(1)}, u32[]{:S(2)}, u32[]{:S(2)}) collective-permute-start(f32[2,64,256]{2,1,0:T(8,128)S(1)} %get-tuple-element.46), channel_id=1, source_target_pairs={{2,4},{3,5},{4,2},{5,3},{6,8},{7,9},{8,6},{9,7},{10,12},{11,13},{1... | collective-permute-start | bytes 393224 | tf_op jit(solution)/shard_map/ppermute | solution.py:534
  69.4 4.2 %collective-permute-start.20 = (f32[2,64,256]{2,1,0:T(8,128)S(1)}, f32[2,64,256]{2,1,0:T(8,128)S(1)}, u32[]{:S(2)}, u32[]{:S(2)}) collective-permute-start(f32[2,64,256]{2,1,0:T(8,128)S(1)} %shard_map.91), channel_id=1, source_target_pairs={{0,2},{1,3},{2,0},{3,1},{4,6},{5,7},{6,4},{7,5},{8,10},{9,11},{10,... | collective-permute-start | bytes 393224 | tf_op jit(solution)/shard_map/ppermute | solution.py:534
  70.0 3.7 %collective-permute-start.22 = (f32[128,128]{1,0:T(8,128)S(1)}, f32[128,128]{1,0:T(8,128)S(1)}, u32[]{:S(2)}, u32[]{:S(2)}) collective-permute-start(f32[128,128]{1,0:T(8,128)S(1)} %slice.19.own_ref), channel_id=1, source_target_pairs={{0,1},{1,0},{2,3},{3,2},{4,5},{5,4},{6,7},{7,6},{8,9},{9,8},{10,11... | collective-permute-start | bytes 196616 | tf_op jit(solution)/shard_map/ppermute | solution.py:537
  73.6 1.9 %collective-permute-start.23 = (f32[256,128]{1,0:T(8,128)S(1)}, f32[256,128]{1,0:T(8,128)S(1)}, u32[]{:S(2)}, u32[]{:S(2)}) collective-permute-start(f32[256,128]{1,0:T(8,128)S(1)} %shard_map.93), channel_id=1, source_target_pairs={{0,2},{2,0},{4,6},{6,4},{8,10},{10,8},{12,14},{14,12},{16,18},{18,... | collective-permute-start | bytes 393224 | tf_op jit(solution)/shard_map/ppermute | solution.py:537
  (6 other events, 66.7 us)

commit v4 on v3

--- a/solution.py
+++ b/solution.py
@@ -30,18 +30,21 @@
     angles = 2.0 * np.pi / width * (counter[:, None] * counter[None, :] % width)
     real = np.cos(angles) / math.sqrt(width)
     imag = -np.sin(angles) / math.sqrt(width)
-    forward = np.block([[real, imag], [-imag, real]]).astype(np.float32)
-    backward = np.block([[real, -imag], [imag, real]]).astype(np.float32)
+    forward = np.block([[real, imag], [-imag, real]])
+    backward = np.block([[real, -imag], [imag, real]])
     parts = []
     for table in (forward, backward):
-        high = table.astype(BF16)
-        parts += [high, (table - high.astype(np.float32)).astype(BF16)]
+        for _ in range(3):
+            parts.append(table.astype(BF16))
+            table = table - parts[-1].astype(np.float64)
     return jnp.asarray(np.stack(parts))
 
 
 def split(value):
     high = value.astype(BF16)
-    return high, (value - high.astype(F32)).astype(BF16)
+    value = value - high.astype(F32)
+    middle = value.astype(BF16)
+    return high, middle, (value - middle.astype(F32)).astype(BF16)
 
 
 def dot(a, b):
@@ -49,8 +52,8 @@
 
 
 def product(left, right):
-    (left_high, left_low), (right_high, right_low) = left, right
-    return dot(left_high, right_high) + dot(left_high, right_low) + dot(left_low, right_high)
+    (a, b, c), (d, e, f) = left, right
+    return dot(a, d) + (dot(a, e) + dot(b, d) + (dot(b, e) + dot(a, f) + dot(c, d)))
 
 
 def lane_of(shape):
@@ -75,8 +78,8 @@
     probe_real, probe_imag = probe
     lane_row = lane_of((1, width)).astype(F32)
     centred = (lane_row - width // 2) / width
-    tables = [tables_ref[k] for k in range(4)]
-    forward, backward = (tables[0], tables[1]), (tables[2], tables[3])
+    tables = [tables_ref[k] for k in range(6)]
+    forward, backward = tables[:3], tables[3:]
 
     fractions = []
     phases = []
@@ -264,26 +267,27 @@
 def pack_kernel(sizes, object_ref, extended_ref, rows_even_ref, rows_odd_ref, *rest):
     tile_rows, tile_cols, width, modes, count, n_fast, n_slow = sizes
     rim = width // 2
-    *rest, semaphore = rest
-    inner = extended_ref.at[:, rim : rim + tile_rows, :tile_cols]
-    copy = pltpu.make_async_copy(object_ref, inner, semaphore)
-    copy.start()
-    copy.wait()
-    fast, slow = lax.rem(lax.axis_index("fast"), 2), lax.rem(lax.axis_index("slow"), 2)
-    initial, final = extended_ref[:, rim:width, :tile_cols], extended_ref[:, tile_rows : rim + tile_rows, :tile_cols]
+    extended_ref[:, rim : rim + tile_rows, :tile_cols] = object_ref[...]
+    fast = lax.rem(lax.axis_index("fast"), 2)
+    initial, final = object_ref[:, :rim], object_ref[:, tile_rows - rim :]
     rows_even_ref[...] = pick(fast, final, initial)
     rows_odd_ref[...] = pick(fast, initial, final)
-    low = lane_of((tile_rows, width)) < rim
-    end = extended_ref[:, rim : rim + tile_rows, tile_cols - width : tile_cols]
-    start = extended_ref[:, rim : rim + tile_rows, :width]
+    swaps = len(rest) // 3
+    put_edges(sizes, object_ref[...], rest[::3])
+    for k in range(swaps):
+        first, last = rest[3 * k][:rim], rest[3 * k][tile_rows - rim :]
+        rest[3 * k + 1][...] = pick(fast, last, first)
+        rest[3 * k + 2][...] = pick(fast, first, last)
+
+
+def put_edges(sizes, rows, refs):
+    tile_rows, tile_cols, width, modes, count, n_fast, n_slow = sizes
+    rim = width // 2
+    end, start = rows[:, :, tile_cols - width :], rows[:, :, :width]
+    low = lane_of(end.shape[1:]) < rim
     to_right = jnp.where(low, pltpu.roll(end[0], rim, 1), end[1])
     to_left = jnp.where(low, start[0], pltpu.roll(start[1], rim, 1))
-    strips = (pick(slow, to_right, to_left), pick(slow, to_left, to_right))
-    for k in range(len(rest) // 3):
-        strip = strips[k]
-        rest[3 * k][...] = strip
-        rest[3 * k + 1][...] = pick(fast, strip[tile_rows - rim :], strip[:rim])
-        rest[3 * k + 2][...] = pick(fast, strip[:rim], strip[tile_rows - rim :])
+    put_strips(lax.axis_index("slow"), to_right, to_left, refs)
 
 
 def first_kernel(
@@ -381,25 +385,25 @@
     out_ref[:, 2 * tile_cols :] = pick(slow, *packed_halo(value[:, :, tile_cols:]))
 
 
-def second_kernel(
-    sizes, total, starts, descan_ref, extended_ref, gradient_in_ref, probe_ref, measured_ref, tables_ref,
-    columns, rows_even_ref, rows_odd_ref, mine_ref, other_ref,
-    base_ref, up_ref, down_ref, strips, own_ref, beside_ref, send_ref, probe_out_ref, descan_out_ref,
-    object_ref, gradient_ref, wave_ref, far_ref,
-):
-    tile_rows, tile_cols, width, modes, count, n_fast, n_slow = sizes
-    fast, slow = lax.axis_index("fast"), lax.axis_index("slow")
-    core = lax.rem(fast, 2)
-    rim = width // 2
-    right, left = both_sides(lax.rem(slow, 2), *columns)
-    object_ref[...] = extended_ref[...] - OBJECT_STEP * add_columns(
-        gradient_in_ref[...], right, left, tile_cols, width
-    )
-    below, above = both_sides(core, rows_even_ref, rows_odd_ref)
+def update_kernel(sizes, extended_ref, gradient_ref, columns, rows_even_ref, rows_odd_ref, object_ref):
+    tile_rows, tile_cols, width, modes, count, n_fast, n_slow = sizes
+    right, left = both_sides(lax.rem(lax.axis_index("slow"), 2), *columns)
+    object_ref[...] = extended_ref[...] - OBJECT_STEP * add_columns(gradient_ref[...], right, left, tile_cols, width)
+    below, above = both_sides(lax.rem(lax.axis_index("fast"), 2), rows_even_ref, rows_odd_ref)
     above, below = rows_of(sizes, above), rows_of(sizes, below)
     for part in range(2):
         object_ref[part, :width] -= OBJECT_STEP * above[part]
         object_ref[part, tile_rows:] -= OBJECT_STEP * below[part]
+
+
+def second_kernel(
+    sizes, total, starts, descan_ref, object_ref, probe_ref, measured_ref, tables_ref, mine_ref, other_ref,
+    gradient_ref, strips, own_ref, beside_ref, send_ref, probe_out_ref, descan_out_ref, wave_ref, far_ref,
+):
+    tile_rows, tile_cols, width, modes, count, n_fast, n_slow = sizes
+    fast, slow = lax.axis_index("fast"), lax.axis_index("slow")
+    core = lax.rem(fast, 2)
+    rim = width // 2
     sums = of_halves((mine_ref, other_ref), core, slow, modes * width)
     probe = updated_probe(probe_ref, sums, total, width, modes)
     probe_out_ref[0] = probe[0].reshape(modes, width, width)
@@ -415,12 +419,6 @@
         sizes + (fast, slow),
     )
     put_quarters(probe_grad, descan_grad, own_ref, beside_ref, send_ref, core, lax.rem(slow, 2), width, modes)
-    base_ref[...] = (
-        object_ref[:, rim : rim + tile_rows, :tile_cols]
-        - OBJECT_STEP * gradient_ref[:, rim : rim + tile_rows, :tile_cols]
-    )
-    up_ref[...] = gradient_ref[:, :rim, :tile_cols]
-    down_ref[...] = gradient_ref[:, rim + tile_rows :, :tile_cols]
     real, imag = gradient_ref[0, :, tile_cols:], gradient_ref[1, :, tile_cols:]
     low = lane_of(real.shape) < rim
     to_right = jnp.where(low, real, pltpu.roll(imag, rim, 1))
@@ -438,16 +436,15 @@
     return first, last
 
 
-def last_rows_kernel(sizes, odd, up_ref, down_ref, columns, mine_ref, *rest):
+def last_rows_kernel(sizes, odd, gradient_ref, columns, mine_ref, *rest):
     tile_rows, tile_cols, width, modes, count, n_fast, n_slow = sizes
     rim = width // 2
     out_ref = rest[-1]
     if odd:
         arrived_ref, sum_ref, out_ref = rest
         sum_ref[...] = mine_ref[...] + arrived_ref[...]
-    following = toward_next(odd)
-    at = pl.multiple_of(jnp.where(following, rim + tile_rows, 0), 8)
-    out_ref[...] = jnp.where(following, down_ref[...], up_ref[...])
+    at = pl.multiple_of(jnp.where(toward_next(odd), rim + tile_rows, 0), 8)
+    out_ref[...] = gradient_ref[:, pl.ds(at, rim), :tile_cols]
     first, last = edge_blocks(lax.axis_index("slow"), columns, pl.ds(at, rim), width)
     for part in range(2):
         out_ref[part, :, :width] += first[part]
@@ -460,10 +457,11 @@
     rest[-1][rows:] = beside_ref[...]
 
 
-def object_kernel(sizes, base_ref, columns, rows_even_ref, rows_odd_ref, out_ref):
-    tile_rows, tile_cols, width, modes, count, n_fast, n_slow = sizes
-    rim = width // 2
-    out_ref[...] = base_ref[...]
+def object_kernel(sizes, object_ref, gradient_ref, columns, rows_even_ref, rows_odd_ref, out_ref):
+    tile_rows, tile_cols, width, modes, count, n_fast, n_slow = sizes
+    rim = width // 2
+    inner = (slice(None), slice(rim, rim + tile_rows), slice(0, tile_cols))
+    out_ref[...] = object_ref[inner] - OBJECT_STEP * gradient_ref[inner]
     first, last = edge_blocks(lax.axis_index("slow"), columns, slice(rim, rim + tile_rows), width)
     for part in range(2):
         out_ref[part, :, :width] -= OBJECT_STEP * first[part]
@@ -568,7 +566,7 @@
         functools.partial(pack_kernel, sizes),
         [(2, ext_rows, ext_cols)] + [(2, rim, tile_cols)] * 2
         + [(tile_rows, width), (rim, width), (rim, width)] * swaps, [],
-        object_field, hbm=True, semaphores=[()], work=WORK,
+        object_field, work=WORK,
     )
     halos = []
     rows_odd = exchanged(rows_odd, 1)
@@ -606,20 +604,25 @@
     mine = fast_ended(mine)
     mine, other = sum_ended(mine)
 
-    def second(starts_ref, descan_ref, extended_ref, gradient_ref, probe_ref, measured_ref, tables_ref, *rest):
-        base_ref, up_ref, down_ref, *rest_out = rest[swaps + 4 :]
-        second_kernel(sizes, total, starts_ref, descan_ref, extended_ref, gradient_ref, probe_ref,
-                      measured_ref, tables_ref, pairwise(rest[:swaps]), *rest[swaps : swaps + 4],
-                      base_ref, up_ref, down_ref, rest_out[:swaps], *rest_out[swaps:])
+    def update(extended_ref, gradient_ref, *rest):
+        update_kernel(sizes, extended_ref, gradient_ref, pairwise(rest[:swaps]), *rest[swaps:])
+
+    (extended,) = call(
+        update, [(2, ext_rows, ext_cols)], [], extended, gradient, *columns, rows_even, rows_odd, aliases={0: 0},
+    )
+
+    def second(starts_ref, descan_ref, object_ref, probe_ref, measured_ref, tables_ref, mine_ref, other_ref, *rest):
+        gradient_ref, *rest_out = rest
+        second_kernel(sizes, total, starts_ref, descan_ref, object_ref, probe_ref, measured_ref, tables_ref,
+                      mine_ref, other_ref, gradient_ref, rest_out[:swaps], *rest_out[swaps:])
 
     part = (half_rows // 2 + EXTRA, width)
-    base, up, down, *strips, mine, beside, send, probes, descan_rows = call(
+    gradient, *strips, mine, beside, send, probes, descan_rows = call(
         second,
-        [(2, tile_rows, tile_cols)] + [(2, rim, tile_cols)] * 2 + [(ext_rows, width)] * swaps + [part, part, (2, *part)]
+        [(2, ext_rows, ext_cols)] + [(ext_rows, width)] * swaps + [part, part, (2, *part)]
         + [probe_modes.shape, (EXTRA, width)],
-        [(2, ext_rows, ext_cols)] * 2 + scratch,
-        starts, descan, extended, gradient, probe_modes, amplitudes, tables,
-        *columns, rows_even, rows_odd, mine, other,
+        scratch,
+        starts, descan, extended, probe_modes, amplitudes, tables, mine, other,
         smem=1,
     )
     columns = [exchanged(strip, None, k) for k, strip in enumerate(strips)]
@@ -627,12 +630,12 @@
     mine = mine + core_part[0] + swapped(beside + core_part[1], "slow", 1)
     steps = [("fast", bit) for bit in fast_bits] + [("slow", bit) for bit in slow_bits[1:]]
 
-    def last_rows(odd, up_ref, down_ref, *rest):
-        last_rows_kernel(sizes, odd, up_ref, down_ref, pairwise(rest[:swaps]), *rest[swaps:])
+    def last_rows(odd, gradient_ref, *rest):
+        last_rows_kernel(sizes, odd, gradient_ref, pairwise(rest[:swaps]), *rest[swaps:])
 
     arrived = swapped(mine, *steps[0]) if regular else jnp.zeros_like(mine)
     mine, rows_odd = call(
-        functools.partial(last_rows, True), [part, (2, rim, tile_cols)], [], up, down, *columns, mine, arrived,
+        functools.partial(last_rows, True), [part, (2, rim, tile_cols)], [], gradient, *columns, mine, arrived,
     )
     rows_odd = exchanged(rows_odd, 1)
     if regular:
@@ -643,7 +646,7 @@
         every = lax.psum(jnp.where(jnp.arange(4)[:, None, None] == place, mine, 0.0), AXES)
         mine = lax.dynamic_index_in_dim(every, place, keepdims=False)
     (rows_even,) = call(
-        functools.partial(last_rows, False), [(2, rim, tile_cols)], [], up, down, *columns, mine,
+        functools.partial(last_rows, False), [(2, rim, tile_cols)], [], gradient, *columns, mine,
     )
     rows_even = exchanged(rows_even, 0)
     own = mine[: half_rows // 2]
@@ -651,11 +654,11 @@
     (both,) = call(join_kernel, [(half_rows, width)], [], own, beside, rows_even, rows_odd)
     other = swapped(both, "fast", 1)
 
-    def objects_of(base_ref, *rest):
-        object_kernel(sizes, base_ref, pairwise(rest[:swaps]), *rest[swaps:])
+    def objects_of(object_ref, gradient_ref, *rest):
+        object_kernel(sizes, object_ref, gradient_ref, pairwise(rest[:swaps]), *rest[swaps:])
 
     (objects,) = call(
-        objects_of, [(2, tile_rows, tile_cols)], [], base, *columns, rows_even, rows_odd,
+        objects_of, [(2, tile_rows, tile_cols)], [], extended, gradient, *columns, rows_even, rows_odd,
     )
 
     def probe_of(probe_ref, descan_ref, q0, q1, q2, *outs):

time: 77.4 us -> 79.9 us (1.032)
  Pallas kernels: 9.25 us -> 11.7 us
    pallas_call x10 -> x11, Pallas kernels: 9.25 us -> 11.7 us  [call(): pl.pallas_call(kernel, out_shape=[out if isinstance(out, jax.ShapeDtypeSt...]
where the time goes in v4:
time: 79.9 us; the launch traced here: 78.9 us
  starting transfers between devices  35.6 us (45%)
  waiting for transfers between devices  29.5 us (37%)
  Pallas kernels  11.7 us (15%)
  local copies, waits for them, and re-layouts  1.15 us (1%)
  between operations  0.89 us (1%)
    ppermute x11, starting transfers between devices, exchanged(): return lax.ppermute(value, AXES, pairs)  23.6 us
    ppermute x13, waiting for transfers between devices, swapped(): lax.ppermute(value, axis, [(i, i ^ bit) for i in range(lax.axis_size(axis...  20.3 us
    ppermute x13, starting transfers between devices, swapped(): lax.ppermute(value, axis, [(i, i ^ bit) for i in range(lax.axis_size(axis...  12 us
    pallas_call x11, Pallas kernels, call(): pl.pallas_call(kernel, out_shape=[out if isinstance(out, jax.ShapeDtypeSt...  11.7 us
    ppermute x11, waiting for transfers between devices, exchanged(): return lax.ppermute(value, AXES, pairs)  9.23 us
  transfers between devices with their start and end apart: 24, of which 13 were waited for; matrix products, arithmetic and copies ran while one was open for 0% of the time, Pallas kernels for 2%

profile of v4, /device:TPU:7, one launch (start us, length us, event | category | flops | bytes accessed | tf_op | source)
XLA Modules:
  0.0 78.9 jit_solution(6854110525539874845)
XLA Ops:
  0.7 1.1 %copy-done.5 = f32[2,256,256]{2,1,0:T(8,128)S(1)} copy-done((f32[2,256,256]{2,1,0:T(8,128)S(1)}, f32[2,256,256]{2,1,0:T(8,128)}, u32[]{:S(2)}) %copy-start.5) | copy-done | bytes 524312
  2.7 3.0 %collective-permute-start.1 = (f32[2,64,256]{2,1,0:T(8,128)S(1)}, f32[2,64,256]{2,1,0:T(8,128)S(1)}, u32[]{:S(2)}, u32[]{:S(2)}) collective-permute-start(f32[2,64,256]{2,1,0:T(8,128)S(1)} %get-tuple-element.27), channel_id=1, source_target_pairs={{2,4},{3,5},{4,2},{5,3},{6,8},{7,9},{8,6},{9,7},{10,12},{11,13},{1... | collective-permute-start | bytes 393224 | tf_op jit(solution)/shard_map/ppermute | solution.py:532
  6.9 3.8 %collective-permute-start.4 = (f32[64,128]{1,0:T(8,128)S(1)}, f32[64,128]{1,0:T(8,128)S(1)}, u32[]{:S(2)}, u32[]{:S(2)}) collective-permute-start(f32[64,128]{1,0:T(8,128)S(1)} %get-tuple-element.30), channel_id=1, source_target_pairs={{2,5},{3,4},{4,3},{5,2},{6,9},{7,8},{8,7},{9,6},{10,13},{11,12},{1... | collective-permute-start | bytes 98312 | tf_op jit(solution)/shard_map/ppermute | solution.py:532
  10.7 1.2 %collective-permute-done.3.rest_3_ = f32[64,128]{1,0:T(8,128)S(1)} collective-permute-done((f32[64,128]{1,0:T(8,128)S(1)}, f32[64,128]{1,0:T(8,128)S(1)}, u32[]{:S(2)}, u32[]{:S(2)}) %collective-permute-start.3) | collective-permute-done | bytes 32800 | tf_op jit(solution)/shard_map/ppermute | solution.py:532
  11.9 2.0 %collective-permute-done.4.rest_4_ = f32[64,128]{1,0:T(8,128)S(1)} collective-permute-done((f32[64,128]{1,0:T(8,128)S(1)}, f32[64,128]{1,0:T(8,128)S(1)}, u32[]{:S(2)}, u32[]{:S(2)}) %collective-permute-start.4) | collective-permute-done | bytes 32800 | tf_op jit(solution)/shard_map/ppermute | solution.py:532
  14.0 4.4 %shard_map.86 = (f32[2,384,384]{2,1,0:T(8,128)S(1)}, f32[2,384,384]{2,1,0:T(8,128)S(1)}, f32[2,384,128]{2,1,0:T(8,128)S(1)}, f32[264,128]{1,0:T(8,128)S(1)}, f32[264,128]{1,0:T(8,128)S(1)}) custom-call(s32[2,1,2]{2,1,0:T(1,128)S(1)} %bitcast.13, f32[2,3]{1,0:T(2,128)S(1)} %copy-done.4, ...), custom_call_target="tpu_custom_call", output_to_operand_aliasing={{0}: (2, {})} | custom-call | tf_op jit(solution)/shard_map/pallas_call | solution.py:491
  19.9 5.0 %collective-permute-done.7 = f32[264,128]{1,0:T(8,128)S(1)} collective-permute-done((f32[264,128]{1,0:T(8,128)S(1)}, f32[264,128]{1,0:T(8,128)S(1)}, u32[]{:S(2)}, u32[]{:S(2)}) %collective-permute-start.7) | collective-permute-done | bytes 135200 | tf_op jit(solution)/shard_map/ppermute | solution.py:535
  25.0 1.4 %collective-permute-start.8 = (f32[264,128]{1,0:T(8,128)S(1)}, f32[264,128]{1,0:T(8,128)S(1)}, u32[]{:S(2)}, u32[]{:S(2)}) collective-permute-start(f32[264,128]{1,0:T(8,128)S(1)} %add.31), channel_id=1, source_target_pairs={{0,8},{2,10},{4,12},{6,14},{8,0},{10,2},{12,4},{14,6},{16,24},{18,... | collective-permute-start | bytes 405512 | tf_op jit(solution)/shard_map/ppermute | solution.py:535
  26.4 2.8 %collective-permute-done.8 = f32[264,128]{1,0:T(8,128)S(1)} collective-permute-done((f32[264,128]{1,0:T(8,128)S(1)}, f32[264,128]{1,0:T(8,128)S(1)}, u32[]{:S(2)}, u32[]{:S(2)}) %collective-permute-start.8) | collective-permute-done | bytes 135200 | tf_op jit(solution)/shard_map/ppermute | solution.py:535
  29.2 2.4 %collective-permute-start.11 = (f32[264,128]{1,0:T(8,128)S(1)}, f32[264,128]{1,0:T(8,128)S(1)}, u32[]{:S(2)}, u32[]{:S(2)}) collective-permute-start(f32[264,128]{1,0:T(8,128)S(1)} %add.32.rest_1_), channel_id=1, source_target_pairs={{0,16},{2,18},{4,20},{6,22},{8,24},{10,26},{12,28},{14,30},{16,0},... | collective-permute-start | bytes 405512 | tf_op jit(solution)/shard_map/ppermute | solution.py:535
  31.7 2.2 %collective-permute-start.9 = (f32[128,640]{1,0:T(8,128)S(1)}, f32[128,640]{1,0:T(8,128)S(1)}, u32[]{:S(2)}, u32[]{:S(2)}) collective-permute-start(f32[128,640]{1,0:T(8,128)S(1)} %shard_map.87), channel_id=1, source_target_pairs={{0,2},{1,3},{2,0},{3,1},{4,6},{5,7},{6,4},{7,5},{8,10},{9,11},{10,... | collective-permute-start | bytes 983048 | tf_op jit(solution)/shard_map/ppermute | solution.py:532
  34.0 3.5 %collective-permute-start.10 = (f32[128,640]{1,0:T(8,128)S(1)}, f32[128,640]{1,0:T(8,128)S(1)}, u32[]{:S(2)}, u32[]{:S(2)}) collective-permute-start(f32[128,640]{1,0:T(8,128)S(1)} %shard_map.88), channel_id=1, source_target_pairs={{2,4},{3,5},{4,2},{5,3},{6,8},{7,9},{8,6},{9,7},{10,12},{11,13},{1... | collective-permute-start | bytes 983048 | tf_op jit(solution)/shard_map/ppermute | solution.py:532
  38.2 3.7 %collective-permute-done.12 = f32[264,128]{1,0:T(8,128)S(1)} collective-permute-done((f32[264,128]{1,0:T(8,128)S(1)}, f32[264,128]{1,0:T(8,128)S(1)}, u32[]{:S(2)}, u32[]{:S(2)}) %collective-permute-start.12) | collective-permute-done | bytes 135200 | tf_op jit(solution)/shard_map/ppermute | solution.py:535
  41.9 2.4 %collective-permute-start.13 = (f32[256,128]{1,0:T(8,128)S(1)}, f32[256,128]{1,0:T(8,128)S(1)}, u32[]{:S(2)}, u32[]{:S(2)}) collective-permute-start(f32[256,128]{1,0:T(8,128)S(1)} %slice.16), channel_id=1, source_target_pairs={{0,2},{2,0},{4,6},{6,4},{8,10},{10,8},{12,14},{14,12},{16,18},{18,... | collective-permute-start | bytes 393224 | tf_op jit(solution)/shard_map/ppermute | solution.py:535
  45.3 4.4 %shard_map.90 = (f32[2,384,384]{2,1,0:T(8,128)S(1)}, f32[384,128]{1,0:T(8,128)S(1)}, f32[136,128]{1,0:T(8,128)S(1)}, f32[136,128]{1,0:T(8,128)S(1)}, f32[2,136,1...) custom-call(s32[2,1,2]{2,1,0:T(1,128)S(1)} %bitcast.14, f32[2,3]{1,0:T(2,128)S(1)} %copy-done.4, ...), custom_call_target="tpu_custom_call" | custom-call | tf_op jit(solution)/shard_map/pallas_call | solution.py:491
  49.7 1.2 %collective-permute-start.15 = (f32[2,136,128]{2,1,0:T(8,128)S(1)}, f32[2,136,128]{2,1,0:T(8,128)S(1)}, u32[]{:S(2)}, u32[]{:S(2)}) collective-permute-start(f32[2,136,128]{2,1,0:T(8,128)S(1)} %get-tuple-element.39), channel_id=1, source_target_pairs={{0,2},{2,0},{4,6},{6,4},{8,10},{10,8},{12,14},{14,12},{16,18},{18,... | collective-permute-start | bytes 417800 | tf_op jit(solution)/shard_map/ppermute | solution.py:535
  52.3 1.1 %collective-permute-start.14 = (f32[384,128]{1,0:T(8,128)S(1)}, f32[384,128]{1,0:T(8,128)S(1)}, u32[]{:S(2)}, u32[]{:S(2)}) collective-permute-start(f32[384,128]{1,0:T(8,128)S(1)} %get-tuple-element.37), channel_id=1, source_target_pairs={{0,1},{1,0},{2,3},{3,2},{4,5},{5,4},{6,7},{7,6},{8,9},{9,8},{10,11... | collective-permute-start | bytes 589832 | tf_op jit(solution)/shard_map/ppermute | solution.py:532
  53.4 1.7 %collective-permute-done.16 = f32[136,128]{1,0:T(8,128)S(1)} collective-permute-done((f32[136,128]{1,0:T(8,128)S(1)}, f32[136,128]{1,0:T(8,128)S(1)}, u32[]{:S(2)}, u32[]{:S(2)}) %collective-permute-start.16) | collective-permute-done | bytes 69664 | tf_op jit(solution)/shard_map/ppermute | solution.py:535
  55.2 4.4 %collective-permute-done.14.rest_0_ = f32[384,128]{1,0:T(8,128)S(1)} collective-permute-done((f32[384,128]{1,0:T(8,128)S(1)}, f32[384,128]{1,0:T(8,128)S(1)}, u32[]{:S(2)}, u32[]{:S(2)}) %collective-permute-start.14) | collective-permute-done | bytes 196640 | tf_op jit(solution)/shard_map/ppermute | solution.py:532
  60.4 2.5 %collective-permute-done.18 = f32[136,128]{1,0:T(8,128)S(1)} collective-permute-done((f32[136,128]{1,0:T(8,128)S(1)}, f32[136,128]{1,0:T(8,128)S(1)}, u32[]{:S(2)}, u32[]{:S(2)}) %collective-permute-start.18) | collective-permute-done | bytes 69664 | tf_op jit(solution)/shard_map/ppermute | solution.py:535
  62.9 1.8 %collective-permute-start.19 = (f32[136,128]{1,0:T(8,128)S(1)}, f32[136,128]{1,0:T(8,128)S(1)}, u32[]{:S(2)}, u32[]{:S(2)}) collective-permute-start(f32[136,128]{1,0:T(8,128)S(1)} %add.38), channel_id=1, source_target_pairs={{0,16},{2,18},{4,20},{6,22},{8,24},{10,26},{12,28},{14,30},{16,0},... | collective-permute-start | bytes 208904 | tf_op jit(solution)/shard_map/ppermute | solution.py:535
  64.7 6.7 %collective-permute-start.21 = (f32[2,64,256]{2,1,0:T(8,128)S(1)}, f32[2,64,256]{2,1,0:T(8,128)S(1)}, u32[]{:S(2)}, u32[]{:S(2)}) collective-permute-start(f32[2,64,256]{2,1,0:T(8,128)S(1)} %get-tuple-element.42), channel_id=1, source_target_pairs={{2,4},{3,5},{4,2},{5,3},{6,8},{7,9},{8,6},{9,7},{10,12},{11,13},{1... | collective-permute-start | bytes 393224 | tf_op jit(solution)/shard_map/ppermute | solution.py:532
  72.4 1.6 %collective-permute-done.21.rest_2_.rest_1_ = f32[2,64,256]{2,1,0:T(8,128)S(1)} collective-permute-done((f32[2,64,256]{2,1,0:T(8,128)S(1)}, f32[2,64,256]{2,1,0:T(8,128)S(1)}, u32[]{:S(2)}, u32[]{:S(2)}) %collective-permute-start.21) | collective-permute-done | bytes 131104 | tf_op jit(solution)/shard_map/ppermute | solution.py:532
  74.1 2.0 %collective-permute-done.22.beside_ref.q1 = f32[128,128]{1,0:T(8,128)S(1)} collective-permute-done((f32[128,128]{1,0:T(8,128)S(1)}, f32[128,128]{1,0:T(8,128)S(1)}, u32[]{:S(2)}, u32[]{:S(2)}) %collective-permute-start.22) | collective-permute-done | bytes 65568 | tf_op jit(solution)/shard_map/ppermute | solution.py:535
  (58 shorter events, 11.7 us)
Async XLA Ops:
  1.9 12.0 %collective-permute-start = (f32[2,64,256]{2,1,0:T(8,128)S(1)}, f32[2,64,256]{2,1,0:T(8,128)S(1)}, u32[]{:S(2)}, u32[]{:S(2)}) collective-permute-start(f32[2,64,256]{2,1,0:T(8,128)S(1)} %get-tuple-element.26), channel_id=1, source_target_pairs={{0,2},{1,3},{2,0},{3,1},{4,6},{5,7},{6,4},{7,5},{8,10},{9,11},{10,... | collective-permute-start | bytes 393224 | tf_op jit(solution)/shard_map/ppermute | solution.py:532
  2.7 11.2 %collective-permute-start.1 = (f32[2,64,256]{2,1,0:T(8,128)S(1)}, f32[2,64,256]{2,1,0:T(8,128)S(1)}, u32[]{:S(2)}, u32[]{:S(2)}) collective-permute-start(f32[2,64,256]{2,1,0:T(8,128)S(1)} %get-tuple-element.27), channel_id=1, source_target_pairs={{2,4},{3,5},{4,2},{5,3},{6,8},{7,9},{8,6},{9,7},{10,12},{11,13},{1... | collective-permute-start | bytes 393224 | tf_op jit(solution)/shard_map/ppermute | solution.py:532
  5.7 8.2 %collective-permute-start.2 = (f32[256,128]{1,0:T(8,128)S(1)}, f32[256,128]{1,0:T(8,128)S(1)}, u32[]{:S(2)}, u32[]{:S(2)}) collective-permute-start(f32[256,128]{1,0:T(8,128)S(1)} %get-tuple-element.28), channel_id=1, source_target_pairs={{0,1},{1,0},{2,3},{3,2},{4,5},{5,4},{6,7},{7,6},{8,9},{9,8},{10,11... | collective-permute-start | bytes 393224 | tf_op jit(solution)/shard_map/ppermute | solution.py:532
  6.1 5.8 %collective-permute-start.3 = (f32[64,128]{1,0:T(8,128)S(1)}, f32[64,128]{1,0:T(8,128)S(1)}, u32[]{:S(2)}, u32[]{:S(2)}) collective-permute-start(f32[64,128]{1,0:T(8,128)S(1)} %get-tuple-element.29), channel_id=1, source_target_pairs={{0,3},{1,2},{2,1},{3,0},{4,7},{5,6},{6,5},{7,4},{8,11},{9,10},{10,... | collective-permute-start | bytes 98312 | tf_op jit(solution)/shard_map/ppermute | solution.py:532
  6.9 7.0 %collective-permute-start.4 = (f32[64,128]{1,0:T(8,128)S(1)}, f32[64,128]{1,0:T(8,128)S(1)}, u32[]{:S(2)}, u32[]{:S(2)}) collective-permute-start(f32[64,128]{1,0:T(8,128)S(1)} %get-tuple-element.30), channel_id=1, source_target_pairs={{2,5},{3,4},{4,3},{5,2},{6,9},{7,8},{8,7},{9,6},{10,13},{11,12},{1... | collective-permute-start | bytes 98312 | tf_op jit(solution)/shard_map/ppermute | solution.py:532
  18.4 1.4 %collective-permute-start.6 = (f32[264,128]{1,0:T(8,128)S(1)}, f32[264,128]{1,0:T(8,128)S(1)}, u32[]{:S(2)}, u32[]{:S(2)}) collective-permute-start(f32[264,128]{1,0:T(8,128)S(1)} %get-tuple-element.35), channel_id=1, source_target_pairs={{0,2},{2,0},{4,6},{6,4},{8,10},{10,8},{12,14},{14,12},{16,18},{18,... | collective-permute-start | bytes 405512 | tf_op jit(solution)/shard_map/ppermute | solution.py:535
  18.5 13.1 %collective-permute-start.5 = (f32[2,384,128]{2,1,0:T(8,128)S(1)}, f32[2,384,128]{2,1,0:T(8,128)S(1)}, u32[]{:S(2)}, u32[]{:S(2)}) collective-permute-start(f32[2,384,128]{2,1,0:T(8,128)S(1)} %get-tuple-element.33), channel_id=1, source_target_pairs={{0,1},{1,0},{2,3},{3,2},{4,5},{5,4},{6,7},{7,6},{8,9},{9,8},{10,11... | collective-permute-start | bytes 1179656 | tf_op jit(solution)/shard_map/ppermute | solution.py:532
  19.9 5.1 %collective-permute-start.7 = (f32[264,128]{1,0:T(8,128)S(1)}, f32[264,128]{1,0:T(8,128)S(1)}, u32[]{:S(2)}, u32[]{:S(2)}) collective-permute-start(f32[264,128]{1,0:T(8,128)S(1)} %add.30), channel_id=1, source_target_pairs={{0,4},{2,6},{4,0},{6,2},{8,12},{10,14},{12,8},{14,10},{16,20},{18,... | collective-permute-start | bytes 405512 | tf_op jit(solution)/shard_map/ppermute | solution.py:535
  25.0 4.2 %collective-permute-start.8 = (f32[264,128]{1,0:T(8,128)S(1)}, f32[264,128]{1,0:T(8,128)S(1)}, u32[]{:S(2)}, u32[]{:S(2)}) collective-permute-start(f32[264,128]{1,0:T(8,128)S(1)} %add.31), channel_id=1, source_target_pairs={{0,8},{2,10},{4,12},{6,14},{8,0},{10,2},{12,4},{14,6},{16,24},{18,... | collective-permute-start | bytes 405512 | tf_op jit(solution)/shard_map/ppermute | solution.py:535
  29.2 8.3 %collective-permute-start.11 = (f32[264,128]{1,0:T(8,128)S(1)}, f32[264,128]{1,0:T(8,128)S(1)}, u32[]{:S(2)}, u32[]{:S(2)}) collective-permute-start(f32[264,128]{1,0:T(8,128)S(1)} %add.32.rest_1_), channel_id=1, source_target_pairs={{0,16},{2,18},{4,20},{6,22},{8,24},{10,26},{12,28},{14,30},{16,0},... | collective-permute-start | bytes 405512 | tf_op jit(solution)/shard_map/ppermute | solution.py:535
  31.7 12.6 %collective-permute-start.9 = (f32[128,640]{1,0:T(8,128)S(1)}, f32[128,640]{1,0:T(8,128)S(1)}, u32[]{:S(2)}, u32[]{:S(2)}) collective-permute-start(f32[128,640]{1,0:T(8,128)S(1)} %shard_map.87), channel_id=1, source_target_pairs={{0,2},{1,3},{2,0},{3,1},{4,6},{5,7},{6,4},{7,5},{8,10},{9,11},{10,... | collective-permute-start | bytes 983048 | tf_op jit(solution)/shard_map/ppermute | solution.py:532
  34.0 10.3 %collective-permute-start.10 = (f32[128,640]{1,0:T(8,128)S(1)}, f32[128,640]{1,0:T(8,128)S(1)}, u32[]{:S(2)}, u32[]{:S(2)}) collective-permute-start(f32[128,640]{1,0:T(8,128)S(1)} %shard_map.88), channel_id=1, source_target_pairs={{2,4},{3,5},{4,2},{5,3},{6,8},{7,9},{8,6},{9,7},{10,12},{11,13},{1... | collective-permute-start | bytes 983048 | tf_op jit(solution)/shard_map/ppermute | solution.py:532
  37.6 4.2 %collective-permute-start.12 = (f32[264,128]{1,0:T(8,128)S(1)}, f32[264,128]{1,0:T(8,128)S(1)}, u32[]{:S(2)}, u32[]{:S(2)}) collective-permute-start(f32[264,128]{1,0:T(8,128)S(1)} %add.33), channel_id=1, source_target_pairs={{0,1},{1,0},{2,3},{3,2},{4,5},{5,4},{6,7},{7,6},{8,9},{9,8},{10,11... | collective-permute-start | bytes 405512 | tf_op jit(solution)/shard_map/ppermute | solution.py:535
  41.9 3.4 %collective-permute-start.13 = (f32[256,128]{1,0:T(8,128)S(1)}, f32[256,128]{1,0:T(8,128)S(1)}, u32[]{:S(2)}, u32[]{:S(2)}) collective-permute-start(f32[256,128]{1,0:T(8,128)S(1)} %slice.16), channel_id=1, source_target_pairs={{0,2},{2,0},{4,6},{6,4},{8,10},{10,8},{12,14},{14,12},{16,18},{18,... | collective-permute-start | bytes 393224 | tf_op jit(solution)/shard_map/ppermute | solution.py:535
  49.7 2.2 %collective-permute-start.15 = (f32[2,136,128]{2,1,0:T(8,128)S(1)}, f32[2,136,128]{2,1,0:T(8,128)S(1)}, u32[]{:S(2)}, u32[]{:S(2)}) collective-permute-start(f32[2,136,128]{2,1,0:T(8,128)S(1)} %get-tuple-element.39), channel_id=1, source_target_pairs={{0,2},{2,0},{4,6},{6,4},{8,10},{10,8},{12,14},{14,12},{16,18},{18,... | collective-permute-start | bytes 417800 | tf_op jit(solution)/shard_map/ppermute | solution.py:535
  51.9 3.2 %collective-permute-start.16 = (f32[136,128]{1,0:T(8,128)S(1)}, f32[136,128]{1,0:T(8,128)S(1)}, u32[]{:S(2)}, u32[]{:S(2)}) collective-permute-start(f32[136,128]{1,0:T(8,128)S(1)} %fusion), channel_id=1, source_target_pairs={{0,1},{1,0},{2,3},{3,2},{4,5},{5,4},{6,7},{7,6},{8,9},{9,8},{10,11... | collective-permute-start | bytes 208904 | tf_op jit(solution)/shard_map/ppermute | solution.py:535
  52.3 7.2 %collective-permute-start.14 = (f32[384,128]{1,0:T(8,128)S(1)}, f32[384,128]{1,0:T(8,128)S(1)}, u32[]{:S(2)}, u32[]{:S(2)}) collective-permute-start(f32[384,128]{1,0:T(8,128)S(1)} %get-tuple-element.37), channel_id=1, source_target_pairs={{0,1},{1,0},{2,3},{3,2},{4,5},{5,4},{6,7},{7,6},{8,9},{9,8},{10,11... | collective-permute-start | bytes 589832 | tf_op jit(solution)/shard_map/ppermute | solution.py:532
  55.1 4.4 %collective-permute-start.17 = (f32[136,128]{1,0:T(8,128)S(1)}, f32[136,128]{1,0:T(8,128)S(1)}, u32[]{:S(2)}, u32[]{:S(2)}) collective-permute-start(f32[136,128]{1,0:T(8,128)S(1)} %fusion.2.rest_1_), channel_id=1, source_target_pairs={{0,4},{2,6},{4,0},{6,2},{8,12},{10,14},{12,8},{14,10},{16,20},{18,... | collective-permute-start | bytes 208904 | tf_op jit(solution)/shard_map/ppermute | solution.py:535
  59.7 3.2 %collective-permute-start.18 = (f32[136,128]{1,0:T(8,128)S(1)}, f32[136,128]{1,0:T(8,128)S(1)}, u32[]{:S(2)}, u32[]{:S(2)}) collective-permute-start(f32[136,128]{1,0:T(8,128)S(1)} %get-tuple-element.41), channel_id=1, source_target_pairs={{0,8},{2,10},{4,12},{6,14},{8,0},{10,2},{12,4},{14,6},{16,24},{18,... | collective-permute-start | bytes 208904 | tf_op jit(solution)/shard_map/ppermute | solution.py:535
  62.9 8.4 %collective-permute-start.19 = (f32[136,128]{1,0:T(8,128)S(1)}, f32[136,128]{1,0:T(8,128)S(1)}, u32[]{:S(2)}, u32[]{:S(2)}) collective-permute-start(f32[136,128]{1,0:T(8,128)S(1)} %add.38), channel_id=1, source_target_pairs={{0,16},{2,18},{4,20},{6,22},{8,24},{10,26},{12,28},{14,30},{16,0},... | collective-permute-start | bytes 208904 | tf_op jit(solution)/shard_map/ppermute | solution.py:535
  64.7 9.4 %collective-permute-start.21 = (f32[2,64,256]{2,1,0:T(8,128)S(1)}, f32[2,64,256]{2,1,0:T(8,128)S(1)}, u32[]{:S(2)}, u32[]{:S(2)}) collective-permute-start(f32[2,64,256]{2,1,0:T(8,128)S(1)} %get-tuple-element.42), channel_id=1, source_target_pairs={{2,4},{3,5},{4,2},{5,3},{6,8},{7,9},{8,6},{9,7},{10,12},{11,13},{1... | collective-permute-start | bytes 393224 | tf_op jit(solution)/shard_map/ppermute | solution.py:532
  71.4 4.6 %collective-permute-start.20 = (f32[2,64,256]{2,1,0:T(8,128)S(1)}, f32[2,64,256]{2,1,0:T(8,128)S(1)}, u32[]{:S(2)}, u32[]{:S(2)}) collective-permute-start(f32[2,64,256]{2,1,0:T(8,128)S(1)} %shard_map.92), channel_id=1, source_target_pairs={{0,2},{1,3},{2,0},{3,1},{4,6},{5,7},{6,4},{7,5},{8,10},{9,11},{10,... | collective-permute-start | bytes 393224 | tf_op jit(solution)/shard_map/ppermute | solution.py:532
  72.4 3.7 %collective-permute-start.22 = (f32[128,128]{1,0:T(8,128)S(1)}, f32[128,128]{1,0:T(8,128)S(1)}, u32[]{:S(2)}, u32[]{:S(2)}) collective-permute-start(f32[128,128]{1,0:T(8,128)S(1)} %slice.19.own_ref), channel_id=1, source_target_pairs={{0,1},{1,0},{2,3},{3,2},{4,5},{5,4},{6,7},{7,6},{8,9},{9,8},{10,11... | collective-permute-start | bytes 196616 | tf_op jit(solution)/shard_map/ppermute | solution.py:535
  76.1 1.9 %collective-permute-start.23 = (f32[256,128]{1,0:T(8,128)S(1)}, f32[256,128]{1,0:T(8,128)S(1)}, u32[]{:S(2)}, u32[]{:S(2)}) collective-permute-start(f32[256,128]{1,0:T(8,128)S(1)} %shard_map.94), channel_id=1, source_target_pairs={{0,2},{2,0},{4,6},{6,4},{8,10},{10,8},{12,14},{14,12},{16,18},{18,... | collective-permute-start | bytes 393224 | tf_op jit(solution)/shard_map/ppermute | solution.py:535
  (6 other events, 66.5 us)

commit v5 on v4

--- a/solution.py
+++ b/solution.py
@@ -15,6 +15,7 @@
 FLOOR_LEVEL = 0.25
 PROBE_POWER = 0.5
 EXTRA = 8
+FIRST, SECOND = 3, 2
 AXES = ("fast", "slow")
 F32 = jnp.float32
 BF16 = jnp.bfloat16
@@ -52,7 +53,10 @@
 
 
 def product(left, right):
-    (a, b, c), (d, e, f) = left, right
+    (a, b, *c), (d, e, *f) = left, right
+    if not c or not f:
+        return dot(a, d) + (dot(a, e) + dot(b, d))
+    (c,), (f,) = c, f
     return dot(a, d) + (dot(a, e) + dot(b, d) + (dot(b, e) + dot(a, f) + dot(c, d)))
 
 
@@ -70,7 +74,7 @@
 
 
 def gradients(
-    object_ref, probe, descan_rows, starts, measured_ref, tables_ref, gradient_ref, wave_ref, far_ref, sizes
+    object_ref, probe, descan_rows, starts, measured_ref, tables_ref, gradient_ref, wave_ref, far_ref, sizes, parts
 ):
     tile_rows, tile_cols, width, modes, count, n_fast, n_slow, fast, slow = sizes
     ext_cols = tile_cols + width
@@ -79,7 +83,7 @@
     lane_row = lane_of((1, width)).astype(F32)
     centred = (lane_row - width // 2) / width
     tables = [tables_ref[k] for k in range(6)]
-    forward, backward = tables[:3], tables[3:]
+    forward, backward = tables[:parts], tables[3 : 3 + parts]
 
     fractions = []
     phases = []
@@ -316,7 +320,7 @@
     probe = tuple(probe_ref[part].reshape(modes * width, width) for part in range(2))
     probe_grad, descan_grad = gradients(
         extended_ref, probe, descan_rows, starts, measured_ref, tables_ref, gradient_ref, wave_ref, far_ref,
-        sizes + (fast, slow),
+        sizes + (fast, slow), FIRST,
     )
     put_sums(probe_grad, descan_grad, keep_ref, send_ref, core, width, modes)
     halo = gradient_ref[:, :, tile_cols:]
@@ -416,7 +420,7 @@
     descan_out_ref[...] = jnp.concatenate(descan_rows + [jnp.zeros((EXTRA - 6, width), F32)], axis=0)
     probe_grad, descan_grad = gradients(
         object_ref, probe, descan_rows, starts, measured_ref, tables_ref, gradient_ref, wave_ref, far_ref,
-        sizes + (fast, slow),
+        sizes + (fast, slow), SECOND,
     )
     put_quarters(probe_grad, descan_grad, own_ref, beside_ref, send_ref, core, lax.rem(slow, 2), width, modes)
     real, imag = gradient_ref[0, :, tile_cols:], gradient_ref[1, :, tile_cols:]

time: 79.9 us -> 78.6 us (0.984)
  Pallas kernels: 11.7 us -> 10.4 us
    pallas_call x11, Pallas kernels: 11.7 us -> 10.4 us  [call(): pl.pallas_call(kernel, out_shape=[out if isinstance(out, jax.ShapeDtypeSt...]
where the time goes in v5:
time: 78.6 us; the launch traced here: 77.7 us
  starting transfers between devices  35.6 us (45%)
  waiting for transfers between devices  29.5 us (38%)
  Pallas kernels  10.4 us (13%)
  local copies, waits for them, and re-layouts  1.15 us (1%)
  between operations  0.89 us (1%)
    ppermute x11, starting transfers between devices, exchanged(): return lax.ppermute(value, AXES, pairs)  23.6 us
    ppermute x13, waiting for transfers between devices, swapped(): lax.ppermute(value, axis, [(i, i ^ bit) for i in range(lax.axis_size(axis...  20.3 us
    ppermute x13, starting transfers between devices, swapped(): lax.ppermute(value, axis, [(i, i ^ bit) for i in range(lax.axis_size(axis...  11.9 us
    pallas_call x11, Pallas kernels, call(): pl.pallas_call(kernel, out_shape=[out if isinstance(out, jax.ShapeDtypeSt...  10.4 us
    ppermute x11, waiting for transfers between devices, exchanged(): return lax.ppermute(value, AXES, pairs)  9.21 us
  transfers between devices with their start and end apart: 24, of which 13 were waited for; matrix products, arithmetic and copies ran while one was open for 0% of the time, Pallas kernels for 2%

profile of v5, /device:TPU:7, one launch (start us, length us, event | category | flops | bytes accessed | tf_op | source)
XLA Modules:
  0.0 77.7 jit_solution(6719959546135634924)
XLA Ops:
  0.7 1.1 %copy-done.5 = f32[2,256,256]{2,1,0:T(8,128)S(1)} copy-done((f32[2,256,256]{2,1,0:T(8,128)S(1)}, f32[2,256,256]{2,1,0:T(8,128)}, u32[]{:S(2)}) %copy-start.5) | copy-done | bytes 524312
  2.7 3.0 %collective-permute-start.1 = (f32[2,64,256]{2,1,0:T(8,128)S(1)}, f32[2,64,256]{2,1,0:T(8,128)S(1)}, u32[]{:S(2)}, u32[]{:S(2)}) collective-permute-start(f32[2,64,256]{2,1,0:T(8,128)S(1)} %get-tuple-element.27), channel_id=1, source_target_pairs={{2,4},{3,5},{4,2},{5,3},{6,8},{7,9},{8,6},{9,7},{10,12},{11,13},{1... | collective-permute-start | bytes 393224 | tf_op jit(solution)/shard_map/ppermute | solution.py:536
  6.9 3.8 %collective-permute-start.4 = (f32[64,128]{1,0:T(8,128)S(1)}, f32[64,128]{1,0:T(8,128)S(1)}, u32[]{:S(2)}, u32[]{:S(2)}) collective-permute-start(f32[64,128]{1,0:T(8,128)S(1)} %get-tuple-element.30), channel_id=1, source_target_pairs={{2,5},{3,4},{4,3},{5,2},{6,9},{7,8},{8,7},{9,6},{10,13},{11,12},{1... | collective-permute-start | bytes 98312 | tf_op jit(solution)/shard_map/ppermute | solution.py:536
  10.7 1.2 %collective-permute-done.3.rest_3_ = f32[64,128]{1,0:T(8,128)S(1)} collective-permute-done((f32[64,128]{1,0:T(8,128)S(1)}, f32[64,128]{1,0:T(8,128)S(1)}, u32[]{:S(2)}, u32[]{:S(2)}) %collective-permute-start.3) | collective-permute-done | bytes 32800 | tf_op jit(solution)/shard_map/ppermute | solution.py:536
  11.9 2.0 %collective-permute-done.4.rest_4_ = f32[64,128]{1,0:T(8,128)S(1)} collective-permute-done((f32[64,128]{1,0:T(8,128)S(1)}, f32[64,128]{1,0:T(8,128)S(1)}, u32[]{:S(2)}, u32[]{:S(2)}) %collective-permute-start.4) | collective-permute-done | bytes 32800 | tf_op jit(solution)/shard_map/ppermute | solution.py:536
  14.0 4.4 %shard_map.86 = (f32[2,384,384]{2,1,0:T(8,128)S(1)}, f32[2,384,384]{2,1,0:T(8,128)S(1)}, f32[2,384,128]{2,1,0:T(8,128)S(1)}, f32[264,128]{1,0:T(8,128)S(1)}, f32[264,128]{1,0:T(8,128)S(1)}) custom-call(s32[2,1,2]{2,1,0:T(1,128)S(1)} %bitcast.13, f32[2,3]{1,0:T(2,128)S(1)} %copy-done.4, ...), custom_call_target="tpu_custom_call", output_to_operand_aliasing={{0}: (2, {})} | custom-call | tf_op jit(solution)/shard_map/pallas_call | solution.py:495
  20.0 5.0 %collective-permute-done.7 = f32[264,128]{1,0:T(8,128)S(1)} collective-permute-done((f32[264,128]{1,0:T(8,128)S(1)}, f32[264,128]{1,0:T(8,128)S(1)}, u32[]{:S(2)}, u32[]{:S(2)}) %collective-permute-start.7) | collective-permute-done | bytes 135200 | tf_op jit(solution)/shard_map/ppermute | solution.py:539
  25.0 1.4 %collective-permute-start.8 = (f32[264,128]{1,0:T(8,128)S(1)}, f32[264,128]{1,0:T(8,128)S(1)}, u32[]{:S(2)}, u32[]{:S(2)}) collective-permute-start(f32[264,128]{1,0:T(8,128)S(1)} %add.31), channel_id=1, source_target_pairs={{0,8},{2,10},{4,12},{6,14},{8,0},{10,2},{12,4},{14,6},{16,24},{18,... | collective-permute-start | bytes 405512 | tf_op jit(solution)/shard_map/ppermute | solution.py:539
  26.4 2.9 %collective-permute-done.8 = f32[264,128]{1,0:T(8,128)S(1)} collective-permute-done((f32[264,128]{1,0:T(8,128)S(1)}, f32[264,128]{1,0:T(8,128)S(1)}, u32[]{:S(2)}, u32[]{:S(2)}) %collective-permute-start.8) | collective-permute-done | bytes 135200 | tf_op jit(solution)/shard_map/ppermute | solution.py:539
  29.2 2.4 %collective-permute-start.11 = (f32[264,128]{1,0:T(8,128)S(1)}, f32[264,128]{1,0:T(8,128)S(1)}, u32[]{:S(2)}, u32[]{:S(2)}) collective-permute-start(f32[264,128]{1,0:T(8,128)S(1)} %add.32.rest_1_), channel_id=1, source_target_pairs={{0,16},{2,18},{4,20},{6,22},{8,24},{10,26},{12,28},{14,30},{16,0},... | collective-permute-start | bytes 405512 | tf_op jit(solution)/shard_map/ppermute | solution.py:539
  31.7 2.2 %collective-permute-start.9 = (f32[128,640]{1,0:T(8,128)S(1)}, f32[128,640]{1,0:T(8,128)S(1)}, u32[]{:S(2)}, u32[]{:S(2)}) collective-permute-start(f32[128,640]{1,0:T(8,128)S(1)} %shard_map.87), channel_id=1, source_target_pairs={{0,2},{1,3},{2,0},{3,1},{4,6},{5,7},{6,4},{7,5},{8,10},{9,11},{10,... | collective-permute-start | bytes 983048 | tf_op jit(solution)/shard_map/ppermute | solution.py:536
  34.0 3.5 %collective-permute-start.10 = (f32[128,640]{1,0:T(8,128)S(1)}, f32[128,640]{1,0:T(8,128)S(1)}, u32[]{:S(2)}, u32[]{:S(2)}) collective-permute-start(f32[128,640]{1,0:T(8,128)S(1)} %shard_map.88), channel_id=1, source_target_pairs={{2,4},{3,5},{4,2},{5,3},{6,8},{7,9},{8,6},{9,7},{10,12},{11,13},{1... | collective-permute-start | bytes 983048 | tf_op jit(solution)/shard_map/ppermute | solution.py:536
  38.2 3.7 %collective-permute-done.12 = f32[264,128]{1,0:T(8,128)S(1)} collective-permute-done((f32[264,128]{1,0:T(8,128)S(1)}, f32[264,128]{1,0:T(8,128)S(1)}, u32[]{:S(2)}, u32[]{:S(2)}) %collective-permute-start.12) | collective-permute-done | bytes 135200 | tf_op jit(solution)/shard_map/ppermute | solution.py:539
  41.9 2.4 %collective-permute-start.13 = (f32[256,128]{1,0:T(8,128)S(1)}, f32[256,128]{1,0:T(8,128)S(1)}, u32[]{:S(2)}, u32[]{:S(2)}) collective-permute-start(f32[256,128]{1,0:T(8,128)S(1)} %slice.16), channel_id=1, source_target_pairs={{0,2},{2,0},{4,6},{6,4},{8,10},{10,8},{12,14},{14,12},{16,18},{18,... | collective-permute-start | bytes 393224 | tf_op jit(solution)/shard_map/ppermute | solution.py:539
  45.3 3.2 %shard_map.90 = (f32[2,384,384]{2,1,0:T(8,128)S(1)}, f32[384,128]{1,0:T(8,128)S(1)}, f32[136,128]{1,0:T(8,128)S(1)}, f32[136,128]{1,0:T(8,128)S(1)}, f32[2,136,1...) custom-call(s32[2,1,2]{2,1,0:T(1,128)S(1)} %bitcast.14, f32[2,3]{1,0:T(2,128)S(1)} %copy-done.4, ...), custom_call_target="tpu_custom_call" | custom-call | tf_op jit(solution)/shard_map/pallas_call | solution.py:495
  48.5 1.2 %collective-permute-start.15 = (f32[2,136,128]{2,1,0:T(8,128)S(1)}, f32[2,136,128]{2,1,0:T(8,128)S(1)}, u32[]{:S(2)}, u32[]{:S(2)}) collective-permute-start(f32[2,136,128]{2,1,0:T(8,128)S(1)} %get-tuple-element.39), channel_id=1, source_target_pairs={{0,2},{2,0},{4,6},{6,4},{8,10},{10,8},{12,14},{14,12},{16,18},{18,... | collective-permute-start | bytes 417800 | tf_op jit(solution)/shard_map/ppermute | solution.py:539
  51.1 1.1 %collective-permute-start.14 = (f32[384,128]{1,0:T(8,128)S(1)}, f32[384,128]{1,0:T(8,128)S(1)}, u32[]{:S(2)}, u32[]{:S(2)}) collective-permute-start(f32[384,128]{1,0:T(8,128)S(1)} %get-tuple-element.37), channel_id=1, source_target_pairs={{0,1},{1,0},{2,3},{3,2},{4,5},{5,4},{6,7},{7,6},{8,9},{9,8},{10,11... | collective-permute-start | bytes 589832 | tf_op jit(solution)/shard_map/ppermute | solution.py:536
  52.2 1.7 %collective-permute-done.16 = f32[136,128]{1,0:T(8,128)S(1)} collective-permute-done((f32[136,128]{1,0:T(8,128)S(1)}, f32[136,128]{1,0:T(8,128)S(1)}, u32[]{:S(2)}, u32[]{:S(2)}) %collective-permute-start.16) | collective-permute-done | bytes 69664 | tf_op jit(solution)/shard_map/ppermute | solution.py:539
  54.0 4.4 %collective-permute-done.14.rest_0_ = f32[384,128]{1,0:T(8,128)S(1)} collective-permute-done((f32[384,128]{1,0:T(8,128)S(1)}, f32[384,128]{1,0:T(8,128)S(1)}, u32[]{:S(2)}, u32[]{:S(2)}) %collective-permute-start.14) | collective-permute-done | bytes 196640 | tf_op jit(solution)/shard_map/ppermute | solution.py:536
  59.1 2.5 %collective-permute-done.18 = f32[136,128]{1,0:T(8,128)S(1)} collective-permute-done((f32[136,128]{1,0:T(8,128)S(1)}, f32[136,128]{1,0:T(8,128)S(1)}, u32[]{:S(2)}, u32[]{:S(2)}) %collective-permute-start.18) | collective-permute-done | bytes 69664 | tf_op jit(solution)/shard_map/ppermute | solution.py:539
  61.7 1.7 %collective-permute-start.19 = (f32[136,128]{1,0:T(8,128)S(1)}, f32[136,128]{1,0:T(8,128)S(1)}, u32[]{:S(2)}, u32[]{:S(2)}) collective-permute-start(f32[136,128]{1,0:T(8,128)S(1)} %add.38), channel_id=1, source_target_pairs={{0,16},{2,18},{4,20},{6,22},{8,24},{10,26},{12,28},{14,30},{16,0},... | collective-permute-start | bytes 208904 | tf_op jit(solution)/shard_map/ppermute | solution.py:539
  63.4 6.7 %collective-permute-start.21 = (f32[2,64,256]{2,1,0:T(8,128)S(1)}, f32[2,64,256]{2,1,0:T(8,128)S(1)}, u32[]{:S(2)}, u32[]{:S(2)}) collective-permute-start(f32[2,64,256]{2,1,0:T(8,128)S(1)} %get-tuple-element.42), channel_id=1, source_target_pairs={{2,4},{3,5},{4,2},{5,3},{6,8},{7,9},{8,6},{9,7},{10,12},{11,13},{1... | collective-permute-start | bytes 393224 | tf_op jit(solution)/shard_map/ppermute | solution.py:536
  71.2 1.6 %collective-permute-done.21.rest_2_.rest_1_ = f32[2,64,256]{2,1,0:T(8,128)S(1)} collective-permute-done((f32[2,64,256]{2,1,0:T(8,128)S(1)}, f32[2,64,256]{2,1,0:T(8,128)S(1)}, u32[]{:S(2)}, u32[]{:S(2)}) %collective-permute-start.21) | collective-permute-done | bytes 131104 | tf_op jit(solution)/shard_map/ppermute | solution.py:536
  72.8 2.0 %collective-permute-done.22.beside_ref.q1 = f32[128,128]{1,0:T(8,128)S(1)} collective-permute-done((f32[128,128]{1,0:T(8,128)S(1)}, f32[128,128]{1,0:T(8,128)S(1)}, u32[]{:S(2)}, u32[]{:S(2)}) %collective-permute-start.22) | collective-permute-done | bytes 65568 | tf_op jit(solution)/shard_map/ppermute | solution.py:539
  (58 shorter events, 11.7 us)
Async XLA Ops:
  1.9 12.0 %collective-permute-start = (f32[2,64,256]{2,1,0:T(8,128)S(1)}, f32[2,64,256]{2,1,0:T(8,128)S(1)}, u32[]{:S(2)}, u32[]{:S(2)}) collective-permute-start(f32[2,64,256]{2,1,0:T(8,128)S(1)} %get-tuple-element.26), channel_id=1, source_target_pairs={{0,2},{1,3},{2,0},{3,1},{4,6},{5,7},{6,4},{7,5},{8,10},{9,11},{10,... | collective-permute-start | bytes 393224 | tf_op jit(solution)/shard_map/ppermute | solution.py:536
  2.7 11.2 %collective-permute-start.1 = (f32[2,64,256]{2,1,0:T(8,128)S(1)}, f32[2,64,256]{2,1,0:T(8,128)S(1)}, u32[]{:S(2)}, u32[]{:S(2)}) collective-permute-start(f32[2,64,256]{2,1,0:T(8,128)S(1)} %get-tuple-element.27), channel_id=1, source_target_pairs={{2,4},{3,5},{4,2},{5,3},{6,8},{7,9},{8,6},{9,7},{10,12},{11,13},{1... | collective-permute-start | bytes 393224 | tf_op jit(solution)/shard_map/ppermute | solution.py:536
  5.7 8.2 %collective-permute-start.2 = (f32[256,128]{1,0:T(8,128)S(1)}, f32[256,128]{1,0:T(8,128)S(1)}, u32[]{:S(2)}, u32[]{:S(2)}) collective-permute-start(f32[256,128]{1,0:T(8,128)S(1)} %get-tuple-element.28), channel_id=1, source_target_pairs={{0,1},{1,0},{2,3},{3,2},{4,5},{5,4},{6,7},{7,6},{8,9},{9,8},{10,11... | collective-permute-start | bytes 393224 | tf_op jit(solution)/shard_map/ppermute | solution.py:536
  6.1 5.8 %collective-permute-start.3 = (f32[64,128]{1,0:T(8,128)S(1)}, f32[64,128]{1,0:T(8,128)S(1)}, u32[]{:S(2)}, u32[]{:S(2)}) collective-permute-start(f32[64,128]{1,0:T(8,128)S(1)} %get-tuple-element.29), channel_id=1, source_target_pairs={{0,3},{1,2},{2,1},{3,0},{4,7},{5,6},{6,5},{7,4},{8,11},{9,10},{10,... | collective-permute-start | bytes 98312 | tf_op jit(solution)/shard_map/ppermute | solution.py:536
  6.9 7.0 %collective-permute-start.4 = (f32[64,128]{1,0:T(8,128)S(1)}, f32[64,128]{1,0:T(8,128)S(1)}, u32[]{:S(2)}, u32[]{:S(2)}) collective-permute-start(f32[64,128]{1,0:T(8,128)S(1)} %get-tuple-element.30), channel_id=1, source_target_pairs={{2,5},{3,4},{4,3},{5,2},{6,9},{7,8},{8,7},{9,6},{10,13},{11,12},{1... | collective-permute-start | bytes 98312 | tf_op jit(solution)/shard_map/ppermute | solution.py:536
  18.4 1.4 %collective-permute-start.6 = (f32[264,128]{1,0:T(8,128)S(1)}, f32[264,128]{1,0:T(8,128)S(1)}, u32[]{:S(2)}, u32[]{:S(2)}) collective-permute-start(f32[264,128]{1,0:T(8,128)S(1)} %get-tuple-element.35), channel_id=1, source_target_pairs={{0,2},{2,0},{4,6},{6,4},{8,10},{10,8},{12,14},{14,12},{16,18},{18,... | collective-permute-start | bytes 405512 | tf_op jit(solution)/shard_map/ppermute | solution.py:539
  18.5 13.1 %collective-permute-start.5 = (f32[2,384,128]{2,1,0:T(8,128)S(1)}, f32[2,384,128]{2,1,0:T(8,128)S(1)}, u32[]{:S(2)}, u32[]{:S(2)}) collective-permute-start(f32[2,384,128]{2,1,0:T(8,128)S(1)} %get-tuple-element.33), channel_id=1, source_target_pairs={{0,1},{1,0},{2,3},{3,2},{4,5},{5,4},{6,7},{7,6},{8,9},{9,8},{10,11... | collective-permute-start | bytes 1179656 | tf_op jit(solution)/shard_map/ppermute | solution.py:536
  19.9 5.1 %collective-permute-start.7 = (f32[264,128]{1,0:T(8,128)S(1)}, f32[264,128]{1,0:T(8,128)S(1)}, u32[]{:S(2)}, u32[]{:S(2)}) collective-permute-start(f32[264,128]{1,0:T(8,128)S(1)} %add.30), channel_id=1, source_target_pairs={{0,4},{2,6},{4,0},{6,2},{8,12},{10,14},{12,8},{14,10},{16,20},{18,... | collective-permute-start | bytes 405512 | tf_op jit(solution)/shard_map/ppermute | solution.py:539
  25.0 4.2 %collective-permute-start.8 = (f32[264,128]{1,0:T(8,128)S(1)}, f32[264,128]{1,0:T(8,128)S(1)}, u32[]{:S(2)}, u32[]{:S(2)}) collective-permute-start(f32[264,128]{1,0:T(8,128)S(1)} %add.31), channel_id=1, source_target_pairs={{0,8},{2,10},{4,12},{6,14},{8,0},{10,2},{12,4},{14,6},{16,24},{18,... | collective-permute-start | bytes 405512 | tf_op jit(solution)/shard_map/ppermute | solution.py:539
  29.2 8.3 %collective-permute-start.11 = (f32[264,128]{1,0:T(8,128)S(1)}, f32[264,128]{1,0:T(8,128)S(1)}, u32[]{:S(2)}, u32[]{:S(2)}) collective-permute-start(f32[264,128]{1,0:T(8,128)S(1)} %add.32.rest_1_), channel_id=1, source_target_pairs={{0,16},{2,18},{4,20},{6,22},{8,24},{10,26},{12,28},{14,30},{16,0},... | collective-permute-start | bytes 405512 | tf_op jit(solution)/shard_map/ppermute | solution.py:539
  31.7 12.6 %collective-permute-start.9 = (f32[128,640]{1,0:T(8,128)S(1)}, f32[128,640]{1,0:T(8,128)S(1)}, u32[]{:S(2)}, u32[]{:S(2)}) collective-permute-start(f32[128,640]{1,0:T(8,128)S(1)} %shard_map.87), channel_id=1, source_target_pairs={{0,2},{1,3},{2,0},{3,1},{4,6},{5,7},{6,4},{7,5},{8,10},{9,11},{10,... | collective-permute-start | bytes 983048 | tf_op jit(solution)/shard_map/ppermute | solution.py:536
  34.0 10.3 %collective-permute-start.10 = (f32[128,640]{1,0:T(8,128)S(1)}, f32[128,640]{1,0:T(8,128)S(1)}, u32[]{:S(2)}, u32[]{:S(2)}) collective-permute-start(f32[128,640]{1,0:T(8,128)S(1)} %shard_map.88), channel_id=1, source_target_pairs={{2,4},{3,5},{4,2},{5,3},{6,8},{7,9},{8,6},{9,7},{10,12},{11,13},{1... | collective-permute-start | bytes 983048 | tf_op jit(solution)/shard_map/ppermute | solution.py:536
  37.6 4.2 %collective-permute-start.12 = (f32[264,128]{1,0:T(8,128)S(1)}, f32[264,128]{1,0:T(8,128)S(1)}, u32[]{:S(2)}, u32[]{:S(2)}) collective-permute-start(f32[264,128]{1,0:T(8,128)S(1)} %add.33), channel_id=1, source_target_pairs={{0,1},{1,0},{2,3},{3,2},{4,5},{5,4},{6,7},{7,6},{8,9},{9,8},{10,11... | collective-permute-start | bytes 405512 | tf_op jit(solution)/shard_map/ppermute | solution.py:539
  41.9 3.4 %collective-permute-start.13 = (f32[256,128]{1,0:T(8,128)S(1)}, f32[256,128]{1,0:T(8,128)S(1)}, u32[]{:S(2)}, u32[]{:S(2)}) collective-permute-start(f32[256,128]{1,0:T(8,128)S(1)} %slice.16), channel_id=1, source_target_pairs={{0,2},{2,0},{4,6},{6,4},{8,10},{10,8},{12,14},{14,12},{16,18},{18,... | collective-permute-start | bytes 393224 | tf_op jit(solution)/shard_map/ppermute | solution.py:539
  48.5 2.2 %collective-permute-start.15 = (f32[2,136,128]{2,1,0:T(8,128)S(1)}, f32[2,136,128]{2,1,0:T(8,128)S(1)}, u32[]{:S(2)}, u32[]{:S(2)}) collective-permute-start(f32[2,136,128]{2,1,0:T(8,128)S(1)} %get-tuple-element.39), channel_id=1, source_target_pairs={{0,2},{2,0},{4,6},{6,4},{8,10},{10,8},{12,14},{14,12},{16,18},{18,... | collective-permute-start | bytes 417800 | tf_op jit(solution)/shard_map/ppermute | solution.py:539
  50.7 3.2 %collective-permute-start.16 = (f32[136,128]{1,0:T(8,128)S(1)}, f32[136,128]{1,0:T(8,128)S(1)}, u32[]{:S(2)}, u32[]{:S(2)}) collective-permute-start(f32[136,128]{1,0:T(8,128)S(1)} %fusion), channel_id=1, source_target_pairs={{0,1},{1,0},{2,3},{3,2},{4,5},{5,4},{6,7},{7,6},{8,9},{9,8},{10,11... | collective-permute-start | bytes 208904 | tf_op jit(solution)/shard_map/ppermute | solution.py:539
  51.1 7.3 %collective-permute-start.14 = (f32[384,128]{1,0:T(8,128)S(1)}, f32[384,128]{1,0:T(8,128)S(1)}, u32[]{:S(2)}, u32[]{:S(2)}) collective-permute-start(f32[384,128]{1,0:T(8,128)S(1)} %get-tuple-element.37), channel_id=1, source_target_pairs={{0,1},{1,0},{2,3},{3,2},{4,5},{5,4},{6,7},{7,6},{8,9},{9,8},{10,11... | collective-permute-start | bytes 589832 | tf_op jit(solution)/shard_map/ppermute | solution.py:536
  53.9 4.4 %collective-permute-start.17 = (f32[136,128]{1,0:T(8,128)S(1)}, f32[136,128]{1,0:T(8,128)S(1)}, u32[]{:S(2)}, u32[]{:S(2)}) collective-permute-start(f32[136,128]{1,0:T(8,128)S(1)} %fusion.2.rest_1_), channel_id=1, source_target_pairs={{0,4},{2,6},{4,0},{6,2},{8,12},{10,14},{12,8},{14,10},{16,20},{18,... | collective-permute-start | bytes 208904 | tf_op jit(solution)/shard_map/ppermute | solution.py:539
  58.4 3.2 %collective-permute-start.18 = (f32[136,128]{1,0:T(8,128)S(1)}, f32[136,128]{1,0:T(8,128)S(1)}, u32[]{:S(2)}, u32[]{:S(2)}) collective-permute-start(f32[136,128]{1,0:T(8,128)S(1)} %get-tuple-element.41), channel_id=1, source_target_pairs={{0,8},{2,10},{4,12},{6,14},{8,0},{10,2},{12,4},{14,6},{16,24},{18,... | collective-permute-start | bytes 208904 | tf_op jit(solution)/shard_map/ppermute | solution.py:539
  61.7 8.4 %collective-permute-start.19 = (f32[136,128]{1,0:T(8,128)S(1)}, f32[136,128]{1,0:T(8,128)S(1)}, u32[]{:S(2)}, u32[]{:S(2)}) collective-permute-start(f32[136,128]{1,0:T(8,128)S(1)} %add.38), channel_id=1, source_target_pairs={{0,16},{2,18},{4,20},{6,22},{8,24},{10,26},{12,28},{14,30},{16,0},... | collective-permute-start | bytes 208904 | tf_op jit(solution)/shard_map/ppermute | solution.py:539
  63.4 9.4 %collective-permute-start.21 = (f32[2,64,256]{2,1,0:T(8,128)S(1)}, f32[2,64,256]{2,1,0:T(8,128)S(1)}, u32[]{:S(2)}, u32[]{:S(2)}) collective-permute-start(f32[2,64,256]{2,1,0:T(8,128)S(1)} %get-tuple-element.42), channel_id=1, source_target_pairs={{2,4},{3,5},{4,2},{5,3},{6,8},{7,9},{8,6},{9,7},{10,12},{11,13},{1... | collective-permute-start | bytes 393224 | tf_op jit(solution)/shard_map/ppermute | solution.py:536
  70.2 4.7 %collective-permute-start.20 = (f32[2,64,256]{2,1,0:T(8,128)S(1)}, f32[2,64,256]{2,1,0:T(8,128)S(1)}, u32[]{:S(2)}, u32[]{:S(2)}) collective-permute-start(f32[2,64,256]{2,1,0:T(8,128)S(1)} %shard_map.92), channel_id=1, source_target_pairs={{0,2},{1,3},{2,0},{3,1},{4,6},{5,7},{6,4},{7,5},{8,10},{9,11},{10,... | collective-permute-start | bytes 393224 | tf_op jit(solution)/shard_map/ppermute | solution.py:536
  71.2 3.7 %collective-permute-start.22 = (f32[128,128]{1,0:T(8,128)S(1)}, f32[128,128]{1,0:T(8,128)S(1)}, u32[]{:S(2)}, u32[]{:S(2)}) collective-permute-start(f32[128,128]{1,0:T(8,128)S(1)} %slice.19.own_ref), channel_id=1, source_target_pairs={{0,1},{1,0},{2,3},{3,2},{4,5},{5,4},{6,7},{7,6},{8,9},{9,8},{10,11... | collective-permute-start | bytes 196616 | tf_op jit(solution)/shard_map/ppermute | solution.py:539
  74.9 1.9 %collective-permute-start.23 = (f32[256,128]{1,0:T(8,128)S(1)}, f32[256,128]{1,0:T(8,128)S(1)}, u32[]{:S(2)}, u32[]{:S(2)}) collective-permute-start(f32[256,128]{1,0:T(8,128)S(1)} %shard_map.94), channel_id=1, source_target_pairs={{0,2},{2,0},{4,6},{6,4},{8,10},{10,8},{12,14},{14,12},{16,18},{18,... | collective-permute-start | bytes 393224 | tf_op jit(solution)/shard_map/ppermute | solution.py:539
  (6 other events, 66.5 us)

commit v6 on v5

--- a/solution.py
+++ b/solution.py
@@ -99,15 +99,18 @@
     phases = jnp.concatenate(phases, axis=0)
     cosines, sines = jnp.cos(phases), jnp.sin(phases)
 
-    def along_rows(row):
-        return jnp.transpose(jnp.broadcast_to(row, (width, width)))
+    turned = jnp.transpose(jnp.concatenate([cosines, sines, jnp.broadcast_to(centred, (8, width))], axis=0))
+    sine_at, centre_at = cosines.shape[0], 2 * cosines.shape[0]
+
+    def along_rows(k):
+        return jnp.broadcast_to(turned[:, k : k + 1], (width, width))
 
     lits = []
     ramps = []
     for j in range(count):
         row_start, row_shift, lane = window_place(starts, j, tile_rows, tile_cols, width, fast, slow)
         row_start = pl.multiple_of(row_start, 8)
-        row_cos, row_sin = along_rows(cosines[2 * j : 2 * j + 1]), along_rows(sines[2 * j : 2 * j + 1])
+        row_cos, row_sin = along_rows(2 * j), along_rows(sine_at + 2 * j)
         col_cos, col_sin = cosines[2 * j + 1 : 2 * j + 2], sines[2 * j + 1 : 2 * j + 2]
         ramp_real = row_cos * col_cos - row_sin * col_sin
         ramp_imag = row_cos * col_sin + row_sin * col_cos
@@ -156,7 +159,7 @@
     gradient_ref[...] = jnp.zeros(gradient_ref.shape, F32)
     probe_grad = [[None] * modes, [None] * modes]
     descan_grad = [None] * 6
-    centred_rows = along_rows(centred)
+    centred_rows = along_rows(centre_at)
     for j in range(count):
         lit_real, lit_imag = lits[j]
         ramp_real, ramp_imag = ramps[j]

time: 78.6 us -> 78.5 us (level)
  no operation moved by 1% of the time
where the time goes in v6:
time: 78.5 us; the launch traced here: 77.6 us
  starting transfers between devices  35.6 us (45%)
  waiting for transfers between devices  29.5 us (38%)
  Pallas kernels  10.4 us (13%)
  local copies, waits for them, and re-layouts  1.15 us (1%)
  between operations  0.89 us (1%)
    ppermute x11, starting transfers between devices, exchanged(): return lax.ppermute(value, AXES, pairs)  23.6 us
    ppermute x13, waiting for transfers between devices, swapped(): lax.ppermute(value, axis, [(i, i ^ bit) for i in range(lax.axis_size(axis...  20.2 us
    ppermute x13, starting transfers between devices, swapped(): lax.ppermute(value, axis, [(i, i ^ bit) for i in range(lax.axis_size(axis...  12 us
    pallas_call x11, Pallas kernels, call(): pl.pallas_call(kernel, out_shape=[out if isinstance(out, jax.ShapeDtypeSt...  10.4 us
    ppermute x11, waiting for transfers between devices, exchanged(): return lax.ppermute(value, AXES, pairs)  9.24 us
  transfers between devices with their start and end apart: 24, of which 13 were waited for; matrix products, arithmetic and copies ran while one was open for 0% of the time, Pallas kernels for 2%

profile of v6, /device:TPU:7, one launch (start us, length us, event | category | flops | bytes accessed | tf_op | source)
XLA Modules:
  0.0 77.6 jit_solution(17399166449502983443)
XLA Ops:
  0.7 1.1 %copy-done.5 = f32[2,256,256]{2,1,0:T(8,128)S(1)} copy-done((f32[2,256,256]{2,1,0:T(8,128)S(1)}, f32[2,256,256]{2,1,0:T(8,128)}, u32[]{:S(2)}) %copy-start.5) | copy-done | bytes 524312
  2.7 3.0 %collective-permute-start.1 = (f32[2,64,256]{2,1,0:T(8,128)S(1)}, f32[2,64,256]{2,1,0:T(8,128)S(1)}, u32[]{:S(2)}, u32[]{:S(2)}) collective-permute-start(f32[2,64,256]{2,1,0:T(8,128)S(1)} %get-tuple-element.27), channel_id=1, source_target_pairs={{2,4},{3,5},{4,2},{5,3},{6,8},{7,9},{8,6},{9,7},{10,12},{11,13},{1... | collective-permute-start | bytes 393224 | tf_op jit(solution)/shard_map/ppermute | solution.py:539
  6.9 3.8 %collective-permute-start.4 = (f32[64,128]{1,0:T(8,128)S(1)}, f32[64,128]{1,0:T(8,128)S(1)}, u32[]{:S(2)}, u32[]{:S(2)}) collective-permute-start(f32[64,128]{1,0:T(8,128)S(1)} %get-tuple-element.30), channel_id=1, source_target_pairs={{2,5},{3,4},{4,3},{5,2},{6,9},{7,8},{8,7},{9,6},{10,13},{11,12},{1... | collective-permute-start | bytes 98312 | tf_op jit(solution)/shard_map/ppermute | solution.py:539
  10.7 1.2 %collective-permute-done.3.rest_3_ = f32[64,128]{1,0:T(8,128)S(1)} collective-permute-done((f32[64,128]{1,0:T(8,128)S(1)}, f32[64,128]{1,0:T(8,128)S(1)}, u32[]{:S(2)}, u32[]{:S(2)}) %collective-permute-start.3) | collective-permute-done | bytes 32800 | tf_op jit(solution)/shard_map/ppermute | solution.py:539
  11.9 2.0 %collective-permute-done.4.rest_4_ = f32[64,128]{1,0:T(8,128)S(1)} collective-permute-done((f32[64,128]{1,0:T(8,128)S(1)}, f32[64,128]{1,0:T(8,128)S(1)}, u32[]{:S(2)}, u32[]{:S(2)}) %collective-permute-start.4) | collective-permute-done | bytes 32800 | tf_op jit(solution)/shard_map/ppermute | solution.py:539
  14.0 4.4 %shard_map.86 = (f32[2,384,384]{2,1,0:T(8,128)S(1)}, f32[2,384,384]{2,1,0:T(8,128)S(1)}, f32[2,384,128]{2,1,0:T(8,128)S(1)}, f32[264,128]{1,0:T(8,128)S(1)}, f32[264,128]{1,0:T(8,128)S(1)}) custom-call(s32[2,1,2]{2,1,0:T(1,128)S(1)} %bitcast.13, f32[2,3]{1,0:T(2,128)S(1)} %copy-done.4, ...), custom_call_target="tpu_custom_call", output_to_operand_aliasing={{0}: (2, {})} | custom-call | tf_op jit(solution)/shard_map/pallas_call | solution.py:498
  19.9 5.0 %collective-permute-done.7 = f32[264,128]{1,0:T(8,128)S(1)} collective-permute-done((f32[264,128]{1,0:T(8,128)S(1)}, f32[264,128]{1,0:T(8,128)S(1)}, u32[]{:S(2)}, u32[]{:S(2)}) %collective-permute-start.7) | collective-permute-done | bytes 135200 | tf_op jit(solution)/shard_map/ppermute | solution.py:542
  24.9 1.4 %collective-permute-start.8 = (f32[264,128]{1,0:T(8,128)S(1)}, f32[264,128]{1,0:T(8,128)S(1)}, u32[]{:S(2)}, u32[]{:S(2)}) collective-permute-start(f32[264,128]{1,0:T(8,128)S(1)} %add.31), channel_id=1, source_target_pairs={{0,8},{2,10},{4,12},{6,14},{8,0},{10,2},{12,4},{14,6},{16,24},{18,... | collective-permute-start | bytes 405512 | tf_op jit(solution)/shard_map/ppermute | solution.py:542
  26.3 2.9 %collective-permute-done.8 = f32[264,128]{1,0:T(8,128)S(1)} collective-permute-done((f32[264,128]{1,0:T(8,128)S(1)}, f32[264,128]{1,0:T(8,128)S(1)}, u32[]{:S(2)}, u32[]{:S(2)}) %collective-permute-start.8) | collective-permute-done | bytes 135200 | tf_op jit(solution)/shard_map/ppermute | solution.py:542
  29.2 2.4 %collective-permute-start.11 = (f32[264,128]{1,0:T(8,128)S(1)}, f32[264,128]{1,0:T(8,128)S(1)}, u32[]{:S(2)}, u32[]{:S(2)}) collective-permute-start(f32[264,128]{1,0:T(8,128)S(1)} %add.32.rest_1_), channel_id=1, source_target_pairs={{0,16},{2,18},{4,20},{6,22},{8,24},{10,26},{12,28},{14,30},{16,0},... | collective-permute-start | bytes 405512 | tf_op jit(solution)/shard_map/ppermute | solution.py:542
  31.7 2.2 %collective-permute-start.9 = (f32[128,640]{1,0:T(8,128)S(1)}, f32[128,640]{1,0:T(8,128)S(1)}, u32[]{:S(2)}, u32[]{:S(2)}) collective-permute-start(f32[128,640]{1,0:T(8,128)S(1)} %shard_map.87), channel_id=1, source_target_pairs={{0,2},{1,3},{2,0},{3,1},{4,6},{5,7},{6,4},{7,5},{8,10},{9,11},{10,... | collective-permute-start | bytes 983048 | tf_op jit(solution)/shard_map/ppermute | solution.py:539
  34.0 3.5 %collective-permute-start.10 = (f32[128,640]{1,0:T(8,128)S(1)}, f32[128,640]{1,0:T(8,128)S(1)}, u32[]{:S(2)}, u32[]{:S(2)}) collective-permute-start(f32[128,640]{1,0:T(8,128)S(1)} %shard_map.88), channel_id=1, source_target_pairs={{2,4},{3,5},{4,2},{5,3},{6,8},{7,9},{8,6},{9,7},{10,12},{11,13},{1... | collective-permute-start | bytes 983048 | tf_op jit(solution)/shard_map/ppermute | solution.py:539
  38.1 3.7 %collective-permute-done.12 = f32[264,128]{1,0:T(8,128)S(1)} collective-permute-done((f32[264,128]{1,0:T(8,128)S(1)}, f32[264,128]{1,0:T(8,128)S(1)}, u32[]{:S(2)}, u32[]{:S(2)}) %collective-permute-start.12) | collective-permute-done | bytes 135200 | tf_op jit(solution)/shard_map/ppermute | solution.py:542
  41.8 2.4 %collective-permute-start.13 = (f32[256,128]{1,0:T(8,128)S(1)}, f32[256,128]{1,0:T(8,128)S(1)}, u32[]{:S(2)}, u32[]{:S(2)}) collective-permute-start(f32[256,128]{1,0:T(8,128)S(1)} %slice.16), channel_id=1, source_target_pairs={{0,2},{2,0},{4,6},{6,4},{8,10},{10,8},{12,14},{14,12},{16,18},{18,... | collective-permute-start | bytes 393224 | tf_op jit(solution)/shard_map/ppermute | solution.py:542
  45.2 3.2 %shard_map.90 = (f32[2,384,384]{2,1,0:T(8,128)S(1)}, f32[384,128]{1,0:T(8,128)S(1)}, f32[136,128]{1,0:T(8,128)S(1)}, f32[136,128]{1,0:T(8,128)S(1)}, f32[2,136,1...) custom-call(s32[2,1,2]{2,1,0:T(1,128)S(1)} %bitcast.14, f32[2,3]{1,0:T(2,128)S(1)} %copy-done.4, ...), custom_call_target="tpu_custom_call" | custom-call | tf_op jit(solution)/shard_map/pallas_call | solution.py:498
  48.4 1.2 %collective-permute-start.15 = (f32[2,136,128]{2,1,0:T(8,128)S(1)}, f32[2,136,128]{2,1,0:T(8,128)S(1)}, u32[]{:S(2)}, u32[]{:S(2)}) collective-permute-start(f32[2,136,128]{2,1,0:T(8,128)S(1)} %get-tuple-element.39), channel_id=1, source_target_pairs={{0,2},{2,0},{4,6},{6,4},{8,10},{10,8},{12,14},{14,12},{16,18},{18,... | collective-permute-start | bytes 417800 | tf_op jit(solution)/shard_map/ppermute | solution.py:542
  51.0 1.1 %collective-permute-start.14 = (f32[384,128]{1,0:T(8,128)S(1)}, f32[384,128]{1,0:T(8,128)S(1)}, u32[]{:S(2)}, u32[]{:S(2)}) collective-permute-start(f32[384,128]{1,0:T(8,128)S(1)} %get-tuple-element.37), channel_id=1, source_target_pairs={{0,1},{1,0},{2,3},{3,2},{4,5},{5,4},{6,7},{7,6},{8,9},{9,8},{10,11... | collective-permute-start | bytes 589832 | tf_op jit(solution)/shard_map/ppermute | solution.py:539
  52.1 1.7 %collective-permute-done.16 = f32[136,128]{1,0:T(8,128)S(1)} collective-permute-done((f32[136,128]{1,0:T(8,128)S(1)}, f32[136,128]{1,0:T(8,128)S(1)}, u32[]{:S(2)}, u32[]{:S(2)}) %collective-permute-start.16) | collective-permute-done | bytes 69664 | tf_op jit(solution)/shard_map/ppermute | solution.py:542
  53.9 4.4 %collective-permute-done.14.rest_0_ = f32[384,128]{1,0:T(8,128)S(1)} collective-permute-done((f32[384,128]{1,0:T(8,128)S(1)}, f32[384,128]{1,0:T(8,128)S(1)}, u32[]{:S(2)}, u32[]{:S(2)}) %collective-permute-start.14) | collective-permute-done | bytes 196640 | tf_op jit(solution)/shard_map/ppermute | solution.py:539
  59.1 2.5 %collective-permute-done.18 = f32[136,128]{1,0:T(8,128)S(1)} collective-permute-done((f32[136,128]{1,0:T(8,128)S(1)}, f32[136,128]{1,0:T(8,128)S(1)}, u32[]{:S(2)}, u32[]{:S(2)}) %collective-permute-start.18) | collective-permute-done | bytes 69664 | tf_op jit(solution)/shard_map/ppermute | solution.py:542
  61.6 1.8 %collective-permute-start.19 = (f32[136,128]{1,0:T(8,128)S(1)}, f32[136,128]{1,0:T(8,128)S(1)}, u32[]{:S(2)}, u32[]{:S(2)}) collective-permute-start(f32[136,128]{1,0:T(8,128)S(1)} %add.38), channel_id=1, source_target_pairs={{0,16},{2,18},{4,20},{6,22},{8,24},{10,26},{12,28},{14,30},{16,0},... | collective-permute-start | bytes 208904 | tf_op jit(solution)/shard_map/ppermute | solution.py:542
  63.4 6.6 %collective-permute-start.21 = (f32[2,64,256]{2,1,0:T(8,128)S(1)}, f32[2,64,256]{2,1,0:T(8,128)S(1)}, u32[]{:S(2)}, u32[]{:S(2)}) collective-permute-start(f32[2,64,256]{2,1,0:T(8,128)S(1)} %get-tuple-element.42), channel_id=1, source_target_pairs={{2,4},{3,5},{4,2},{5,3},{6,8},{7,9},{8,6},{9,7},{10,12},{11,13},{1... | collective-permute-start | bytes 393224 | tf_op jit(solution)/shard_map/ppermute | solution.py:539
  71.1 1.6 %collective-permute-done.21.rest_2_.rest_1_ = f32[2,64,256]{2,1,0:T(8,128)S(1)} collective-permute-done((f32[2,64,256]{2,1,0:T(8,128)S(1)}, f32[2,64,256]{2,1,0:T(8,128)S(1)}, u32[]{:S(2)}, u32[]{:S(2)}) %collective-permute-start.21) | collective-permute-done | bytes 131104 | tf_op jit(solution)/shard_map/ppermute | solution.py:539
  72.8 2.0 %collective-permute-done.22.beside_ref.q1 = f32[128,128]{1,0:T(8,128)S(1)} collective-permute-done((f32[128,128]{1,0:T(8,128)S(1)}, f32[128,128]{1,0:T(8,128)S(1)}, u32[]{:S(2)}, u32[]{:S(2)}) %collective-permute-start.22) | collective-permute-done | bytes 65568 | tf_op jit(solution)/shard_map/ppermute | solution.py:542
  (58 shorter events, 11.7 us)
Async XLA Ops:
  1.9 12.0 %collective-permute-start = (f32[2,64,256]{2,1,0:T(8,128)S(1)}, f32[2,64,256]{2,1,0:T(8,128)S(1)}, u32[]{:S(2)}, u32[]{:S(2)}) collective-permute-start(f32[2,64,256]{2,1,0:T(8,128)S(1)} %get-tuple-element.26), channel_id=1, source_target_pairs={{0,2},{1,3},{2,0},{3,1},{4,6},{5,7},{6,4},{7,5},{8,10},{9,11},{10,... | collective-permute-start | bytes 393224 | tf_op jit(solution)/shard_map/ppermute | solution.py:539
  2.7 11.2 %collective-permute-start.1 = (f32[2,64,256]{2,1,0:T(8,128)S(1)}, f32[2,64,256]{2,1,0:T(8,128)S(1)}, u32[]{:S(2)}, u32[]{:S(2)}) collective-permute-start(f32[2,64,256]{2,1,0:T(8,128)S(1)} %get-tuple-element.27), channel_id=1, source_target_pairs={{2,4},{3,5},{4,2},{5,3},{6,8},{7,9},{8,6},{9,7},{10,12},{11,13},{1... | collective-permute-start | bytes 393224 | tf_op jit(solution)/shard_map/ppermute | solution.py:539
  5.7 8.2 %collective-permute-start.2 = (f32[256,128]{1,0:T(8,128)S(1)}, f32[256,128]{1,0:T(8,128)S(1)}, u32[]{:S(2)}, u32[]{:S(2)}) collective-permute-start(f32[256,128]{1,0:T(8,128)S(1)} %get-tuple-element.28), channel_id=1, source_target_pairs={{0,1},{1,0},{2,3},{3,2},{4,5},{5,4},{6,7},{7,6},{8,9},{9,8},{10,11... | collective-permute-start | bytes 393224 | tf_op jit(solution)/shard_map/ppermute | solution.py:539
  6.1 5.8 %collective-permute-start.3 = (f32[64,128]{1,0:T(8,128)S(1)}, f32[64,128]{1,0:T(8,128)S(1)}, u32[]{:S(2)}, u32[]{:S(2)}) collective-permute-start(f32[64,128]{1,0:T(8,128)S(1)} %get-tuple-element.29), channel_id=1, source_target_pairs={{0,3},{1,2},{2,1},{3,0},{4,7},{5,6},{6,5},{7,4},{8,11},{9,10},{10,... | collective-permute-start | bytes 98312 | tf_op jit(solution)/shard_map/ppermute | solution.py:539
  6.9 7.0 %collective-permute-start.4 = (f32[64,128]{1,0:T(8,128)S(1)}, f32[64,128]{1,0:T(8,128)S(1)}, u32[]{:S(2)}, u32[]{:S(2)}) collective-permute-start(f32[64,128]{1,0:T(8,128)S(1)} %get-tuple-element.30), channel_id=1, source_target_pairs={{2,5},{3,4},{4,3},{5,2},{6,9},{7,8},{8,7},{9,6},{10,13},{11,12},{1... | collective-permute-start | bytes 98312 | tf_op jit(solution)/shard_map/ppermute | solution.py:539
  18.4 1.4 %collective-permute-start.6 = (f32[264,128]{1,0:T(8,128)S(1)}, f32[264,128]{1,0:T(8,128)S(1)}, u32[]{:S(2)}, u32[]{:S(2)}) collective-permute-start(f32[264,128]{1,0:T(8,128)S(1)} %get-tuple-element.35), channel_id=1, source_target_pairs={{0,2},{2,0},{4,6},{6,4},{8,10},{10,8},{12,14},{14,12},{16,18},{18,... | collective-permute-start | bytes 405512 | tf_op jit(solution)/shard_map/ppermute | solution.py:542
  18.5 13.1 %collective-permute-start.5 = (f32[2,384,128]{2,1,0:T(8,128)S(1)}, f32[2,384,128]{2,1,0:T(8,128)S(1)}, u32[]{:S(2)}, u32[]{:S(2)}) collective-permute-start(f32[2,384,128]{2,1,0:T(8,128)S(1)} %get-tuple-element.33), channel_id=1, source_target_pairs={{0,1},{1,0},{2,3},{3,2},{4,5},{5,4},{6,7},{7,6},{8,9},{9,8},{10,11... | collective-permute-start | bytes 1179656 | tf_op jit(solution)/shard_map/ppermute | solution.py:539
  19.8 5.1 %collective-permute-start.7 = (f32[264,128]{1,0:T(8,128)S(1)}, f32[264,128]{1,0:T(8,128)S(1)}, u32[]{:S(2)}, u32[]{:S(2)}) collective-permute-start(f32[264,128]{1,0:T(8,128)S(1)} %add.30), channel_id=1, source_target_pairs={{0,4},{2,6},{4,0},{6,2},{8,12},{10,14},{12,8},{14,10},{16,20},{18,... | collective-permute-start | bytes 405512 | tf_op jit(solution)/shard_map/ppermute | solution.py:542
  24.9 4.2 %collective-permute-start.8 = (f32[264,128]{1,0:T(8,128)S(1)}, f32[264,128]{1,0:T(8,128)S(1)}, u32[]{:S(2)}, u32[]{:S(2)}) collective-permute-start(f32[264,128]{1,0:T(8,128)S(1)} %add.31), channel_id=1, source_target_pairs={{0,8},{2,10},{4,12},{6,14},{8,0},{10,2},{12,4},{14,6},{16,24},{18,... | collective-permute-start | bytes 405512 | tf_op jit(solution)/shard_map/ppermute | solution.py:542
  29.2 8.3 %collective-permute-start.11 = (f32[264,128]{1,0:T(8,128)S(1)}, f32[264,128]{1,0:T(8,128)S(1)}, u32[]{:S(2)}, u32[]{:S(2)}) collective-permute-start(f32[264,128]{1,0:T(8,128)S(1)} %add.32.rest_1_), channel_id=1, source_target_pairs={{0,16},{2,18},{4,20},{6,22},{8,24},{10,26},{12,28},{14,30},{16,0},... | collective-permute-start | bytes 405512 | tf_op jit(solution)/shard_map/ppermute | solution.py:542
  31.7 12.6 %collective-permute-start.9 = (f32[128,640]{1,0:T(8,128)S(1)}, f32[128,640]{1,0:T(8,128)S(1)}, u32[]{:S(2)}, u32[]{:S(2)}) collective-permute-start(f32[128,640]{1,0:T(8,128)S(1)} %shard_map.87), channel_id=1, source_target_pairs={{0,2},{1,3},{2,0},{3,1},{4,6},{5,7},{6,4},{7,5},{8,10},{9,11},{10,... | collective-permute-start | bytes 983048 | tf_op jit(solution)/shard_map/ppermute | solution.py:539
  34.0 10.3 %collective-permute-start.10 = (f32[128,640]{1,0:T(8,128)S(1)}, f32[128,640]{1,0:T(8,128)S(1)}, u32[]{:S(2)}, u32[]{:S(2)}) collective-permute-start(f32[128,640]{1,0:T(8,128)S(1)} %shard_map.88), channel_id=1, source_target_pairs={{2,4},{3,5},{4,2},{5,3},{6,8},{7,9},{8,6},{9,7},{10,12},{11,13},{1... | collective-permute-start | bytes 983048 | tf_op jit(solution)/shard_map/ppermute | solution.py:539
  37.6 4.2 %collective-permute-start.12 = (f32[264,128]{1,0:T(8,128)S(1)}, f32[264,128]{1,0:T(8,128)S(1)}, u32[]{:S(2)}, u32[]{:S(2)}) collective-permute-start(f32[264,128]{1,0:T(8,128)S(1)} %add.33), channel_id=1, source_target_pairs={{0,1},{1,0},{2,3},{3,2},{4,5},{5,4},{6,7},{7,6},{8,9},{9,8},{10,11... | collective-permute-start | bytes 405512 | tf_op jit(solution)/shard_map/ppermute | solution.py:542
  41.8 3.4 %collective-permute-start.13 = (f32[256,128]{1,0:T(8,128)S(1)}, f32[256,128]{1,0:T(8,128)S(1)}, u32[]{:S(2)}, u32[]{:S(2)}) collective-permute-start(f32[256,128]{1,0:T(8,128)S(1)} %slice.16), channel_id=1, source_target_pairs={{0,2},{2,0},{4,6},{6,4},{8,10},{10,8},{12,14},{14,12},{16,18},{18,... | collective-permute-start | bytes 393224 | tf_op jit(solution)/shard_map/ppermute | solution.py:542
  48.4 2.2 %collective-permute-start.15 = (f32[2,136,128]{2,1,0:T(8,128)S(1)}, f32[2,136,128]{2,1,0:T(8,128)S(1)}, u32[]{:S(2)}, u32[]{:S(2)}) collective-permute-start(f32[2,136,128]{2,1,0:T(8,128)S(1)} %get-tuple-element.39), channel_id=1, source_target_pairs={{0,2},{2,0},{4,6},{6,4},{8,10},{10,8},{12,14},{14,12},{16,18},{18,... | collective-permute-start | bytes 417800 | tf_op jit(solution)/shard_map/ppermute | solution.py:542
  50.6 3.2 %collective-permute-start.16 = (f32[136,128]{1,0:T(8,128)S(1)}, f32[136,128]{1,0:T(8,128)S(1)}, u32[]{:S(2)}, u32[]{:S(2)}) collective-permute-start(f32[136,128]{1,0:T(8,128)S(1)} %fusion), channel_id=1, source_target_pairs={{0,1},{1,0},{2,3},{3,2},{4,5},{5,4},{6,7},{7,6},{8,9},{9,8},{10,11... | collective-permute-start | bytes 208904 | tf_op jit(solution)/shard_map/ppermute | solution.py:542
  51.0 7.2 %collective-permute-start.14 = (f32[384,128]{1,0:T(8,128)S(1)}, f32[384,128]{1,0:T(8,128)S(1)}, u32[]{:S(2)}, u32[]{:S(2)}) collective-permute-start(f32[384,128]{1,0:T(8,128)S(1)} %get-tuple-element.37), channel_id=1, source_target_pairs={{0,1},{1,0},{2,3},{3,2},{4,5},{5,4},{6,7},{7,6},{8,9},{9,8},{10,11... | collective-permute-start | bytes 589832 | tf_op jit(solution)/shard_map/ppermute | solution.py:539
  53.8 4.4 %collective-permute-start.17 = (f32[136,128]{1,0:T(8,128)S(1)}, f32[136,128]{1,0:T(8,128)S(1)}, u32[]{:S(2)}, u32[]{:S(2)}) collective-permute-start(f32[136,128]{1,0:T(8,128)S(1)} %fusion.2.rest_1_), channel_id=1, source_target_pairs={{0,4},{2,6},{4,0},{6,2},{8,12},{10,14},{12,8},{14,10},{16,20},{18,... | collective-permute-start | bytes 208904 | tf_op jit(solution)/shard_map/ppermute | solution.py:542
  58.4 3.2 %collective-permute-start.18 = (f32[136,128]{1,0:T(8,128)S(1)}, f32[136,128]{1,0:T(8,128)S(1)}, u32[]{:S(2)}, u32[]{:S(2)}) collective-permute-start(f32[136,128]{1,0:T(8,128)S(1)} %get-tuple-element.41), channel_id=1, source_target_pairs={{0,8},{2,10},{4,12},{6,14},{8,0},{10,2},{12,4},{14,6},{16,24},{18,... | collective-permute-start | bytes 208904 | tf_op jit(solution)/shard_map/ppermute | solution.py:542
  61.6 8.4 %collective-permute-start.19 = (f32[136,128]{1,0:T(8,128)S(1)}, f32[136,128]{1,0:T(8,128)S(1)}, u32[]{:S(2)}, u32[]{:S(2)}) collective-permute-start(f32[136,128]{1,0:T(8,128)S(1)} %add.38), channel_id=1, source_target_pairs={{0,16},{2,18},{4,20},{6,22},{8,24},{10,26},{12,28},{14,30},{16,0},... | collective-permute-start | bytes 208904 | tf_op jit(solution)/shard_map/ppermute | solution.py:542
  63.4 9.4 %collective-permute-start.21 = (f32[2,64,256]{2,1,0:T(8,128)S(1)}, f32[2,64,256]{2,1,0:T(8,128)S(1)}, u32[]{:S(2)}, u32[]{:S(2)}) collective-permute-start(f32[2,64,256]{2,1,0:T(8,128)S(1)} %get-tuple-element.42), channel_id=1, source_target_pairs={{2,4},{3,5},{4,2},{5,3},{6,8},{7,9},{8,6},{9,7},{10,12},{11,13},{1... | collective-permute-start | bytes 393224 | tf_op jit(solution)/shard_map/ppermute | solution.py:539
  70.1 4.6 %collective-permute-start.20 = (f32[2,64,256]{2,1,0:T(8,128)S(1)}, f32[2,64,256]{2,1,0:T(8,128)S(1)}, u32[]{:S(2)}, u32[]{:S(2)}) collective-permute-start(f32[2,64,256]{2,1,0:T(8,128)S(1)} %shard_map.92), channel_id=1, source_target_pairs={{0,2},{1,3},{2,0},{3,1},{4,6},{5,7},{6,4},{7,5},{8,10},{9,11},{10,... | collective-permute-start | bytes 393224 | tf_op jit(solution)/shard_map/ppermute | solution.py:539
  71.1 3.7 %collective-permute-start.22 = (f32[128,128]{1,0:T(8,128)S(1)}, f32[128,128]{1,0:T(8,128)S(1)}, u32[]{:S(2)}, u32[]{:S(2)}) collective-permute-start(f32[128,128]{1,0:T(8,128)S(1)} %slice.19.own_ref), channel_id=1, source_target_pairs={{0,1},{1,0},{2,3},{3,2},{4,5},{5,4},{6,7},{7,6},{8,9},{9,8},{10,11... | collective-permute-start | bytes 196616 | tf_op jit(solution)/shard_map/ppermute | solution.py:542
  74.8 1.9 %collective-permute-start.23 = (f32[256,128]{1,0:T(8,128)S(1)}, f32[256,128]{1,0:T(8,128)S(1)}, u32[]{:S(2)}, u32[]{:S(2)}) collective-permute-start(f32[256,128]{1,0:T(8,128)S(1)} %shard_map.94), channel_id=1, source_target_pairs={{0,2},{2,0},{4,6},{6,4},{8,10},{10,8},{12,14},{14,12},{16,18},{18,... | collective-permute-start | bytes 393224 | tf_op jit(solution)/shard_map/ppermute | solution.py:542
  (6 other events, 66.5 us)
